TPU v7x, 256 devices: a whole 4x4x8 slice. The times are simulated.
256 devices in a mesh: seq: 32 (over z, y_hi, core), chan: 8 (over x, y_lo).
Axes of the slice: x: 4, y: 4 (y_hi: 2, y_lo: 2; y = y_hi * 2 + y_lo), z: 8, core: 2. Of those that a mesh axis runs over, the one named last changes fastest.
Arguments:
- queries: bfloat16 [4096, 4096], P('seq', 'chan'), may hold values from -6 to 6
- keys: bfloat16 [4096, 4096], P('seq', 'chan'), may hold values from -6 to 6
- values: bfloat16 [4096, 4096], P('seq', 'chan'), may hold values from -6 to 6
- filter_weight: float32 [4096, 4096], P('seq', 'chan'), may hold values from -48 to 48
- out_weight: bfloat16 [4096, 4096], P('chan', 'seq'), may hold values from -12 to 12
- cotangent: bfloat16 [4096, 4096], P('seq', 'chan'), may hold values from -6 to 6
Outputs:
- block_out: bfloat16 [4096, 4096], P('seq', 'chan')
- query_grad: bfloat16 [4096, 4096], P('seq', 'chan')
- key_grad: bfloat16 [4096, 4096], P('seq', 'chan')
- value_grad: bfloat16 [4096, 4096], P('seq', 'chan')
- filter_grad: float32 [4096, 4096], P('seq', 'chan')
- weight_grad: float32 [4096, 4096], P('chan', 'seq')
All inputs are finite; a program needn't handle non-finite values.
Results may differ from a plain program's by a relative error of at most 0.02.
Values may be sent and summed in bfloat16 or wider, within the bound.
No kernel may reach another device: no remote copies, remote signals or barrier semaphores. Data moves between devices by JAX's collectives and lax.ppermute only.
A program may use at most 128 MiB of HBM per device.

v0:
```python
import math

import jax
import jax.numpy as jnp
from jax import lax
from jax.sharding import PartitionSpec as P

D = 4096
BLOCK = 1024


highest = lax.Precision.HIGHEST


def make_tables(outer_size, padded):
    block_idx = jnp.arange(BLOCK, dtype=jnp.int32)
    block_angle = (
        -2.0
        * math.pi
        / BLOCK
        * (block_idx[:, None] * block_idx[None, :] % BLOCK).astype(jnp.float32)
    )
    outer_idx = jnp.arange(outer_size, dtype=jnp.int32)
    outer_angle = (
        -2.0
        * math.pi
        / outer_size
        * (outer_idx[:, None] * outer_idx[None, :] % outer_size).astype(jnp.float32)
    )
    twist_angle = (
        -2.0 * math.pi / padded * (outer_idx[:, None] * block_idx[None, :]).astype(jnp.float32)
    )
    return (
        jnp.cos(block_angle),
        jnp.sin(block_angle),
        jnp.cos(outer_angle),
        jnp.sin(outer_angle),
        jnp.cos(twist_angle),
        jnp.sin(twist_angle),
    )


def block_section(first, second, table_cos, table_sin):
    stacked = jnp.concatenate([first, second], axis=0)
    flat = stacked.reshape(-1, BLOCK)
    with_cos = jnp.dot(flat, table_cos, precision=highest).reshape((2,) + first.shape)
    with_sin = jnp.dot(flat, table_sin, precision=highest).reshape((2,) + first.shape)
    return (with_cos, with_sin)


def forward_real(signal, tables):
    block_cos, block_sin, outer_cos, outer_sin, twist_cos, twist_sin = tables
    outer_size = outer_cos.shape[0]
    half_outer = outer_size // 2
    narrow = signal.shape[0]
    cube = signal.reshape(narrow, half_outer, BLOCK)
    first_real = jnp.einsum("ba,car->cbr", outer_cos[:, :half_outer], cube, precision=highest)
    first_imag = jnp.einsum("ba,car->cbr", outer_sin[:, :half_outer], cube, precision=highest)
    twist_real = first_real * twist_cos - first_imag * twist_sin
    twist_imag = first_real * twist_sin + first_imag * twist_cos
    with_cos, with_sin = block_section(twist_real, twist_imag, block_cos, block_sin)
    spec_real = with_cos[0] - with_sin[1]
    spec_imag = with_sin[0] + with_cos[1]
    return (spec_real, spec_imag)


def inverse_real(spec_real, spec_imag, tables, padded):
    block_cos, block_sin, outer_cos, outer_sin, twist_cos, twist_sin = tables
    outer_size = outer_cos.shape[0]
    half_outer = outer_size // 2
    narrow = spec_real.shape[0]
    with_cos, with_sin = block_section(spec_real, spec_imag, block_cos, block_sin)
    mid_real = with_cos[0] + with_sin[1]
    mid_imag = with_cos[1] - with_sin[0]
    turn_real = mid_real * twist_cos + mid_imag * twist_sin
    turn_imag = mid_imag * twist_cos - mid_real * twist_sin
    result = (
        jnp.einsum("ab,cbr->car", outer_cos[:half_outer, :], turn_real, precision=highest)
        + jnp.einsum("ab,cbr->car", outer_sin[:half_outer, :], turn_imag, precision=highest)
    ) / padded
    return result.reshape(narrow, half_outer * BLOCK)


def local(queries, keys, values, filter_weight, out_weight, cotangent):
    length = queries.shape[0] * lax.axis_size("seq")
    padded = 2 * length
    outer_size = padded // BLOCK
    tables = make_tables(outer_size, padded)
    query_f = queries.astype(jnp.float32)
    key_f = keys.astype(jnp.float32)
    value_f = values.astype(jnp.float32)
    product = key_f * value_f
    filter_scaled = filter_weight / math.sqrt(length)
    product_cols, filter_cols = (
        lax.all_to_all(product.T, "seq", split_axis=0, concat_axis=1, tiled=True),
        lax.all_to_all(filter_scaled.T, "seq", split_axis=0, concat_axis=1, tiled=True),
    )
    narrow = product_cols.shape[0]
    stacked_real, stacked_imag = forward_real(
        jnp.concatenate([product_cols, filter_cols], axis=0), tables
    )
    prod_real, filt_real = (stacked_real[:narrow], stacked_real[narrow:])
    prod_imag, filt_imag = (stacked_imag[:narrow], stacked_imag[narrow:])
    conv_real = prod_real * filt_real - prod_imag * filt_imag
    conv_imag = prod_real * filt_imag + prod_imag * filt_real
    conv_cols = inverse_real(conv_real, conv_imag, tables, padded)
    conv = lax.all_to_all(conv_cols, "seq", split_axis=1, concat_axis=0, tiled=True).T
    mixed = (query_f * conv).astype(jnp.bfloat16)
    weight_scale = 1.0 / math.sqrt(D)
    weight_all = lax.all_gather(out_weight, "seq", axis=1, tiled=True)
    partial_value = jnp.dot(mixed, weight_all, preferred_element_type=jnp.float32) * weight_scale
    block_out = lax.psum_scatter(partial_value, "chan", scatter_dimension=1, tiled=True).astype(
        jnp.bfloat16
    )
    grad_full = lax.all_gather(cotangent, "chan", axis=1, tiled=True)
    mixed_grad = (
        lax.dot_general(
            grad_full, weight_all, (((1,), (1,)), ((), ())), preferred_element_type=jnp.float32
        )
        * weight_scale
    )
    query_grad = (mixed_grad * conv).astype(jnp.bfloat16)
    conv_grad = mixed_grad * query_f
    grad_cols = lax.all_to_all(conv_grad.T, "seq", split_axis=0, concat_axis=1, tiled=True)
    grad_real, grad_imag = forward_real(grad_cols, tables)
    back_real = jnp.concatenate(
        [
            grad_real * filt_real + grad_imag * filt_imag,
            grad_real * prod_real + grad_imag * prod_imag,
        ],
        axis=0,
    )
    back_imag = jnp.concatenate(
        [
            grad_imag * filt_real - grad_real * filt_imag,
            grad_imag * prod_real - grad_real * prod_imag,
        ],
        axis=0,
    )
    back_cols = inverse_real(back_real, back_imag, tables, padded)
    product_back, filter_back = (
        lax.all_to_all(back_cols[:narrow], "seq", split_axis=1, concat_axis=0, tiled=True),
        lax.all_to_all(back_cols[narrow:], "seq", split_axis=1, concat_axis=0, tiled=True),
    )
    product_grad = product_back.T
    filter_raw = filter_back.T
    key_grad = (product_grad * value_f).astype(jnp.bfloat16)
    value_grad = (product_grad * key_f).astype(jnp.bfloat16)
    filter_grad = filter_raw / math.sqrt(length)
    weight_part = lax.dot_general(
        mixed, grad_full, (((0,), (0,)), ((), ())), preferred_element_type=jnp.float32
    )
    weight_grad = (
        lax.psum_scatter(
            weight_part.astype(jnp.bfloat16), "seq", scatter_dimension=1, tiled=True
        ).astype(jnp.float32)
        * weight_scale
    )
    return (block_out, query_grad, key_grad, value_grad, filter_grad, weight_grad)


def solution(mesh):
    in_specs = (
        P("seq", "chan"),
        P("seq", "chan"),
        P("seq", "chan"),
        P("seq", "chan"),
        P("chan", "seq"),
        P("seq", "chan"),
    )
    out_specs = (
        P("seq", "chan"),
        P("seq", "chan"),
        P("seq", "chan"),
        P("seq", "chan"),
        P("seq", "chan"),
        P("chan", "seq"),
    )
    return jax.shard_map(local, mesh=mesh, in_specs=in_specs, out_specs=out_specs, check_vma=False)
```

profile of v0, /device:TPU:1, one launch (start us, length us, event | category | flops | bytes accessed | tf_op | source)
XLA Modules:
  0.0 481.5 jit_solution(14942106974859983269)
XLA Ops:
  9.7 1.0 copy.40
  11.4 12.8 %all-to-all-start = ((f32[32,16,128]{2,1,0:T(8,128)}), f32[32,16,128]{2,1,0:T(8,128)S(1)}, u32[]{:S(2)}, u32[]{:S(2)}) async-start(f32[32,16,128]{2,1,0:T(8,128)} %bitcast.1), calls=%async_computation | async-start | bytes 524288 | tf_op jit(solution)/shard_map/all_to_all | solution.py:95
  26.0 11.1 %all-to-all-done = f32[32,16,128]{2,1,0:T(8,128)S(1)} async-done(((f32[32,16,128]{2,1,0:T(8,128)}), f32[32,16,128]{2,1,0:T(8,128)S(1)}, u32[]{:S(2)}, u32[]{:S(2)}) %all-to-all-start) | async-done | bytes 262176 | tf_op jit(solution)/shard_map/all_to_all | solution.py:95
  37.1 4.1 all-to-all-start.1
  41.7 12.5 %all-to-all-done.1 = f32[32,16,128]{2,1,0:T(8,128)S(1)} async-done(((f32[32,16,128]{2,1,0:T(8,128)}), f32[32,16,128]{2,1,0:T(8,128)S(1)}, u32[]{:S(2)}, u32[]{:S(2)}) %all-to-all-start.1) | async-done | bytes 262176 | tf_op jit(solution)/shard_map/all_to_all | solution.py:96
  54.5 1.1 convolution_bitcast_fusion.1
  55.6 1.4 multiply_subtract_fusion
  56.9 24.0 %fusion.22 = f32[512,1024]{1,0:T(8,128)} fusion(f32[32,8,1024]{2,1,0:T(8,128)S(1)} %get-tuple-element.27, f32[32,8,1024]{2,1,0:T(8,128)S(1)} %get-tuple-element.26), kind=kOutput, calls=%fused_computation.22 | convolution fusion | flops 6457655296 | bytes 4194304 | tf_op jit(solution)/shard_map/dot_general | solution.py:47
  80.9 70.7 %all-gather.3.cloned.1.call-done = bf16[512,4096]{1,0:T(8,128)(2,1)} async-done(((bf16[512,128]{1,0:T(8,128)(2,1)}), bf16[512,4096]{1,0:T(8,128)(2,1)}) %all-gather.3.cloned.1.call-update) | async-done | bytes 4194320 | tf_op jit(solution)/shard_map/all_gather | solution.py:110
  151.7 4.0 convolution_multiply_fusion.1
  156.6 4.7 all-to-all-start.3
  161.4 23.0 %fusion.14 = f32[512,1024]{1,0:T(8,128)S(1)} fusion(f32[32,8,1024]{2,1,0:T(8,128)S(1)} %get-tuple-element.27, f32[32,8,1024]{2,1,0:T(8,128)S(1)} %get-tuple-element.26), kind=kOutput, calls=%fused_computation.18 | convolution fusion | flops 6457655296 | bytes 4194304 | tf_op jit(solution)/shard_map/dot_general | solution.py:46
  186.4 19.3 %fusion.10 = f32[256,1024]{1,0:T(8,128)S(1)} fusion(f32[16,8,1024]{2,1,0:T(8,128)S(1)} %get-tuple-element.31, f32[16,8,1024]{2,1,0:T(8,128)S(1)} %get-tuple-element.30), kind=kOutput, calls=%fused_computation.16 | convolution fusion | flops 3236167680 | bytes 2097152 | tf_op jit(solution)/shard_map/dot_general | solution.py:46
  205.7 19.4 %fusion.18 = f32[256,1024]{1,0:T(8,128)S(1)} fusion(f32[16,8,1024]{2,1,0:T(8,128)S(1)} %get-tuple-element.31, f32[16,8,1024]{2,1,0:T(8,128)S(1)} %get-tuple-element.30), kind=kOutput, calls=%fused_computation.20 | convolution fusion | flops 3236167680 | bytes 2097152 | tf_op jit(solution)/shard_map/dot_general | solution.py:47
  225.1 1.1 add_bitcast_fusion.1
  226.2 1.5 add_bitcast_fusion
  227.7 19.6 %fusion.20 = f32[256,1024]{1,0:T(8,128)S(1)} fusion(f32[16,8,1024]{2,1,0:T(8,128)S(1)} %get-tuple-element.28, f32[16,8,1024]{2,1,0:T(8,128)S(1)} %get-tuple-element.29), kind=kOutput, calls=%fused_computation.21 | convolution fusion | flops 3236167680 | bytes 2097152 | tf_op jit(solution)/shard_map/dot_general | solution.py:47
  247.3 19.3 %fusion.12 = f32[256,1024]{1,0:T(8,128)S(1)} fusion(f32[16,8,1024]{2,1,0:T(8,128)S(1)} %get-tuple-element.28, f32[16,8,1024]{2,1,0:T(8,128)S(1)} %get-tuple-element.29), kind=kOutput, calls=%fused_computation.17 | convolution fusion | flops 3236167680 | bytes 2097152 | tf_op jit(solution)/shard_map/dot_general | solution.py:46
  268.4 22.7 %all_to_all.99 = f32[16,32,128]{2,0,1:T(8,128)S(1)} all-to-all(f32[16,32,128]{2,0,1:T(8,128)S(1)} %copy.47), channel_id=1, replica_groups=mesh['seq'=32,'chan'=8] {'seq'}, dimensions={1} | all-to-all | bytes 524288 | tf_op jit(solution)/shard_map/all_to_all | solution.py:107
  291.2 4.4 convolution_multiply_fusion
  295.7 3.3 convolution_convert_fusion
  299.0 6.5 %copy.66 = bf16[512,4096]{0,1:T(8,128)(2,1)} copy(bf16[512,4096]{1,0:T(8,128)(2,1)} %convolution_convert_fusion) | data formatting | bytes 8388608
  307.0 22.7 %fusion.16 = f32[512,1024]{1,0:T(8,128)S(1)} fusion(f32[16,8,1024]{2,1,0:T(8,128)S(1)} %copy-done.6, f32[16,8,1024]{2,1,0:T(8,128)S(1)} %copy-done.5, f32[16,8,1024]{2,1,0:T(8,128)S(1)} %copy-done.4, f32[16,8,1024]{2,1,0:T(8,128)S(1)} %copy-done.3), kind=kOutput, calls=%fused_computation.19 | convolution fusion | flops 6458703872 | bytes 4194304 | tf_op jit(solution)/shard_map/dot_general | solution.py:47
  329.7 23.1 %fusion.8 = f32[512,1024]{1,0:T(8,128)S(1)} fusion(f32[16,8,1024]{2,1,0:T(8,128)S(1)} %copy-done.6, f32[16,8,1024]{2,1,0:T(8,128)S(1)} %copy-done.5, f32[16,8,1024]{2,1,0:T(8,128)S(1)} %copy-done.4, f32[16,8,1024]{2,1,0:T(8,128)S(1)} %copy-done.3), kind=kOutput, calls=%fused_computation.15 | convolution fusion | flops 6458703872 | bytes 4194304 | tf_op jit(solution)/shard_map/dot_general | solution.py:46
  352.8 1.4 fusion.33
  354.2 1.4 fusion.25
  356.6 4.2 all-to-all-start.4
  361.8 12.0 %all-to-all-done.4 = f32[16,32,128]{2,0,1:T(8,128)S(1)} async-done(((f32[16,32,128]{2,0,1:T(8,128)}), f32[16,32,128]{2,0,1:T(8,128)S(1)}, u32[]{:S(2)}, u32[]{:S(2)}) %all-to-all-start.4) | async-done | bytes 262176 | tf_op jit(solution)/shard_map/all_to_all | solution.py:142
  373.8 4.1 all-to-all-start.5
  379.5 11.3 %all-to-all-done.5 = f32[16,32,128]{2,0,1:T(8,128)S(1)} async-done(((f32[16,32,128]{2,0,1:T(8,128)}), f32[16,32,128]{2,0,1:T(8,128)S(1)}, u32[]{:S(2)}, u32[]{:S(2)}) %all-to-all-start.5) | async-done | bytes 262176 | tf_op jit(solution)/shard_map/all_to_all | solution.py:143
  392.4 1.6 convert_element_type.111
  394.1 78.9 %reduce-scatter.7.cloned.1.call-done = bf16[128,512]{1,0:T(8,128)(2,1)} async-done(((bf16[4096,512]{1,0:T(8,128)(2,1)}), bf16[128,512]{1,0:T(8,128)(2,1)}) %reduce-scatter.7.cloned.1.call-update) | async-done | bytes 131088
  (63 shorter events, 18.8 us)
Async XLA Ops:
  7.2 73.8 %all-gather.5.cloned.1.call-start = ((), (), s32[]{:S(2)}) async-start(), calls=%async_computation.10 | async-start | bytes 1179648 | tf_op jit(solution)/shard_map/all_gather | solution.py:115
  7.9 143.8 %all-gather.3.cloned.1.call-start = ((), (), s32[]{:S(2)}) async-start(), calls=%async_computation.8 | async-start | bytes 4325376 | tf_op jit(solution)/shard_map/all_gather | solution.py:110
  11.4 25.7 %all-to-all-start = ((f32[32,16,128]{2,1,0:T(8,128)}), f32[32,16,128]{2,1,0:T(8,128)S(1)}, u32[]{:S(2)}, u32[]{:S(2)}) async-start(f32[32,16,128]{2,1,0:T(8,128)} %bitcast.1), calls=%async_computation | async-start | bytes 524288 | tf_op jit(solution)/shard_map/all_to_all | solution.py:95
  37.1 17.1 %all-to-all-start.1 = ((f32[32,16,128]{2,1,0:T(8,128)}), f32[32,16,128]{2,1,0:T(8,128)S(1)}, u32[]{:S(2)}, u32[]{:S(2)}) async-start(f32[32,16,128]{2,1,0:T(8,128)} %bitcast.4), calls=%async_computation.1 | async-start | bytes 524288 | tf_op jit(solution)/shard_map/all_to_all | solution.py:96
  80.9 74.8 %copy-start.2 = (bf16[128,512]{1,0:T(8,128)(2,1)S(1)}, bf16[128,512]{1,0:T(8,128)(2,1)}, u32[]{:S(2)}) copy-start(bf16[128,512]{1,0:T(8,128)(2,1)} %param.6) | copy-start | bytes 393220
  156.6 28.2 %all-to-all-start.3 = ((f32[32,16,128]{2,1,0:T(8,128)}), f32[32,16,128]{2,1,0:T(8,128)S(1)}, u32[]{:S(2)}, u32[]{:S(2)}) async-start(f32[32,16,128]{2,1,0:T(8,128)} %bitcast.23), calls=%async_computation.4 | async-start | bytes 524288 | tf_op jit(solution)/shard_map/all_to_all | solution.py:124
  161.3 231.1 %reduce-scatter.5.cloned.1.call-start = ((), (), s32[]{:S(2)}) async-start(), calls=%async_computation.9 | async-start | bytes 2359296 | tf_op jit(solution)/shard_map/reduce_scatter | solution.py:112
  161.4 23.0 %copy-start.1 = (f32[512,1024]{1,0:T(8,128)S(1)}, f32[512,1024]{1,0:T(8,128)}, u32[]{:S(2)}) copy-start(f32[512,1024]{1,0:T(8,128)} %fusion.22) | copy-start | bytes 6291460
  291.2 4.5 copy-start
  295.6 177.3 %reduce-scatter.7.cloned.1.call-start = ((), (), s32[]{:S(2)}) async-start(), calls=%async_computation.11 | async-start | bytes 4325376
  305.4 1.0 copy-start.3
  305.4 1.2 copy-start.4
  305.4 1.4 copy-start.5
  305.4 1.5 copy-start.6
  356.6 17.2 %all-to-all-start.4 = ((f32[16,32,128]{2,0,1:T(8,128)}), f32[16,32,128]{2,0,1:T(8,128)S(1)}, u32[]{:S(2)}, u32[]{:S(2)}) async-start(f32[16,32,128]{2,0,1:T(8,128)} %copy.53), calls=%async_computation.5 | async-start | bytes 524288 | tf_op jit(solution)/shard_map/all_to_all | solution.py:142
  373.8 17.1 %all-to-all-start.5 = ((f32[16,32,128]{2,0,1:T(8,128)}), f32[16,32,128]{2,0,1:T(8,128)S(1)}, u32[]{:S(2)}, u32[]{:S(2)}) async-start(f32[16,32,128]{2,0,1:T(8,128)} %copy.54), calls=%async_computation.6 | async-start | bytes 524288 | tf_op jit(solution)/shard_map/all_to_all | solution.py:143
Sparse Core Ops, SparseCore 0:
  9.8 45.2 all-gather.4
  57.6 94.0 all-gather.2
  295.7 48.6 reduce-scatter.4
  348.5 124.3 reduce-scatter.6
where the time goes:
time: 490 us; the launch traced here: 481 us
  waiting for transfers between devices  198 us (40%)
  matrix products  190 us (39%)
  starting transfers between devices  30.1 us (6%)
  blocking collectives  22.7 us (5%)
  local copies, waits for them, and re-layouts  18 us (4%)
  between operations  14.4 us (3%)
  other arithmetic  8.08 us (2%)
    dot_general x4, matrix products, block_section(): jnp.dot(flat, table_sin, precision=highest).reshape((2,) + first.shape)  85.7 us
    dot_general x4, matrix products, block_section(): jnp.dot(flat, table_cos, precision=highest).reshape((2,) + first.shape)  84.7 us
    unnamed x5, waiting for transfers between devices  80.3 us
    all_gather x1, waiting for transfers between devices, local(): weight_all = lax.all_gather(out_weight, 'seq', axis=1, tiled=True)  70.7 us
    all_to_all x1, blocking collectives, local(): lax.all_to_all(conv_cols, 'seq', split_axis=1, concat_axis=0, tiled=True)  22.7 us
    unnamed x22, local copies, waits for them, and re-layouts  13.4 us
    all_to_all x1, starting transfers between devices, local(): lax.all_to_all(product.T, 'seq', split_axis=0, concat_axis=1, tiled=True)  12.8 us
    all_to_all x1, waiting for transfers between devices, local(): lax.all_to_all(filter_scaled.T, 'seq', split_axis=0, concat_axis=1, tiled...  12.5 us
  transfers between devices with their start and end apart: 9, of which 6 were waited for; matrix products, arithmetic and copies ran while one was open for 25% of the time, Pallas kernels for 0%

commit v1 on v0

v1 whole, which is shorter than its diff:
```python
import functools
import math

import jax
import jax.numpy as jnp
import numpy as np
from jax import lax
from jax.experimental import pallas as pl
from jax.experimental.pallas import tpu as pltpu
from jax.sharding import Mesh
from jax.sharding import PartitionSpec as P

D = 4096
LENGTH = 4096
PADDED = 2 * LENGTH
LANE = 128
OUTER = PADDED // LANE
HALF = OUTER // 2
ROWS = HALF + 1
CH = 16
WIDE = 512
Z, H, K, C = 8, 2, 2, 8
SEQ = ("z", "h", "k")
PLANE = ("h", "chan")
BF = jnp.bfloat16
F32 = jnp.float32
SCALE = 1.0 / math.sqrt(D)


def halves(table):
    high = np.asarray(table, np.float32).astype(BF)
    low = (np.asarray(table, np.float64) - high.astype(np.float64)).astype(np.float32).astype(BF)
    return np.stack([high, low])


@functools.lru_cache(maxsize=1)
def make_tables():
    outer = np.arange(ROWS)[:, None] * np.arange(HALF)[None, :] % OUTER
    angle = -2.0 * np.pi / OUTER * outer
    eye = np.eye(CH)
    first = np.concatenate([np.kron(np.cos(angle), eye), np.kron(np.sin(angle), eye)], axis=0)
    inner = np.arange(LANE)[:, None] * np.arange(LANE)[None, :] % LANE
    inner_cos = np.cos(2.0 * np.pi / LANE * inner)
    inner_sin = np.sin(-2.0 * np.pi / LANE * inner)
    second = np.block([[inner_cos, inner_sin], [-inner_sin, inner_cos]])
    turn = -2.0 * np.pi / PADDED * (np.arange(ROWS)[:, None] * np.arange(LANE)[None, :])
    turn = np.repeat(turn, CH, axis=0)
    twist = np.stack([np.cos(turn), np.sin(turn)]).astype(np.float32)
    count = np.full((ROWS,), 2.0)
    count[0] = count[-1] = 1.0
    back = count[None, :] / PADDED
    last = np.concatenate(
        [np.kron(np.cos(angle).T * back, eye), np.kron(np.sin(angle).T * back, eye)], axis=1
    )
    return (halves(first), halves(second), halves(second.T), twist, halves(last))


def split(x):
    high = x.astype(BF)
    return high, (x - high.astype(F32)).astype(BF)


def dot(a, b):
    return jnp.dot(a, b, preferred_element_type=F32)


def dot3(a, table):
    high, low = split(a)
    return dot(high, table[0]) + (dot(low, table[0]) + dot(high, table[1]))


def table_dot3(table, b):
    high, low = split(b)
    return dot(table[0], high) + (dot(table[0], low) + dot(table[1], high))


N = ROWS * CH


def spread(mid, twist, col):
    real = mid[:N, col : col + LANE]
    imag = mid[N:, col : col + LANE]
    return jnp.concatenate(
        [real * twist[0] - imag * twist[1], real * twist[1] + imag * twist[0]], axis=1
    )


def unspread(mid, twist):
    real = mid[:, :LANE]
    imag = mid[:, LANE:]
    return jnp.concatenate(
        [real * twist[0] + imag * twist[1], imag * twist[0] - real * twist[1]], axis=0
    )


def times(a, b):
    ar, ai, br, bi = a[:, :LANE], a[:, LANE:], b[:, :LANE], b[:, LANE:]
    return jnp.concatenate([ar * br - ai * bi, ar * bi + ai * br], axis=1)


def times_conj(a, b):
    ar, ai, br, bi = a[:, :LANE], a[:, LANE:], b[:, :LANE], b[:, LANE:]
    return jnp.concatenate([ar * br + ai * bi, ai * br - ar * bi], axis=1)


def pack_kernel(query, key, value, weight, out):
    product = key[...].astype(F32) * value[...].astype(F32)
    signals = (product, weight[...] * (1.0 / math.sqrt(LENGTH)), query[...].astype(F32))
    for i, signal in enumerate(signals):
        rows = signal.T.astype(BF).reshape(HALF, CH, LANE)
        out[:, i * CH : (i + 1) * CH, :] = rows


def share_kernel(cot, out):
    k = lax.axis_index("k")
    for h in range(H):
        for j in range(K):
            side = pl.multiple_of((2 * h + (k + j) % 2) * LANE, LANE)
            piece = cot[:, pl.ds(side, LANE)]
            for c in range(C):
                out[h * C + c, :, j * LANE : (j + 1) * LANE] = piece


def conv_kernel(packed, first, second, second_back, twist, last, mixed, conv, spectra):
    product = packed[:, 0:CH, :].reshape(HALF * CH, LANE)
    weight = packed[:, CH : 2 * CH, :].reshape(HALF * CH, LANE)
    query = packed[:, 2 * CH :, :].reshape(HALF * CH, LANE)
    both = jnp.concatenate([product, weight], axis=1)
    mid = dot(first[0], both) + dot(first[1], both)
    spec = dot3(
        jnp.concatenate([spread(mid, twist, 0), spread(mid, twist, LANE)], axis=0), second
    )
    spectra[...] = spec
    turned = unspread(dot3(times(spec[:N], spec[N:]), second_back), twist)
    result = table_dot3(last, turned)
    conv[...] = result
    mixed[...] = (query.astype(F32) * result).astype(BF)


def grad_kernel(own, other, cot, mixed, out):
    for z in range(Z):
        for h in range(H):
            for k in range(K):
                for part in range(2):
                    a = 4 * z + 2 * part + k
                    out[4 * z + 2 * h + k, part * CH : (part + 1) * CH, :] = mixed[
                        a * CH : (a + 1) * CH, :
                    ]
    total = jnp.zeros((WIDE, H * LANE), F32)
    for z in range(Z):
        weight = jnp.concatenate([own[z], other[z]], axis=1)
        rows = jnp.concatenate([cot[h * C + z] for h in range(H)], axis=0)
        total = total + lax.dot_general(
            weight, rows, (((1,), (1,)), ((), ())), preferred_element_type=F32
        )
    total = (total * SCALE).astype(BF)
    for part in range(2):
        out[:, (2 + part) * CH : (3 + part) * CH, :] = total[
            :, part * LANE : (part + 1) * LANE
        ].reshape(HALF, CH, LANE)


def tile_of(moved):
    return jnp.concatenate(
        [moved[:, p * CH : (p + 1) * CH, :].reshape(WIDE, LANE) for p in range(2)], axis=1
    )


def project_kernel(moved, own, other, out):
    mixed = tile_of(moved).astype(F32).T.astype(BF)
    for z in range(Z):
        weight = jnp.concatenate([own[z], other[z]], axis=1)
        part = (dot(mixed, weight) * SCALE).astype(BF)
        for h in range(H):
            out[h * C + z] = part[h * LANE : (h + 1) * LANE]


def weight_kernel(moved, moved_other, cot, cot_other, out):
    mixed = jnp.concatenate([tile_of(moved), tile_of(moved_other)], axis=1)
    for z in range(0, Z, 2):
        columns = []
        for y in (z, z + 1):
            rows = [cot[h * C + y, :, :LANE] for h in range(H)]
            rows += [cot_other[h * C + y, :, LANE:] for h in range(H)]
            columns.append(jnp.concatenate(rows, axis=0))
        grad = dot(mixed, jnp.concatenate(columns, axis=1)) * SCALE
        out[z] = grad[:, :LANE].astype(out.dtype)
        out[z + 1] = grad[:, LANE:].astype(out.dtype)


def back_kernel(moved, packed, conv, spectra, first, second, second_back, twist, last, out):
    pieces = []
    for z in range(Z):
        for part in range(2):
            for k in range(K):
                low = (2 + part) * CH
                pieces.append(
                    moved[4 * z + k, low : low + CH, :].astype(F32)
                    + moved[4 * z + 2 + k, low : low + CH, :].astype(F32)
                )
    mixed_grad = jnp.concatenate(pieces, axis=0)
    query = packed[:, 2 * CH :, :].reshape(HALF * CH, LANE).astype(F32)
    query_grad = (mixed_grad * conv[...]).astype(BF)
    high, low = split(mixed_grad * query)
    sides = dot(first[0], jnp.concatenate([high, low], axis=1))
    mid = sides[:, :LANE] + (sides[:, LANE:] + dot(first[1], high))
    grad = dot3(spread(mid, twist, 0), second)
    product_spec, filter_spec = spectra[:N], spectra[N:]
    both = dot3(
        jnp.concatenate([times_conj(grad, filter_spec), times_conj(grad, product_spec)], axis=0),
        second_back,
    )
    turned = jnp.concatenate([unspread(both[:N], twist), unspread(both[N:], twist)], axis=1)
    result = table_dot3(last, turned).astype(BF)
    out[:, 0:CH, :] = result[:, :LANE].reshape(HALF, CH, LANE)
    out[:, CH : 2 * CH, :] = result[:, LANE:].reshape(HALF, CH, LANE)
    out[:, 2 * CH :, :] = query_grad.reshape(HALF, CH, LANE)


def finish_kernel(moved, key, value, query_grad, key_grad, value_grad, filter_grad):
    def turned(i):
        return moved[:, i * CH : (i + 1) * CH, :].reshape(WIDE, LANE).astype(F32).T

    product_grad = turned(0)
    key_grad[...] = (product_grad * value[...].astype(F32)).astype(BF)
    value_grad[...] = (product_grad * key[...].astype(F32)).astype(BF)
    filter_grad[...] = turned(1) * (1.0 / math.sqrt(LENGTH))
    query_grad[...] = turned(2).astype(BF)


def sum_kernel(moved, out):
    k = lax.axis_index("k")
    for h in range(H):
        total = moved[h * C].astype(F32)
        for c in range(1, C):
            total = total + moved[h * C + c].astype(F32)
        total = total.astype(BF)
        for j in range(K):
            side = pl.multiple_of((2 * h + (k + j) % 2) * LANE, LANE)
            out[:, pl.ds(side, LANE)] = total[:, j * LANE : (j + 1) * LANE]


def call(kernel, outs, *args, flops=0):
    shapes = tuple(jax.ShapeDtypeStruct(s, d) for s, d in outs)
    return pl.pallas_call(
        kernel,
        out_shape=shapes,
        in_specs=[pl.BlockSpec(memory_space=pltpu.VMEM)] * len(args),
        out_specs=tuple([pl.BlockSpec(memory_space=pltpu.VMEM)] * len(outs)),
        compiler_params=pltpu.CompilerParams(vmem_limit_bytes=60 * 1024 * 1024),
        cost_estimate=pl.CostEstimate(flops=flops, bytes_accessed=4 << 20, transcendentals=0),
        name=kernel.__name__,
    )(*args)


def exchange(x, axes):
    return lax.all_to_all(x, axes, split_axis=0, concat_axis=0, tiled=True)


def local(queries, keys, values, filter_weight, out_weight, cotangent):
    first, second, second_back, twist, last = make_tables()
    core_pair = [(0, 1), (1, 0)]
    (packed,) = call(
        pack_kernel, [((HALF, 3 * CH, LANE), BF)], queries, keys, values, filter_weight
    )
    (shared,) = call(share_kernel, [((H * C, LANE, K * LANE), BF)], cotangent)
    own = lax.all_gather(out_weight, "z")
    packed = exchange(packed, SEQ)
    packed, shared = lax.optimization_barrier((packed, shared))
    cot = exchange(shared, PLANE)
    mixed, conv, spectra = call(
        conv_kernel,
        [((HALF * CH, LANE), BF), ((HALF * CH, LANE), F32), ((2 * N, 2 * LANE), F32)],
        packed, first, second, second_back, twist, last, flops=5_000_000_000,
    )
    mixed, conv, spectra = call(
        conv_kernel,
        [((HALF * CH, LANE), BF), ((HALF * CH, LANE), F32), ((2 * N, 2 * LANE), F32)],
        packed, first, second, second_back, twist, last, flops=5_000_000_000,
    )
    own, cot = lax.optimization_barrier((own, cot))
    other = lax.ppermute(own, "k", core_pair)
    cot_other = lax.ppermute(cot, "k", core_pair)
    own, cot, mixed = lax.optimization_barrier((own, cot, mixed))
    other = lax.ppermute(own, "k", core_pair)
    cot_other = lax.ppermute(cot, "k", core_pair)
    (sent,) = call(grad_kernel, [((HALF, 4 * CH, LANE), BF)], own, other, cot, mixed)
    moved = exchange(sent, SEQ)
    moved_other = lax.ppermute(moved, "k", core_pair)
    (out_part,) = call(project_kernel, [((H * C, LANE, K * LANE), BF)], moved, own, other)
    (weight_part,) = call(
        weight_kernel, [((Z, WIDE, LANE), F32)], moved, moved_other, cot, cot_other
    )
    weight_grad = lax.psum_scatter(
        weight_part.reshape(Z * WIDE, LANE), "z", scatter_dimension=0, tiled=True
    )
    out_parts = exchange(out_part, PLANE)
    (back,) = call(
        back_kernel, [((HALF, 3 * CH, LANE), BF)],
        moved, packed, conv, spectra, first, second, second_back, twist, last, flops=8_000_000_000,
    )
    back, out_parts = lax.optimization_barrier((back, out_parts))
    back = exchange(back, SEQ)
    (block_out,) = call(sum_kernel, [((LANE, WIDE), BF)], out_parts)
    query_grad, key_grad, value_grad, filter_grad = call(
        finish_kernel,
        [((LANE, WIDE), BF), ((LANE, WIDE), BF), ((LANE, WIDE), BF), ((LANE, WIDE), F32)],
        back, keys, values,
    )
    return (block_out, query_grad, key_grad, value_grad, filter_grad, weight_grad)


def solution(mesh):
    split_mesh = Mesh(mesh.devices.reshape(Z, H, K, C), ("z", "h", "k", "chan"))
    by_position = P(SEQ, "chan")
    by_channel = P("chan", SEQ)
    in_specs = (by_position,) * 4 + (by_channel, by_position)
    out_specs = (by_position,) * 5 + (by_channel,)
    return jax.shard_map(
        local, mesh=split_mesh, in_specs=in_specs, out_specs=out_specs, check_vma=False
    )
```

time: 490 us -> 156 us (0.32); the launches traced: 481 us -> 155 us
  matrix products: 190 us -> 0 us
  waiting for transfers between devices: 198 us -> 66.5 us
  Pallas kernels: 0 us -> 35 us
  blocking collectives: 22.7 us -> 0 us
  local copies, waits for them, and re-layouts: 18 us -> 2.64 us
  other arithmetic: 8.08 us -> 0 us
  starting transfers between devices: 30.1 us -> 37.2 us
    dot_general x19 -> x0, matrix products: 190 us -> none  [the longest x4 85.7 us: block_section(): jnp.dot(flat, table_sin, precision=highest).reshape((2,) + first.shape)]
    unnamed x5 -> x2, waiting for transfers between devices: 80.3 us -> 0.7 us
    all_gather x2 -> x1, waiting for transfers between devices: 70.7 us -> 0.01 us  [local(): own = lax.all_gather(out_weight, 'z')]
    pallas_call x0 -> x9, Pallas kernels: none -> 35 us  [call(): pl.pallas_call(kernel, out_shape=shapes, in_specs=[pl.BlockSpec(memory_sp...]
    all_to_all x1 -> x0, blocking collectives: 22.7 us -> none  [local(): lax.all_to_all(conv_cols, 'seq', split_axis=1, concat_axis=0, tiled=True)]
    all_to_all x5, waiting for transfers between devices: 46.9 us -> 61.8 us  [exchange(): return lax.all_to_all(x, axes, split_axis=0, concat_axis=0, tiled=True)]
    unnamed x22 -> x16, local copies, waits for them, and re-layouts: 13.4 us -> 2.64 us
  transfers between devices with their start and end apart: 9 -> 10, of which waited for: 6 -> 7; matrix products, arithmetic and copies ran while one was open for 25% -> 0% of each run, Pallas kernels for 0% -> 18%
where the time goes in v1:
time: 156 us; the launch traced here: 155 us
  waiting for transfers between devices  66.5 us (43%)
  starting transfers between devices  37.2 us (24%)
  Pallas kernels  35 us (22%)
  between operations  14.1 us (9%)
  local copies, waits for them, and re-layouts  2.64 us (2%)
    all_to_all x5, waiting for transfers between devices, exchange(): return lax.all_to_all(x, axes, split_axis=0, concat_axis=0, tiled=True)  61.8 us
    pallas_call x9, Pallas kernels, call(): pl.pallas_call(kernel, out_shape=shapes, in_specs=[pl.BlockSpec(memory_sp...  35 us
    all_to_all x5, starting transfers between devices, exchange(): return lax.all_to_all(x, axes, split_axis=0, concat_axis=0, tiled=True)  32.8 us
  transfers between devices with their start and end apart: 10, of which 7 were waited for; matrix products, arithmetic and copies ran while one was open for 0% of the time, Pallas kernels for 18%

profile of v1, /device:TPU:1, one launch (start us, length us, event | category | flops | bytes accessed | tf_op | source)
XLA Modules:
  0.0 155.5 jit_solution(9592454456795493915)
XLA Ops:
  7.2 0.0 all-gather.3.cloned.1.call-start
  7.2 0.7 all-gather.3.cloned.1.call-update
  7.9 2.1 %pack_kernel.1 = bf16[32,48,128]{2,1,0:T(8,128)(2,1)} custom-call(bf16[128,512]{1,0:T(8,128)(2,1)} %query.1, bf16[128,512]{1,0:T(8,128)(2,1)} %key.3, bf16[128,512]{1,0:T(8,128)(2,1)} %value.3, f32[128,512]{1,0:T(8,128)} %weight.1), custom_call_target="tpu_custom_call" | custom-call | bytes 4194304 | tf_op jit(solution)/shard_map/pack_kernel/pallas_call | solution.py:245
  10.0 12.8 %all-to-all-start = ((bf16[32,48,128]{2,1,0:T(8,128)(2,1)}), bf16[32,48,128]{2,1,0:T(8,128)(2,1)S(1)}, u32[]{:S(2)}, u32[]{:S(2)}) async-start(bf16[32,48,128]{2,1,0:T(8,128)(2,1)} %pack_kernel.1), calls=%async_computation | async-start | bytes 786432 | tf_op jit(solution)/shard_map/all_to_all | solution.py:257
  22.7 2.1 %share_kernel.1 = bf16[16,128,256]{2,1,0:T(8,128)(2,1)} custom-call(bf16[128,512]{1,0:T(8,128)(2,1)} %cot.1), custom_call_target="tpu_custom_call" | custom-call | bytes 4194304 | tf_op jit(solution)/shard_map/share_kernel/pallas_call | solution.py:245
  24.8 15.3 %all-to-all-done.packed = bf16[32,48,128]{2,1,0:T(8,128)(2,1)S(1)} async-done(((bf16[32,48,128]{2,1,0:T(8,128)(2,1)}), bf16[32,48,128]{2,1,0:T(8,128)(2,1)S(1)}, u32[]{:S(2)}, u32[]{:S(2)}) %all-to-all-start) | async-done | bytes 393248 | tf_op jit(solution)/shard_map/all_to_all | solution.py:257
  40.1 6.5 %all-to-all-start.1 = ((bf16[16,128,256]{2,1,0:T(8,128)(2,1)}), bf16[16,128,256]{2,1,0:T(8,128)(2,1)S(1)}, u32[]{:S(2)}, u32[]{:S(2)}) async-start(bf16[16,128,256]{2,1,0:T(8,128)(2,1)} %share_kernel.1), calls=%async_computation.1 | async-start | bytes 2097152 | tf_op jit(solution)/shard_map/all_to_all | solution.py:257
  46.6 7.5 %conv_kernel.1 = (bf16[512,128]{1,0:T(8,128)(2,1)}, f32[512,128]{1,0:T(8,128)}, f32[1056,256]{1,0:T(8,128)}) custom-call(bf16[32,48,128]{2,1,0:T(8,128)(2,1)} %copy-done.7, bf16[2,1056,512]{2,1,0:T(8,128)(2,1)} %constant.10.clone.first, bf16[2,256,256]{2,1,0:T(8,128)(2,1)} %constant.11.clone.second, bf16[2,256,256]{2,1,0:T(8,128)(2,1)} %constant.12.clone.second_back, ...), custom_call_target="tpu_custom_call" | custom-call | flops 5000000000 | bytes 4194304 | tf_op jit(solution)/shard_map/conv_kernel/pallas_call | solution.py:245
  54.1 8.3 %all-to-all-done.1.cot = bf16[16,128,256]{2,1,0:T(8,128)(2,1)S(1)} async-done(((bf16[16,128,256]{2,1,0:T(8,128)(2,1)}), bf16[16,128,256]{2,1,0:T(8,128)(2,1)S(1)}, u32[]{:S(2)}, u32[]{:S(2)}) %all-to-all-start.1) | async-done | bytes 1048608 | tf_op jit(solution)/shard_map/all_to_all | solution.py:257
  62.4 2.9 %collective-permute-start = (bf16[8,512,128]{2,1,0:T(8,128)(2,1)}, bf16[8,512,128]{2,1,0:T(8,128)(2,1)S(1)}, u32[]{:S(2)}, u32[]{:S(2)}) collective-permute-start(bf16[8,512,128]{2,1,0:T(8,128)(2,1)} %bitcast.3), channel_id=1, source_target_pairs={{0,8},{8,0},{1,9},{9,1},{2,10},{10,2},{3,11},{11,3},{4,12},{12,4},... | collective-permute-start | bytes 3145736 | tf_op jit(solution)/shard_map/ppermute | solution.py:285
  65.2 2.5 %collective-permute-done.other = bf16[8,512,128]{2,1,0:T(8,128)(2,1)S(1)} collective-permute-done((bf16[8,512,128]{2,1,0:T(8,128)(2,1)}, bf16[8,512,128]{2,1,0:T(8,128)(2,1)S(1)}, u32[]{:S(2)}, u32[]{:S(2)}) %collective-permute-start) | collective-permute-done | bytes 1048608 | tf_op jit(solution)/shard_map/ppermute | solution.py:285
  67.7 1.0 copy-done.2
  68.7 3.4 %grad_kernel.1 = bf16[32,64,128]{2,1,0:T(8,128)(2,1)} custom-call(bf16[8,512,128]{2,1,0:T(8,128)(2,1)} %bitcast.4, bf16[8,512,128]{2,1,0:T(8,128)(2,1)} %copy-done.2, bf16[16,128,256]{2,1,0:T(8,128)(2,1)} %copy-done, bf16[512,128]{1,0:T(8,128)(2,1)} %get-tuple-element.29.mixed), custom_call_target="tpu_custom_call" | custom-call | bytes 4194304 | tf_op jit(solution)/shard_map/grad_kernel/pallas_call | solution.py:245
  72.1 3.9 %all-to-all-start.2 = ((bf16[32,64,128]{2,1,0:T(8,128)(2,1)}), bf16[32,64,128]{2,1,0:T(8,128)(2,1)S(1)}, u32[]{:S(2)}, u32[]{:S(2)}) async-start(bf16[32,64,128]{2,1,0:T(8,128)(2,1)} %grad_kernel.1), calls=%async_computation.2 | async-start | bytes 1048576 | tf_op jit(solution)/shard_map/all_to_all | solution.py:257
  76.1 0.0 reduce-scatter.2.cloned.1.call-start
  76.1 0.4 collective-permute-start.2
  76.6 16.9 %all-to-all-done.2.moved = bf16[32,64,128]{2,1,0:T(8,128)(2,1)S(1)} async-done(((bf16[32,64,128]{2,1,0:T(8,128)(2,1)}), bf16[32,64,128]{2,1,0:T(8,128)(2,1)S(1)}, u32[]{:S(2)}, u32[]{:S(2)}) %all-to-all-start.2) | async-done | bytes 524320 | tf_op jit(solution)/shard_map/all_to_all | solution.py:257
  93.4 1.0 collective-permute-start.1
  94.4 0.0 collective-permute-done.2.cot_other
  94.4 1.5 collective-permute-done.1.moved_other
  96.0 0.9 copy-done.6
  96.8 3.9 %weight_kernel.1 = f32[8,512,128]{2,1,0:T(8,128)} custom-call(bf16[32,64,128]{2,1,0:T(8,128)(2,1)} %copy-done.1, bf16[32,64,128]{2,1,0:T(8,128)(2,1)} %copy-done.6, bf16[16,128,256]{2,1,0:T(8,128)(2,1)} %copy-done, bf16[16,128,256]{2,1,0:T(8,128)(2,1)} %copy-done.5), custom_call_target="tpu_custom_call" | custom-call | bytes 4194304 | tf_op jit(solution)/shard_map/weight_kernel/pallas_call | solution.py:245
  100.7 0.0 reduce-scatter.2.cloned.1.call-update
  100.8 3.4 %project_kernel.1 = bf16[16,128,256]{2,1,0:T(8,128)(2,1)} custom-call(bf16[32,64,128]{2,1,0:T(8,128)(2,1)} %copy-done.1, bf16[8,512,128]{2,1,0:T(8,128)(2,1)} %bitcast.5, bf16[8,512,128]{2,1,0:T(8,128)(2,1)} %copy-done.2), custom_call_target="tpu_custom_call" | custom-call | bytes 4194304 | tf_op jit(solution)/shard_map/project_kernel/pallas_call | solution.py:245
  104.2 4.1 %all-to-all-start.3 = ((bf16[16,128,256]{2,1,0:T(8,128)(2,1)}), bf16[16,128,256]{2,1,0:T(8,128)(2,1)S(1)}, u32[]{:S(2)}, u32[]{:S(2)}) async-start(bf16[16,128,256]{2,1,0:T(8,128)(2,1)} %project_kernel.1), calls=%async_computation.3 | async-start | bytes 2097152 | tf_op jit(solution)/shard_map/all_to_all | solution.py:257
  108.3 8.6 %back_kernel.1 = bf16[32,48,128]{2,1,0:T(8,128)(2,1)} custom-call(bf16[32,64,128]{2,1,0:T(8,128)(2,1)} %copy-done.1, bf16[32,48,128]{2,1,0:T(8,128)(2,1)} %copy-done.7, f32[512,128]{1,0:T(8,128)} %get-tuple-element.30.conv, f32[1056,256]{1,0:T(8,128)} %get-tuple-element.31.spectra, bf16[2,1056,512]{2,1,0:T(8,128)(2,1)} %constant.10.clone.first, ...), custom_call_target="tpu_custom_call" | custom-call | flops 8000000000 | bytes 4194304 | tf_op jit(solution)/shard_map/back_kernel/pallas_call | solution.py:245
  116.9 8.9 %all-to-all-done.3.moved = bf16[16,128,256]{2,1,0:T(8,128)(2,1)S(1)} async-done(((bf16[16,128,256]{2,1,0:T(8,128)(2,1)}), bf16[16,128,256]{2,1,0:T(8,128)(2,1)S(1)}, u32[]{:S(2)}, u32[]{:S(2)}) %all-to-all-start.3) | async-done | bytes 1048608 | tf_op jit(solution)/shard_map/all_to_all | solution.py:257
  125.8 5.6 %all-to-all-start.4 = ((bf16[32,48,128]{2,1,0:T(8,128)(2,1)}), bf16[32,48,128]{2,1,0:T(8,128)(2,1)S(1)}, u32[]{:S(2)}, u32[]{:S(2)}) async-start(bf16[32,48,128]{2,1,0:T(8,128)(2,1)} %back_kernel.1), calls=%async_computation.4 | async-start | bytes 786432 | tf_op jit(solution)/shard_map/all_to_all | solution.py:257
  131.4 2.0 %sum_kernel.1 = bf16[128,512]{1,0:T(8,128)(2,1)} custom-call(bf16[16,128,256]{2,1,0:T(8,128)(2,1)} %copy-done.3), custom_call_target="tpu_custom_call" | custom-call | bytes 4194304 | tf_op jit(solution)/shard_map/sum_kernel/pallas_call | solution.py:245
  133.4 12.4 %all-to-all-done.4.moved = bf16[32,48,128]{2,1,0:T(8,128)(2,1)S(1)} async-done(((bf16[32,48,128]{2,1,0:T(8,128)(2,1)}), bf16[32,48,128]{2,1,0:T(8,128)(2,1)S(1)}, u32[]{:S(2)}, u32[]{:S(2)}) %all-to-all-start.4) | async-done | bytes 393248 | tf_op jit(solution)/shard_map/all_to_all | solution.py:257
  145.8 0.7 copy-done.4
  146.6 2.0 %finish_kernel.1 = (bf16[128,512]{1,0:T(8,128)(2,1)}, bf16[128,512]{1,0:T(8,128)(2,1)}, bf16[128,512]{1,0:T(8,128)(2,1)}, f32[128,512]{1,0:T(8,128)}) custom-call(bf16[32,48,128]{2,1,0:T(8,128)(2,1)} %copy-done.4, bf16[128,512]{1,0:T(8,128)(2,1)} %key.3, bf16[128,512]{1,0:T(8,128)(2,1)} %value.3), custom_call_target="tpu_custom_call" | custom-call | bytes 4194304 | tf_op jit(solution)/shard_map/finish_kernel/pallas_call | solution.py:245
  (15 shorter events, 0.0 us)
Async XLA Ops:
  7.2 55.2 %all-gather.3.cloned.1.call-start = ((), (), s32[]{:S(2)}) async-start(), calls=%async_computation.7 | async-start | bytes 1179648 | tf_op jit(solution)/shard_map/all_gather | solution.py:267
  10.0 30.1 %all-to-all-start = ((bf16[32,48,128]{2,1,0:T(8,128)(2,1)}), bf16[32,48,128]{2,1,0:T(8,128)(2,1)S(1)}, u32[]{:S(2)}, u32[]{:S(2)}) async-start(bf16[32,48,128]{2,1,0:T(8,128)(2,1)} %pack_kernel.1), calls=%async_computation | async-start | bytes 786432 | tf_op jit(solution)/shard_map/all_to_all | solution.py:257
  40.1 6.5 %copy-start.7 = (bf16[32,48,128]{2,1,0:T(8,128)(2,1)}, bf16[32,48,128]{2,1,0:T(8,128)(2,1)S(1)}, u32[]{:S(2)}) copy-start(bf16[32,48,128]{2,1,0:T(8,128)(2,1)S(1)} %all-to-all-done.packed) | copy-start | bytes 1179652
  40.1 22.3 %all-to-all-start.1 = ((bf16[16,128,256]{2,1,0:T(8,128)(2,1)}), bf16[16,128,256]{2,1,0:T(8,128)(2,1)S(1)}, u32[]{:S(2)}, u32[]{:S(2)}) async-start(bf16[16,128,256]{2,1,0:T(8,128)(2,1)} %share_kernel.1), calls=%async_computation.1 | async-start | bytes 2097152 | tf_op jit(solution)/shard_map/all_to_all | solution.py:257
  62.4 5.4 %copy-start = (bf16[16,128,256]{2,1,0:T(8,128)(2,1)}, bf16[16,128,256]{2,1,0:T(8,128)(2,1)S(1)}, u32[]{:S(2)}) copy-start(bf16[16,128,256]{2,1,0:T(8,128)(2,1)S(1)} %all-to-all-done.1.cot) | copy-start | bytes 3145732
  62.4 5.4 %collective-permute-start = (bf16[8,512,128]{2,1,0:T(8,128)(2,1)}, bf16[8,512,128]{2,1,0:T(8,128)(2,1)S(1)}, u32[]{:S(2)}, u32[]{:S(2)}) collective-permute-start(bf16[8,512,128]{2,1,0:T(8,128)(2,1)} %bitcast.3), channel_id=1, source_target_pairs={{0,8},{8,0},{1,9},{9,1},{2,10},{10,2},{3,11},{11,3},{4,12},{12,4},... | collective-permute-start | bytes 3145736 | tf_op jit(solution)/shard_map/ppermute | solution.py:285
  67.7 1.0 copy-start.2
  72.1 21.3 %all-to-all-start.2 = ((bf16[32,64,128]{2,1,0:T(8,128)(2,1)}), bf16[32,64,128]{2,1,0:T(8,128)(2,1)S(1)}, u32[]{:S(2)}, u32[]{:S(2)}) async-start(bf16[32,64,128]{2,1,0:T(8,128)(2,1)} %grad_kernel.1), calls=%async_computation.2 | async-start | bytes 1048576 | tf_op jit(solution)/shard_map/all_to_all | solution.py:257
  76.1 72.6 %reduce-scatter.2.cloned.1.call-start = ((), (), s32[]{:S(2)}) async-start(), calls=%async_computation.6 | async-start | bytes 2359296 | tf_op jit(solution)/shard_map/reduce_scatter | solution.py:294
  76.1 18.3 %collective-permute-start.2 = (bf16[16,128,256]{2,1,0:T(8,128)(2,1)}, bf16[16,128,256]{2,1,0:T(8,128)(2,1)S(1)}, u32[]{:S(2)}, u32[]{:S(2)}) collective-permute-start(bf16[16,128,256]{2,1,0:T(8,128)(2,1)} %copy-done), channel_id=1, source_target_pairs={{0,8},{8,0},{1,9},{9,1},{2,10},{10,2},{3,11},{11,3},{4,12},{12,4},... | collective-permute-start | bytes 3145736 | tf_op jit(solution)/shard_map/ppermute | solution.py:286
  93.4 2.5 %copy-start.1 = (bf16[32,64,128]{2,1,0:T(8,128)(2,1)}, bf16[32,64,128]{2,1,0:T(8,128)(2,1)S(1)}, u32[]{:S(2)}) copy-start(bf16[32,64,128]{2,1,0:T(8,128)(2,1)S(1)} %all-to-all-done.2.moved) | copy-start | bytes 1572868
  93.4 2.5 %collective-permute-start.1 = (bf16[32,64,128]{2,1,0:T(8,128)(2,1)S(1)}, bf16[32,64,128]{2,1,0:T(8,128)(2,1)S(1)}, u32[]{:S(2)}, u32[]{:S(2)}) collective-permute-start(bf16[32,64,128]{2,1,0:T(8,128)(2,1)S(1)} %all-to-all-done.2.moved), channel_id=1, source_target_pairs={{0,8},{8,0},{1,9},{9,1},{2,10},{10,2},{3,11},{11,3},{4,12},{12,4},... | collective-permute-start | bytes 1572872 | tf_op jit(solution)/shard_map/ppermute | solution.py:289
  94.4 1.5 copy-start.5
  96.0 0.9 copy-start.6
  104.2 21.6 %all-to-all-start.3 = ((bf16[16,128,256]{2,1,0:T(8,128)(2,1)}), bf16[16,128,256]{2,1,0:T(8,128)(2,1)S(1)}, u32[]{:S(2)}, u32[]{:S(2)}) async-start(bf16[16,128,256]{2,1,0:T(8,128)(2,1)} %project_kernel.1), calls=%async_computation.3 | async-start | bytes 2097152 | tf_op jit(solution)/shard_map/all_to_all | solution.py:257
  125.8 5.6 %copy-start.3 = (bf16[16,128,256]{2,1,0:T(8,128)(2,1)}, bf16[16,128,256]{2,1,0:T(8,128)(2,1)S(1)}, u32[]{:S(2)}) copy-start(bf16[16,128,256]{2,1,0:T(8,128)(2,1)S(1)} %all-to-all-done.3.moved) | copy-start | bytes 3145732
  125.8 20.0 %all-to-all-start.4 = ((bf16[32,48,128]{2,1,0:T(8,128)(2,1)}), bf16[32,48,128]{2,1,0:T(8,128)(2,1)S(1)}, u32[]{:S(2)}, u32[]{:S(2)}) async-start(bf16[32,48,128]{2,1,0:T(8,128)(2,1)} %back_kernel.1), calls=%async_computation.4 | async-start | bytes 786432 | tf_op jit(solution)/shard_map/all_to_all | solution.py:257
  145.8 0.7 copy-start.4
Sparse Core Ops, SparseCore 0:
  9.8 42.5 all-gather.2
  100.9 31.5 reduce-scatter.1

commit v2 on v1

--- a/solution.py
+++ b/solution.py
@@ -25,6 +25,8 @@
 BF = jnp.bfloat16
 F32 = jnp.float32
 SCALE = 1.0 / math.sqrt(D)
+GRANT = 40 * 1024 * 1024
+FULL = 64 * 1024 * 1024
 
 
 def halves(table):
@@ -103,12 +105,11 @@
     return jnp.concatenate([ar * br + ai * bi, ai * br - ar * bi], axis=1)
 
 
-def pack_kernel(query, key, value, weight, out):
+def pack_kernel(key, value, weight, query, out, query_t):
     product = key[...].astype(F32) * value[...].astype(F32)
-    signals = (product, weight[...] * (1.0 / math.sqrt(LENGTH)), query[...].astype(F32))
-    for i, signal in enumerate(signals):
-        rows = signal.T.astype(BF).reshape(HALF, CH, LANE)
-        out[:, i * CH : (i + 1) * CH, :] = rows
+    for i, signal in enumerate((product, weight[...] * (1.0 / math.sqrt(LENGTH)))):
+        out[:, i * CH : (i + 1) * CH, :] = signal.T.astype(BF).reshape(HALF, CH, LANE)
+    query_t[...] = query[...].astype(F32).T.astype(BF)
 
 
 def share_kernel(cot, out):
@@ -121,10 +122,9 @@
                 out[h * C + c, :, j * LANE : (j + 1) * LANE] = piece
 
 
-def conv_kernel(packed, first, second, second_back, twist, last, mixed, conv, spectra):
+def conv_kernel(packed, first, second, second_back, twist, last, conv, spectra):
     product = packed[:, 0:CH, :].reshape(HALF * CH, LANE)
-    weight = packed[:, CH : 2 * CH, :].reshape(HALF * CH, LANE)
-    query = packed[:, 2 * CH :, :].reshape(HALF * CH, LANE)
+    weight = packed[:, CH:, :].reshape(HALF * CH, LANE)
     both = jnp.concatenate([product, weight], axis=1)
     mid = dot(first[0], both) + dot(first[1], both)
     spec = dot3(
@@ -132,18 +132,17 @@
     )
     spectra[...] = spec
     turned = unspread(dot3(times(spec[:N], spec[N:]), second_back), twist)
-    result = table_dot3(last, turned)
-    conv[...] = result
-    mixed[...] = (query.astype(F32) * result).astype(BF)
-
-
-def grad_kernel(own, other, cot, mixed, out):
+    conv[...] = table_dot3(last, turned).astype(BF)
+
+
+def grad_kernel(own, other, cot, conv, query, query_pair, out, kept, sent):
+    here = lax.axis_index("h")
     for z in range(Z):
         for h in range(H):
             for k in range(K):
                 for part in range(2):
                     a = 4 * z + 2 * part + k
-                    out[4 * z + 2 * h + k, part * CH : (part + 1) * CH, :] = mixed[
+                    out[4 * z + 2 * h + k, part * CH : (part + 1) * CH, :] = conv[
                         a * CH : (a + 1) * CH, :
                     ]
     total = jnp.zeros((WIDE, H * LANE), F32)
@@ -153,21 +152,28 @@
         total = total + lax.dot_general(
             weight, rows, (((1,), (1,)), ((), ())), preferred_element_type=F32
         )
-    total = (total * SCALE).astype(BF)
-    for part in range(2):
-        out[:, (2 + part) * CH : (3 + part) * CH, :] = total[
-            :, part * LANE : (part + 1) * LANE
-        ].reshape(HALF, CH, LANE)
-
-
-def tile_of(moved):
-    return jnp.concatenate(
-        [moved[:, p * CH : (p + 1) * CH, :].reshape(WIDE, LANE) for p in range(2)], axis=1
-    )
-
-
-def project_kernel(moved, own, other, out):
-    mixed = tile_of(moved).astype(F32).T.astype(BF)
+    total = total * SCALE
+    left, right = total[:, :LANE], total[:, LANE:]
+    kept[...] = jnp.where(here == 0, left, right)
+    sent[...] = jnp.where(here == 0, right, left).astype(BF)
+    for part, side in enumerate((left, right)):
+        gate = jnp.where(here == part, query[...].astype(F32), query_pair[...].astype(F32))
+        grad = (side * gate).astype(BF)
+        out[:, (2 + part) * CH : (3 + part) * CH, :] = grad.reshape(HALF, CH, LANE)
+
+
+def tile_of(moved, query, query_pair):
+    here = lax.axis_index("h")
+    parts = []
+    for p in range(2):
+        conv = moved[:, p * CH : (p + 1) * CH, :].reshape(WIDE, LANE).astype(F32)
+        gate = jnp.where(here == p, query[...].astype(F32), query_pair[...].astype(F32))
+        parts.append((gate * conv).astype(BF))
+    return jnp.concatenate(parts, axis=1)
+
+
+def project_kernel(moved, query, query_pair, own, other, out):
+    mixed = tile_of(moved, query, query_pair).astype(F32).T.astype(BF)
     for z in range(Z):
         weight = jnp.concatenate([own[z], other[z]], axis=1)
         part = (dot(mixed, weight) * SCALE).astype(BF)
@@ -175,8 +181,10 @@
             out[h * C + z] = part[h * LANE : (h + 1) * LANE]
 
 
-def weight_kernel(moved, moved_other, cot, cot_other, out):
-    mixed = jnp.concatenate([tile_of(moved), tile_of(moved_other)], axis=1)
+def weight_kernel(moved, moved_other, query, pair, query_other, pair_other, cot, cot_other, out):
+    mixed = jnp.concatenate(
+        [tile_of(moved, query, pair), tile_of(moved_other, query_other, pair_other)], axis=1
+    )
     for z in range(0, Z, 2):
         columns = []
         for y in (z, z + 1):
@@ -188,7 +196,7 @@
         out[z + 1] = grad[:, LANE:].astype(out.dtype)
 
 
-def back_kernel(moved, packed, conv, spectra, first, second, second_back, twist, last, out):
+def back_kernel(moved, spectra, first, second, second_back, twist, last, out):
     pieces = []
     for z in range(Z):
         for part in range(2):
@@ -198,10 +206,7 @@
                     moved[4 * z + k, low : low + CH, :].astype(F32)
                     + moved[4 * z + 2 + k, low : low + CH, :].astype(F32)
                 )
-    mixed_grad = jnp.concatenate(pieces, axis=0)
-    query = packed[:, 2 * CH :, :].reshape(HALF * CH, LANE).astype(F32)
-    query_grad = (mixed_grad * conv[...]).astype(BF)
-    high, low = split(mixed_grad * query)
+    high, low = split(jnp.concatenate(pieces, axis=0))
     sides = dot(first[0], jnp.concatenate([high, low], axis=1))
     mid = sides[:, :LANE] + (sides[:, LANE:] + dot(first[1], high))
     grad = dot3(spread(mid, twist, 0), second)
@@ -213,11 +218,10 @@
     turned = jnp.concatenate([unspread(both[:N], twist), unspread(both[N:], twist)], axis=1)
     result = table_dot3(last, turned).astype(BF)
     out[:, 0:CH, :] = result[:, :LANE].reshape(HALF, CH, LANE)
-    out[:, CH : 2 * CH, :] = result[:, LANE:].reshape(HALF, CH, LANE)
-    out[:, 2 * CH :, :] = query_grad.reshape(HALF, CH, LANE)
-
-
-def finish_kernel(moved, key, value, query_grad, key_grad, value_grad, filter_grad):
+    out[:, CH:, :] = result[:, LANE:].reshape(HALF, CH, LANE)
+
+
+def finish_kernel(moved, key, value, key_grad, value_grad, filter_grad):
     def turned(i):
         return moved[:, i * CH : (i + 1) * CH, :].reshape(WIDE, LANE).astype(F32).T
 
@@ -225,29 +229,66 @@
     key_grad[...] = (product_grad * value[...].astype(F32)).astype(BF)
     value_grad[...] = (product_grad * key[...].astype(F32)).astype(BF)
     filter_grad[...] = turned(1) * (1.0 / math.sqrt(LENGTH))
-    query_grad[...] = turned(2).astype(BF)
-
-
-def sum_kernel(moved, out):
+
+
+def sum_kernel(parts, moved, kept, received, out, query_grad):
     k = lax.axis_index("k")
     for h in range(H):
-        total = moved[h * C].astype(F32)
+        total = parts[h * C].astype(F32)
         for c in range(1, C):
-            total = total + moved[h * C + c].astype(F32)
+            total = total + parts[h * C + c].astype(F32)
         total = total.astype(BF)
         for j in range(K):
             side = pl.multiple_of((2 * h + (k + j) % 2) * LANE, LANE)
             out[:, pl.ds(side, LANE)] = total[:, j * LANE : (j + 1) * LANE]
-
-
-def call(kernel, outs, *args, flops=0):
+    left = moved[:, 0:CH, :].reshape(WIDE, LANE).astype(F32)
+    right = moved[:, CH : 2 * CH, :].reshape(WIDE, LANE).astype(F32)
+    conv = jnp.where(lax.axis_index("h") == 0, left, right)
+    grad = (kept[...] + received[...].astype(F32)) * conv
+    query_grad[...] = grad.T.astype(BF)
+
+
+class Late:
+    def __init__(self, ref, buffer, semaphore):
+        self.buffer, self.copy, self.waiting = buffer, pltpu.make_async_copy(ref, buffer, semaphore), True
+        self.copy.start()
+
+    def __getitem__(self, index):
+        if self.waiting:
+            self.copy.wait()
+            self.waiting = False
+        return self.buffer[index]
+
+
+def call(kernel, outs, *args, flops=0, late=(), grant=GRANT):
     shapes = tuple(jax.ShapeDtypeStruct(s, d) for s, d in outs)
+
+    def body(*refs):
+        refs = list(refs)
+        if late:
+            semaphores = refs.pop()
+            buffers = refs[len(args) + len(outs) :]
+            refs = refs[: len(args) + len(outs)]
+            for i, at in enumerate(late):
+                refs[at] = Late(refs[at], buffers[i], semaphores.at[i])
+        kernel(*refs)
+        for at in late:
+            if refs[at].waiting:
+                refs[at].copy.wait()
+
+    scratch = [pltpu.VMEM(args[at].shape, args[at].dtype) for at in late]
+    if late:
+        scratch.append(pltpu.SemaphoreType.DMA((len(late),)))
     return pl.pallas_call(
-        kernel,
+        body,
         out_shape=shapes,
-        in_specs=[pl.BlockSpec(memory_space=pltpu.VMEM)] * len(args),
+        in_specs=[
+            pl.BlockSpec(memory_space=pltpu.HBM if i in late else pltpu.VMEM)
+            for i in range(len(args))
+        ],
         out_specs=tuple([pl.BlockSpec(memory_space=pltpu.VMEM)] * len(outs)),
-        compiler_params=pltpu.CompilerParams(vmem_limit_bytes=60 * 1024 * 1024),
+        scratch_shapes=scratch,
+        compiler_params=pltpu.CompilerParams(vmem_limit_bytes=grant),
         cost_estimate=pl.CostEstimate(flops=flops, bytes_accessed=4 << 20, transcendentals=0),
         name=kernel.__name__,
     )(*args)
@@ -260,51 +301,60 @@
 def local(queries, keys, values, filter_weight, out_weight, cotangent):
     first, second, second_back, twist, last = make_tables()
     core_pair = [(0, 1), (1, 0)]
-    (packed,) = call(
-        pack_kernel, [((HALF, 3 * CH, LANE), BF)], queries, keys, values, filter_weight
+    packed, query_t = call(
+        pack_kernel,
+        [((HALF, 2 * CH, LANE), BF), ((WIDE, LANE), BF)],
+        keys, values, filter_weight, queries, late=(0, 1, 2, 3), grant=FULL,
     )
     (shared,) = call(share_kernel, [((H * C, LANE, K * LANE), BF)], cotangent)
+    query = (query_t, lax.ppermute(query_t, "h", core_pair))
     own = lax.all_gather(out_weight, "z")
     packed = exchange(packed, SEQ)
-    packed, shared = lax.optimization_barrier((packed, shared))
+    packed, shared, query = lax.optimization_barrier((packed, shared, query))
+    query_other = tuple(lax.ppermute(side, "k", core_pair) for side in query)
     cot = exchange(shared, PLANE)
-    mixed, conv, spectra = call(
+    conv, spectra = call(
         conv_kernel,
-        [((HALF * CH, LANE), BF), ((HALF * CH, LANE), F32), ((2 * N, 2 * LANE), F32)],
-        packed, first, second, second_back, twist, last, flops=5_000_000_000,
-    )
-    mixed, conv, spectra = call(
-        conv_kernel,
-        [((HALF * CH, LANE), BF), ((HALF * CH, LANE), F32), ((2 * N, 2 * LANE), F32)],
-        packed, first, second, second_back, twist, last, flops=5_000_000_000,
-    )
-    own, cot = lax.optimization_barrier((own, cot))
+        [((HALF * CH, LANE), BF), ((2 * N, 2 * LANE), F32)],
+        packed, first, second, second_back, twist, last, flops=5_000_000_000, late=(1, 2, 3, 4, 5),
+    )
+    own, cot, conv = lax.optimization_barrier((own, cot, conv))
     other = lax.ppermute(own, "k", core_pair)
     cot_other = lax.ppermute(cot, "k", core_pair)
-    own, cot, mixed = lax.optimization_barrier((own, cot, mixed))
-    other = lax.ppermute(own, "k", core_pair)
-    cot_other = lax.ppermute(cot, "k", core_pair)
-    (sent,) = call(grad_kernel, [((HALF, 4 * CH, LANE), BF)], own, other, cot, mixed)
+    sent, kept, passed = call(
+        grad_kernel,
+        [((HALF, 4 * CH, LANE), BF), ((WIDE, LANE), F32), ((WIDE, LANE), BF)],
+        own, other, cot, conv, *query,
+    )
+    received = lax.ppermute(passed, "h", core_pair)
     moved = exchange(sent, SEQ)
     moved_other = lax.ppermute(moved, "k", core_pair)
-    (out_part,) = call(project_kernel, [((H * C, LANE, K * LANE), BF)], moved, own, other)
+    (out_part,) = call(project_kernel, [((H * C, LANE, K * LANE), BF)], moved, *query, own, other)
+    moved_other, _ = lax.optimization_barrier((moved_other, out_part))
     (weight_part,) = call(
-        weight_kernel, [((Z, WIDE, LANE), F32)], moved, moved_other, cot, cot_other
+        weight_kernel,
+        [((Z, WIDE, LANE), F32)],
+        moved, moved_other, *query, *query_other, cot, cot_other,
     )
     weight_grad = lax.psum_scatter(
         weight_part.reshape(Z * WIDE, LANE), "z", scatter_dimension=0, tiled=True
     )
     out_parts = exchange(out_part, PLANE)
     (back,) = call(
-        back_kernel, [((HALF, 3 * CH, LANE), BF)],
-        moved, packed, conv, spectra, first, second, second_back, twist, last, flops=8_000_000_000,
+        back_kernel, [((HALF, 2 * CH, LANE), BF)],
+        moved, spectra, first, second, second_back, twist, last, flops=8_000_000_000,
+        late=(1, 2, 3, 4, 5, 6),
     )
     back, out_parts = lax.optimization_barrier((back, out_parts))
     back = exchange(back, SEQ)
-    (block_out,) = call(sum_kernel, [((LANE, WIDE), BF)], out_parts)
-    query_grad, key_grad, value_grad, filter_grad = call(
+    block_out, query_grad = call(
+        sum_kernel,
+        [((LANE, WIDE), BF), ((LANE, WIDE), BF)],
+        out_parts, moved, kept, received,
+    )
+    key_grad, value_grad, filter_grad = call(
         finish_kernel,
-        [((LANE, WIDE), BF), ((LANE, WIDE), BF), ((LANE, WIDE), BF), ((LANE, WIDE), F32)],
+        [((LANE, WIDE), BF), ((LANE, WIDE), BF), ((LANE, WIDE), F32)],
         back, keys, values,
     )
     return (block_out, query_grad, key_grad, value_grad, filter_grad, weight_grad)

time: 156 us -> 146 us (0.936)
  waiting for transfers between devices: 66.5 us -> 52.8 us
  Pallas kernels: 35 us -> 23.4 us
  local copies, waits for them, and re-layouts: 2.64 us -> 12.3 us
  starting transfers between devices: 37.2 us -> 42.3 us
    all_to_all x5, waiting for transfers between devices: 61.8 us -> 42.9 us  [exchange(): return lax.all_to_all(x, axes, split_axis=0, concat_axis=0, tiled=True)]
    pallas_call x9, Pallas kernels: 35 us -> 23.4 us  [call(): pl.pallas_call(body, out_shape=shapes, in_specs=[pl.BlockSpec(memory_spac...]
    unnamed x16 -> x38, local copies, waits for them, and re-layouts: 2.64 us -> 12.3 us
    ppermute x0 -> x4, waiting for transfers between devices: none -> 6.7 us  [the longest x1 4.1 us: local(): received = lax.ppermute(passed, 'h', core_pair)]
    ppermute x0 -> x4, starting transfers between devices: none -> 6.47 us  [the longest x1 2.98 us: local(): received = lax.ppermute(passed, 'h', core_pair)]
  transfers between devices with their start and end apart: 10 -> 14, of which waited for: 7 -> 8; matrix products, arithmetic and copies ran while one was open for 0% -> 0% of each run, Pallas kernels for 18% -> 13%
where the time goes in v2:
time: 146 us; the launch traced here: 145 us
  waiting for transfers between devices  52.8 us (36%)
  starting transfers between devices  42.3 us (29%)
  Pallas kernels  23.4 us (16%)
  between operations  14.2 us (10%)
  local copies, waits for them, and re-layouts  12.3 us (8%)
    all_to_all x5, waiting for transfers between devices, exchange(): return lax.all_to_all(x, axes, split_axis=0, concat_axis=0, tiled=True)  42.9 us
    all_to_all x5, starting transfers between devices, exchange(): return lax.all_to_all(x, axes, split_axis=0, concat_axis=0, tiled=True)  31.5 us
    pallas_call x9, Pallas kernels, call(): pl.pallas_call(body, out_shape=shapes, in_specs=[pl.BlockSpec(memory_spac...  23.4 us
    unnamed x38, local copies, waits for them, and re-layouts  12.3 us
    ppermute x1, waiting for transfers between devices, local(): received = lax.ppermute(passed, 'h', core_pair)  4.1 us
    ppermute x1, starting transfers between devices, local(): received = lax.ppermute(passed, 'h', core_pair)  2.98 us
    ppermute x1, starting transfers between devices, local(): query = (query_t, lax.ppermute(query_t, 'h', core_pair))  2.98 us
  transfers between devices with their start and end apart: 14, of which 8 were waited for; matrix products, arithmetic and copies ran while one was open for 0% of the time, Pallas kernels for 13%

profile of v2, /device:TPU:1, one launch (start us, length us, event | category | flops | bytes accessed | tf_op | source)
XLA Modules:
  0.0 145.0 jit_solution(11270574412928376096)
XLA Ops:
  7.9 2.0 %pack_kernel.1 = (bf16[32,32,128]{2,1,0:T(8,128)(2,1)}, bf16[512,128]{1,0:T(8,128)(2,1)}) custom-call(bf16[128,512]{1,0:T(8,128)(2,1)} %refs_1_.4, bf16[128,512]{1,0:T(8,128)(2,1)} %refs_2_.5, f32[128,512]{1,0:T(8,128)} %refs_2_.4, bf16[128,512]{1,0:T(8,128)(2,1)} %refs_3_.3), custom_call_target="tpu_custom_call" | custom-call | bytes 4194304 | tf_op jit(solution)/shard_map/pack_kernel/pallas_call | solution.py:282
  10.0 12.9 %all-to-all-start = ((bf16[32,32,128]{2,1,0:T(8,128)(2,1)}), bf16[32,32,128]{2,1,0:T(8,128)(2,1)S(1)}, u32[]{:S(2)}, u32[]{:S(2)}) async-start(bf16[32,32,128]{2,1,0:T(8,128)(2,1)} %get-tuple-element.28), calls=%async_computation | async-start | bytes 524288 | tf_op jit(solution)/shard_map/all_to_all | solution.py:298
  22.9 3.0 %collective-permute-start = (bf16[512,128]{1,0:T(8,128)(2,1)}, bf16[512,128]{1,0:T(8,128)(2,1)S(1)}, u32[]{:S(2)}, u32[]{:S(2)}) collective-permute-start(bf16[512,128]{1,0:T(8,128)(2,1)} %get-tuple-element.36.refs_4_.refs_1_.refs_2_), channel_id=1, source_target_pairs={{0,16},{16,0},{1,17},{17,1},{2,18},{18,2},{3,19},{19,3},{4,20},{20... | collective-permute-start | bytes 393224 | tf_op jit(solution)/shard_map/ppermute | solution.py:310
  26.7 1.1 share_kernel.1
  27.9 2.6 %collective-permute-done.refs_5_.refs_2_.refs_3_ = bf16[512,128]{1,0:T(8,128)(2,1)S(1)} collective-permute-done((bf16[512,128]{1,0:T(8,128)(2,1)}, bf16[512,128]{1,0:T(8,128)(2,1)S(1)}, u32[]{:S(2)}, u32[]{:S(2)}) %collective-permute-start) | collective-permute-done | bytes 131104 | tf_op jit(solution)/shard_map/ppermute | solution.py:310
  30.5 6.5 %all-to-all-done.refs_0_ = bf16[32,32,128]{2,1,0:T(8,128)(2,1)S(1)} async-done(((bf16[32,32,128]{2,1,0:T(8,128)(2,1)}), bf16[32,32,128]{2,1,0:T(8,128)(2,1)S(1)}, u32[]{:S(2)}, u32[]{:S(2)}) %all-to-all-start) | async-done | bytes 262176 | tf_op jit(solution)/shard_map/all_to_all | solution.py:298
  37.0 5.5 %all-to-all-start.1 = ((bf16[16,128,256]{2,1,0:T(8,128)(2,1)}), bf16[16,128,256]{2,1,0:T(8,128)(2,1)S(1)}, u32[]{:S(2)}, u32[]{:S(2)}) async-start(bf16[16,128,256]{2,1,0:T(8,128)(2,1)} %share_kernel.1), calls=%async_computation.1 | async-start | bytes 2097152 | tf_op jit(solution)/shard_map/all_to_all | solution.py:298
  42.5 1.7 %copy-done.8 = bf16[2,512,1056]{2,1,0:T(8,128)(2,1)S(1)} copy-done((bf16[2,512,1056]{2,1,0:T(8,128)(2,1)S(1)}, bf16[2,512,1056]{2,1,0:T(8,128)(2,1)}, u32[]{:S(2)}) %copy-start.8) | copy-done | bytes 2162712
  44.2 1.6 %copy-done.10 = bf16[2,1056,512]{2,1,0:T(8,128)(2,1)S(1)} copy-done((bf16[2,1056,512]{2,1,0:T(8,128)(2,1)S(1)}, bf16[2,1056,512]{2,1,0:T(8,128)(2,1)}, u32[]{:S(2)}) %copy-start.10) | copy-done | bytes 2162712
  45.8 4.9 %conv_kernel.1 = (bf16[512,128]{1,0:T(8,128)(2,1)S(1)}, f32[1056,256]{1,0:T(8,128)S(1)}) custom-call(bf16[32,32,128]{2,1,0:T(8,128)(2,1)S(1)} %all-to-all-done.refs_0_, bf16[2,1056,512]{2,1,0:T(8,128)(2,1)S(1)} %copy-done.10, bf16[2,256,256]{2,1,0:T(8,128)(2,1)S(1)} %copy-done.14, bf16[2,256,256]{2,1,0:T(8,128)(2,1)S(1)} %copy-done.15, ...), custom_call_target="tpu_custom_call" | custom-call | flops 5000000000 | bytes 4194304 | tf_op jit(solution)/shard_map/conv_kernel/pallas_call | solution.py:282
  50.8 1.0 copy-done.17
  51.8 6.5 %all-to-all-done.1.refs_2_.refs_6_ = bf16[16,128,256]{2,1,0:T(8,128)(2,1)S(1)} async-done(((bf16[16,128,256]{2,1,0:T(8,128)(2,1)}), bf16[16,128,256]{2,1,0:T(8,128)(2,1)S(1)}, u32[]{:S(2)}, u32[]{:S(2)}) %all-to-all-start.1) | async-done | bytes 1048608 | tf_op jit(solution)/shard_map/all_to_all | solution.py:298
  58.3 2.8 %collective-permute-start.1 = (bf16[8,512,128]{2,1,0:T(8,128)(2,1)}, bf16[8,512,128]{2,1,0:T(8,128)(2,1)S(1)}, u32[]{:S(2)}, u32[]{:S(2)}) collective-permute-start(bf16[8,512,128]{2,1,0:T(8,128)(2,1)} %bitcast.2), channel_id=1, source_target_pairs={{0,8},{8,0},{1,9},{9,1},{2,10},{10,2},{3,11},{11,3},{4,12},{12,4},... | collective-permute-start | bytes 3145736 | tf_op jit(solution)/shard_map/ppermute | solution.py:322
  61.1 2.5 %collective-permute-done.1.refs_1_.refs_4_ = bf16[8,512,128]{2,1,0:T(8,128)(2,1)S(1)} collective-permute-done((bf16[8,512,128]{2,1,0:T(8,128)(2,1)}, bf16[8,512,128]{2,1,0:T(8,128)(2,1)S(1)}, u32[]{:S(2)}, u32[]{:S(2)}) %collective-permute-start.1) | collective-permute-done | bytes 1048608 | tf_op jit(solution)/shard_map/ppermute | solution.py:322
  63.6 1.2 copy-done
  64.9 1.5 %grad_kernel.1 = (bf16[32,64,128]{2,1,0:T(8,128)(2,1)}, f32[512,128]{1,0:T(8,128)S(1)}, bf16[512,128]{1,0:T(8,128)(2,1)S(1)}) custom-call(bf16[8,512,128]{2,1,0:T(8,128)(2,1)S(1)} %bitcast.3, bf16[8,512,128]{2,1,0:T(8,128)(2,1)S(1)} %collective-permute-done.1.refs_1_.refs_4_, bf16[16,128,256]{2,1,0:T(8,128)(2,1)S(1)} %all-to-all-done.1.refs_2_.refs_6_, ...), custom_call_target="tpu_custom_call" | custom-call | bytes 4194304 | tf_op jit(solution)/shard_map/grad_kernel/pallas_call | solution.py:282
  66.4 3.9 %all-to-all-start.2 = ((bf16[32,64,128]{2,1,0:T(8,128)(2,1)}), bf16[32,64,128]{2,1,0:T(8,128)(2,1)S(1)}, u32[]{:S(2)}, u32[]{:S(2)}) async-start(bf16[32,64,128]{2,1,0:T(8,128)(2,1)} %get-tuple-element.38), calls=%async_computation.2 | async-start | bytes 1048576 | tf_op jit(solution)/shard_map/all_to_all | solution.py:298
  70.8 16.9 %all-to-all-done.2.refs_0_.refs_1_ = bf16[32,64,128]{2,1,0:T(8,128)(2,1)S(1)} async-done(((bf16[32,64,128]{2,1,0:T(8,128)(2,1)}), bf16[32,64,128]{2,1,0:T(8,128)(2,1)S(1)}, u32[]{:S(2)}, u32[]{:S(2)}) %all-to-all-start.2) | async-done | bytes 524320 | tf_op jit(solution)/shard_map/all_to_all | solution.py:298
  87.7 1.0 collective-permute-start.3
  89.2 1.2 copy-done.3
  90.4 1.8 %project_kernel.1 = bf16[16,128,256]{2,1,0:T(8,128)(2,1)} custom-call(bf16[32,64,128]{2,1,0:T(8,128)(2,1)S(1)} %all-to-all-done.2.refs_0_.refs_1_, bf16[512,128]{1,0:T(8,128)(2,1)S(1)} %copy-done.4, bf16[512,128]{1,0:T(8,128)(2,1)S(1)} %collective-permute-done.refs_5_.refs_2_.refs_3_, bf16[8,512,128]{2,1,0:T(8,128)(2,1)S(1)} %bitcast.4, ...), custom_call_target="tpu_custom_call" | custom-call | bytes 4194304 | tf_op jit(solution)/shard_map/project_kernel/pallas_call | solution.py:282
  92.3 3.3 %weight_kernel.1 = f32[8,512,128]{2,1,0:T(8,128)} custom-call(bf16[32,64,128]{2,1,0:T(8,128)(2,1)S(1)} %all-to-all-done.2.refs_0_.refs_1_, bf16[32,64,128]{2,1,0:T(8,128)(2,1)S(1)} %collective-permute-done.3.refs_1_, bf16[512,128]{1,0:T(8,128)(2,1)S(1)} %copy-done.4, bf16[512,128]{1,0:T(8,128)(2,1)S(1)} %collective-permute-done.refs_5_.refs_2_.refs_3_, ...), custom_call_target="tpu_custom_call" | custom-call | bytes 4194304 | tf_op jit(solution)/shard_map/weight_kernel/pallas_call | solution.py:282
  95.6 4.6 %all-to-all-start.3 = ((bf16[16,128,256]{2,1,0:T(8,128)(2,1)}), bf16[16,128,256]{2,1,0:T(8,128)(2,1)S(1)}, u32[]{:S(2)}, u32[]{:S(2)}) async-start(bf16[16,128,256]{2,1,0:T(8,128)(2,1)} %project_kernel.1), calls=%async_computation.3 | async-start | bytes 2097152 | tf_op jit(solution)/shard_map/all_to_all | solution.py:298
  100.2 1.7 %copy-done.9 = bf16[2,512,1056]{2,1,0:T(8,128)(2,1)S(1)} copy-done((bf16[2,512,1056]{2,1,0:T(8,128)(2,1)S(1)}, bf16[2,512,1056]{2,1,0:T(8,128)(2,1)}, u32[]{:S(2)}) %copy-start.9) | copy-done | bytes 2162712
  101.9 1.6 %copy-done.11 = bf16[2,1056,512]{2,1,0:T(8,128)(2,1)S(1)} copy-done((bf16[2,1056,512]{2,1,0:T(8,128)(2,1)S(1)}, bf16[2,1056,512]{2,1,0:T(8,128)(2,1)}, u32[]{:S(2)}) %copy-start.11) | copy-done | bytes 2162712
  103.5 1.2 copy-done.18
  104.8 6.8 %back_kernel.1 = bf16[32,32,128]{2,1,0:T(8,128)(2,1)} custom-call(bf16[32,64,128]{2,1,0:T(8,128)(2,1)S(1)} %all-to-all-done.2.refs_0_.refs_1_, f32[1056,256]{1,0:T(8,128)S(1)} %copy-done.18, bf16[2,1056,512]{2,1,0:T(8,128)(2,1)S(1)} %copy-done.11, bf16[2,256,256]{2,1,0:T(8,128)(2,1)S(1)} %copy-done.14, bf16[2,256,256]{2,1,0:T(8,128)(2,1)S(1)} %copy-done.16, ...), custom_call_target="tpu_custom_call" | custom-call | flops 8000000000 | bytes 4194304 | tf_op jit(solution)/shard_map/back_kernel/pallas_call | solution.py:282
  111.7 6.9 %all-to-all-done.3.refs_0_ = bf16[16,128,256]{2,1,0:T(8,128)(2,1)S(1)} async-done(((bf16[16,128,256]{2,1,0:T(8,128)(2,1)}), bf16[16,128,256]{2,1,0:T(8,128)(2,1)S(1)}, u32[]{:S(2)}, u32[]{:S(2)}) %all-to-all-start.3) | async-done | bytes 1048608 | tf_op jit(solution)/shard_map/all_to_all | solution.py:298
  118.5 4.6 %all-to-all-start.4 = ((bf16[32,32,128]{2,1,0:T(8,128)(2,1)}), bf16[32,32,128]{2,1,0:T(8,128)(2,1)S(1)}, u32[]{:S(2)}, u32[]{:S(2)}) async-start(bf16[32,32,128]{2,1,0:T(8,128)(2,1)} %back_kernel.1), calls=%async_computation.4 | async-start | bytes 524288 | tf_op jit(solution)/shard_map/all_to_all | solution.py:298
  123.1 3.0 %collective-permute-start.2 = (bf16[512,128]{1,0:T(8,128)(2,1)S(1)}, bf16[512,128]{1,0:T(8,128)(2,1)S(1)}, u32[]{:S(2)}, u32[]{:S(2)}) collective-permute-start(bf16[512,128]{1,0:T(8,128)(2,1)S(1)} %get-tuple-element.42), channel_id=1, source_target_pairs={{0,16},{16,0},{1,17},{17,1},{2,18},{18,2},{3,19},{19,3},{4,20},{20... | collective-permute-start | bytes 393224 | tf_op jit(solution)/shard_map/ppermute | solution.py:329
  126.1 4.1 %collective-permute-done.2.refs_3_ = bf16[512,128]{1,0:T(8,128)(2,1)S(1)} collective-permute-done((bf16[512,128]{1,0:T(8,128)(2,1)S(1)}, bf16[512,128]{1,0:T(8,128)(2,1)S(1)}, u32[]{:S(2)}, u32[]{:S(2)}) %collective-permute-start.2) | collective-permute-done | bytes 131104 | tf_op jit(solution)/shard_map/ppermute | solution.py:329
  131.1 6.1 %all-to-all-done.4.refs_0_ = bf16[32,32,128]{2,1,0:T(8,128)(2,1)S(1)} async-done(((bf16[32,32,128]{2,1,0:T(8,128)(2,1)}), bf16[32,32,128]{2,1,0:T(8,128)(2,1)S(1)}, u32[]{:S(2)}, u32[]{:S(2)}) %all-to-all-start.4) | async-done | bytes 262176 | tf_op jit(solution)/shard_map/all_to_all | solution.py:298
  (45 shorter events, 4.5 us)
Async XLA Ops:
  7.2 51.1 %all-gather.3.cloned.1.call-start = ((), (), s32[]{:S(2)}) async-start(), calls=%async_computation.7 | async-start | bytes 1179648 | tf_op jit(solution)/shard_map/all_gather | solution.py:311
  9.9 32.5 %copy-start.14 = (bf16[2,256,256]{2,1,0:T(8,128)(2,1)S(1)}, bf16[2,256,256]{2,1,0:T(8,128)(2,1)}, u32[]{:S(2)}) copy-start(bf16[2,256,256]{2,1,0:T(8,128)(2,1)} %constant.11.clone.refs_2_.refs_3_) | copy-start | bytes 786436
  9.9 32.5 %copy-start.15 = (bf16[2,256,256]{2,1,0:T(8,128)(2,1)S(1)}, bf16[2,256,256]{2,1,0:T(8,128)(2,1)}, u32[]{:S(2)}) copy-start(bf16[2,256,256]{2,1,0:T(8,128)(2,1)} %constant.12.clone.refs_3_.refs_4_) | copy-start | bytes 786436
  10.0 27.0 %all-to-all-start = ((bf16[32,32,128]{2,1,0:T(8,128)(2,1)}), bf16[32,32,128]{2,1,0:T(8,128)(2,1)S(1)}, u32[]{:S(2)}, u32[]{:S(2)}) async-start(bf16[32,32,128]{2,1,0:T(8,128)(2,1)} %get-tuple-element.28), calls=%async_computation | async-start | bytes 524288 | tf_op jit(solution)/shard_map/all_to_all | solution.py:298
  22.9 7.6 %collective-permute-start = (bf16[512,128]{1,0:T(8,128)(2,1)}, bf16[512,128]{1,0:T(8,128)(2,1)S(1)}, u32[]{:S(2)}, u32[]{:S(2)}) collective-permute-start(bf16[512,128]{1,0:T(8,128)(2,1)} %get-tuple-element.36.refs_4_.refs_1_.refs_2_), channel_id=1, source_target_pairs={{0,16},{16,0},{1,17},{17,1},{2,18},{18,2},{3,19},{19,3},{4,20},{20... | collective-permute-start | bytes 393224 | tf_op jit(solution)/shard_map/ppermute | solution.py:310
  26.7 15.8 %copy-start.12 = (f32[2,528,128]{2,1,0:T(8,128)S(1)}, f32[2,528,128]{2,1,0:T(8,128)}, u32[]{:S(2)}) copy-start(f32[2,528,128]{2,1,0:T(8,128)} %constant.13.clone.refs_4_.refs_5_) | copy-start | bytes 1622020
  37.0 21.3 %all-to-all-start.1 = ((bf16[16,128,256]{2,1,0:T(8,128)(2,1)}), bf16[16,128,256]{2,1,0:T(8,128)(2,1)S(1)}, u32[]{:S(2)}, u32[]{:S(2)}) async-start(bf16[16,128,256]{2,1,0:T(8,128)(2,1)} %share_kernel.1), calls=%async_computation.1 | async-start | bytes 2097152 | tf_op jit(solution)/shard_map/all_to_all | solution.py:298
  42.5 1.7 %copy-start.8 = (bf16[2,512,1056]{2,1,0:T(8,128)(2,1)S(1)}, bf16[2,512,1056]{2,1,0:T(8,128)(2,1)}, u32[]{:S(2)}) copy-start(bf16[2,512,1056]{2,1,0:T(8,128)(2,1)} %constant.14.clone.refs_5_.refs_6_) | copy-start | bytes 6488068
  44.2 1.6 %copy-start.10 = (bf16[2,1056,512]{2,1,0:T(8,128)(2,1)S(1)}, bf16[2,1056,512]{2,1,0:T(8,128)(2,1)}, u32[]{:S(2)}) copy-start(bf16[2,1056,512]{2,1,0:T(8,128)(2,1)} %constant.10.clone.refs_1_.refs_2_) | copy-start | bytes 6488068
  45.8 17.8 %copy-start.4 = (bf16[512,128]{1,0:T(8,128)(2,1)S(1)}, bf16[512,128]{1,0:T(8,128)(2,1)}, u32[]{:S(2)}) copy-start(bf16[512,128]{1,0:T(8,128)(2,1)} %get-tuple-element.36.refs_4_.refs_1_.refs_2_) | copy-start | bytes 393220
  50.8 1.0 copy-start.17
  58.3 5.3 %collective-permute-start.1 = (bf16[8,512,128]{2,1,0:T(8,128)(2,1)}, bf16[8,512,128]{2,1,0:T(8,128)(2,1)S(1)}, u32[]{:S(2)}, u32[]{:S(2)}) collective-permute-start(bf16[8,512,128]{2,1,0:T(8,128)(2,1)} %bitcast.2), channel_id=1, source_target_pairs={{0,8},{8,0},{1,9},{9,1},{2,10},{10,2},{3,11},{11,3},{4,12},{12,4},... | collective-permute-start | bytes 3145736 | tf_op jit(solution)/shard_map/ppermute | solution.py:322
  63.6 1.2 copy-start
  64.9 1.6 %copy-start.2 = (bf16[8,512,128]{2,1,0:T(8,128)(2,1)}, bf16[8,512,128]{2,1,0:T(8,128)(2,1)S(1)}, u32[]{:S(2)}) copy-start(bf16[8,512,128]{2,1,0:T(8,128)(2,1)S(1)} %collective-permute-done.1.refs_1_.refs_4_) | copy-start | bytes 3145732
  64.9 24.4 %copy-start.1 = (bf16[4096,128]{1,0:T(8,128)(2,1)S(1)}, bf16[4096,128]{1,0:T(8,128)(2,1)}, u32[]{:S(2)}) copy-start(bf16[4096,128]{1,0:T(8,128)(2,1)} %all-gather.3.cloned.1.call-done) | copy-start | bytes 3145732
  66.4 21.3 %all-to-all-start.2 = ((bf16[32,64,128]{2,1,0:T(8,128)(2,1)}), bf16[32,64,128]{2,1,0:T(8,128)(2,1)S(1)}, u32[]{:S(2)}, u32[]{:S(2)}) async-start(bf16[32,64,128]{2,1,0:T(8,128)(2,1)} %get-tuple-element.38), calls=%async_computation.2 | async-start | bytes 1048576 | tf_op jit(solution)/shard_map/all_to_all | solution.py:298
  70.3 67.8 %reduce-scatter.2.cloned.1.call-start = ((), (), s32[]{:S(2)}) async-start(), calls=%async_computation.6 | async-start | bytes 2359296 | tf_op jit(solution)/shard_map/reduce_scatter | solution.py:339
  70.4 21.9 %collective-permute-start.6 = (bf16[16,128,256]{2,1,0:T(8,128)(2,1)S(1)}, bf16[16,128,256]{2,1,0:T(8,128)(2,1)}, u32[]{:S(2)}, u32[]{:S(2)}) collective-permute-start(bf16[16,128,256]{2,1,0:T(8,128)(2,1)S(1)} %all-to-all-done.1.refs_2_.refs_6_), channel_id=1, source_target_pairs={{0,8},{8,0},{1,9},{9,1},{2,10},{10,2},{3,11},{11,3},{4,12},{12,4},... | collective-permute-start | bytes 3145736 | tf_op jit(solution)/shard_map/ppermute | solution.py:323
  87.7 4.5 %collective-permute-start.3 = (bf16[32,64,128]{2,1,0:T(8,128)(2,1)S(1)}, bf16[32,64,128]{2,1,0:T(8,128)(2,1)S(1)}, u32[]{:S(2)}, u32[]{:S(2)}) collective-permute-start(bf16[32,64,128]{2,1,0:T(8,128)(2,1)S(1)} %all-to-all-done.2.refs_0_.refs_1_), channel_id=1, source_target_pairs={{0,8},{8,0},{1,9},{9,1},{2,10},{10,2},{3,11},{11,3},{4,12},{12,4},... | collective-permute-start | bytes 1572872 | tf_op jit(solution)/shard_map/ppermute | solution.py:331
  88.7 3.5 %collective-permute-start.4 = (bf16[512,128]{1,0:T(8,128)(2,1)S(1)}, bf16[512,128]{1,0:T(8,128)(2,1)S(1)}, u32[]{:S(2)}, u32[]{:S(2)}) collective-permute-start(bf16[512,128]{1,0:T(8,128)(2,1)S(1)} %copy-done.4), channel_id=1, source_target_pairs={{0,8},{8,0},{1,9},{9,1},{2,10},{10,2},{3,11},{11,3},{4,12},{12,4},... | collective-permute-start | bytes 393224 | tf_op jit(solution)/shard_map/ppermute | solution.py:314
  88.7 3.5 %collective-permute-start.5 = (bf16[512,128]{1,0:T(8,128)(2,1)S(1)}, bf16[512,128]{1,0:T(8,128)(2,1)S(1)}, u32[]{:S(2)}, u32[]{:S(2)}) collective-permute-start(bf16[512,128]{1,0:T(8,128)(2,1)S(1)} %collective-permute-done.refs_5_.refs_2_.refs_3_), channel_id=1, source_target_pairs={{0,8},{8,0},{1,9},{9,1},{2,10},{10,2},{3,11},{11,3},{4,12},{12,4},... | collective-permute-start | bytes 393224 | tf_op jit(solution)/shard_map/ppermute | solution.py:314
  89.2 1.2 copy-start.3
  95.6 4.6 %copy-start.13 = (f32[2,528,128]{2,1,0:T(8,128)S(1)}, f32[2,528,128]{2,1,0:T(8,128)}, u32[]{:S(2)}) copy-start(f32[2,528,128]{2,1,0:T(8,128)} %constant.13.clone.refs_4_.refs_5_) | copy-start | bytes 1622020
  95.6 4.6 %copy-start.16 = (bf16[2,256,256]{2,1,0:T(8,128)(2,1)S(1)}, bf16[2,256,256]{2,1,0:T(8,128)(2,1)}, u32[]{:S(2)}) copy-start(bf16[2,256,256]{2,1,0:T(8,128)(2,1)} %constant.12.clone.refs_3_.refs_4_) | copy-start | bytes 786436
  95.6 22.9 %all-to-all-start.3 = ((bf16[16,128,256]{2,1,0:T(8,128)(2,1)}), bf16[16,128,256]{2,1,0:T(8,128)(2,1)S(1)}, u32[]{:S(2)}, u32[]{:S(2)}) async-start(bf16[16,128,256]{2,1,0:T(8,128)(2,1)} %project_kernel.1), calls=%async_computation.3 | async-start | bytes 2097152 | tf_op jit(solution)/shard_map/all_to_all | solution.py:298
  100.2 1.7 %copy-start.9 = (bf16[2,512,1056]{2,1,0:T(8,128)(2,1)S(1)}, bf16[2,512,1056]{2,1,0:T(8,128)(2,1)}, u32[]{:S(2)}) copy-start(bf16[2,512,1056]{2,1,0:T(8,128)(2,1)} %constant.14.clone.refs_5_.refs_6_) | copy-start | bytes 6488068
  101.9 1.6 %copy-start.11 = (bf16[2,1056,512]{2,1,0:T(8,128)(2,1)S(1)}, bf16[2,1056,512]{2,1,0:T(8,128)(2,1)}, u32[]{:S(2)}) copy-start(bf16[2,1056,512]{2,1,0:T(8,128)(2,1)} %constant.10.clone.refs_1_.refs_2_) | copy-start | bytes 6488068
  103.5 1.2 copy-start.18
  111.6 25.6 %copy-start.5 = (bf16[128,512]{1,0:T(8,128)(2,1)S(1)}, bf16[128,512]{1,0:T(8,128)(2,1)}, u32[]{:S(2)}) copy-start(bf16[128,512]{1,0:T(8,128)(2,1)} %refs_1_.4) | copy-start | bytes 393220
  111.6 25.6 %copy-start.6 = (bf16[128,512]{1,0:T(8,128)(2,1)S(1)}, bf16[128,512]{1,0:T(8,128)(2,1)}, u32[]{:S(2)}) copy-start(bf16[128,512]{1,0:T(8,128)(2,1)} %refs_2_.5) | copy-start | bytes 393220
  118.5 18.7 %all-to-all-start.4 = ((bf16[32,32,128]{2,1,0:T(8,128)(2,1)}), bf16[32,32,128]{2,1,0:T(8,128)(2,1)S(1)}, u32[]{:S(2)}, u32[]{:S(2)}) async-start(bf16[32,32,128]{2,1,0:T(8,128)(2,1)} %back_kernel.1), calls=%async_computation.4 | async-start | bytes 524288 | tf_op jit(solution)/shard_map/all_to_all | solution.py:298
  123.1 7.1 %collective-permute-start.2 = (bf16[512,128]{1,0:T(8,128)(2,1)S(1)}, bf16[512,128]{1,0:T(8,128)(2,1)S(1)}, u32[]{:S(2)}, u32[]{:S(2)}) collective-permute-start(bf16[512,128]{1,0:T(8,128)(2,1)S(1)} %get-tuple-element.42), channel_id=1, source_target_pairs={{0,16},{16,0},{1,17},{17,1},{2,18},{18,2},{3,19},{19,3},{4,20},{20... | collective-permute-start | bytes 393224 | tf_op jit(solution)/shard_map/ppermute | solution.py:329
  (1 other events, 0.9 us)
Sparse Core Ops, SparseCore 0:
  9.8 40.8 all-gather.2
  95.7 31.5 reduce-scatter.1

commit v3 on v2

--- a/solution.py
+++ b/solution.py
@@ -105,11 +105,14 @@
     return jnp.concatenate([ar * br + ai * bi, ai * br - ar * bi], axis=1)
 
 
-def pack_kernel(key, value, weight, query, out, query_t):
+def pack_kernel(key, value, weight, out):
     product = key[...].astype(F32) * value[...].astype(F32)
     for i, signal in enumerate((product, weight[...] * (1.0 / math.sqrt(LENGTH)))):
         out[:, i * CH : (i + 1) * CH, :] = signal.T.astype(BF).reshape(HALF, CH, LANE)
-    query_t[...] = query[...].astype(F32).T.astype(BF)
+
+
+def turn_kernel(query, out):
+    out[...] = query[...].astype(F32).T.astype(BF)
 
 
 def share_kernel(cot, out):
@@ -135,7 +138,29 @@
     conv[...] = table_dot3(last, turned).astype(BF)
 
 
-def grad_kernel(own, other, cot, conv, query, query_pair, out, kept, sent):
+def partial_grad(weights, cot, side):
+    total = jnp.zeros((WIDE, H * LANE), F32)
+    columns = slice(side * LANE, (side + 1) * LANE)
+    for z in range(0, Z, 2):
+        weight = jnp.concatenate([weights[z], weights[z + 1]], axis=1)
+        rows = [
+            jnp.concatenate([cot[h * C + z, :, columns], cot[h * C + z + 1, :, columns]], axis=1)
+            for h in range(H)
+        ]
+        total = total + lax.dot_general(
+            weight,
+            jnp.concatenate(rows, axis=0),
+            (((1,), (1,)), ((), ())),
+            preferred_element_type=F32,
+        )
+    return total
+
+
+def own_grad_kernel(own, cot, out):
+    out[...] = partial_grad(own, cot, 0)
+
+
+def grad_kernel(first, other, cot, conv, query, query_pair, out, kept, sent):
     here = lax.axis_index("h")
     for z in range(Z):
         for h in range(H):
@@ -145,14 +170,7 @@
                     out[4 * z + 2 * h + k, part * CH : (part + 1) * CH, :] = conv[
                         a * CH : (a + 1) * CH, :
                     ]
-    total = jnp.zeros((WIDE, H * LANE), F32)
-    for z in range(Z):
-        weight = jnp.concatenate([own[z], other[z]], axis=1)
-        rows = jnp.concatenate([cot[h * C + z] for h in range(H)], axis=0)
-        total = total + lax.dot_general(
-            weight, rows, (((1,), (1,)), ((), ())), preferred_element_type=F32
-        )
-    total = total * SCALE
+    total = (first[...] + partial_grad(other, cot, 1)) * SCALE
     left, right = total[:, :LANE], total[:, LANE:]
     kept[...] = jnp.where(here == 0, left, right)
     sent[...] = jnp.where(here == 0, right, left).astype(BF)
@@ -260,25 +278,44 @@
         return self.buffer[index]
 
 
-def call(kernel, outs, *args, flops=0, late=(), grant=GRANT):
+class Stream:
+    def __init__(self, ref, buffer, semaphores):
+        self.ref, self.buffer, self.semaphores, self.copies = ref, buffer, semaphores, []
+        self.dtype = ref.dtype
+
+    def __setitem__(self, index, value):
+        self.buffer[index] = value
+        copy = pltpu.make_async_copy(
+            self.buffer.at[index], self.ref.at[index], self.semaphores.at[len(self.copies)]
+        )
+        copy.start()
+        self.copies.append(copy)
+
+
+def call(kernel, outs, *args, flops=0, late=(), grant=GRANT, stream=False):
     shapes = tuple(jax.ShapeDtypeStruct(s, d) for s, d in outs)
+    count = len(args) + len(outs)
 
     def body(*refs):
-        refs = list(refs)
-        if late:
-            semaphores = refs.pop()
-            buffers = refs[len(args) + len(outs) :]
-            refs = refs[: len(args) + len(outs)]
-            for i, at in enumerate(late):
-                refs[at] = Late(refs[at], buffers[i], semaphores.at[i])
+        refs, rest = list(refs[:count]), list(refs[count:])
+        for i, at in enumerate(late):
+            refs[at] = Late(refs[at], rest[i], rest[len(late)].at[i])
+        if stream:
+            refs[-1] = Stream(refs[-1], rest[-2], rest[-1])
         kernel(*refs)
         for at in late:
             if refs[at].waiting:
                 refs[at].copy.wait()
+        if stream:
+            for copy in refs[-1].copies:
+                copy.wait()
 
     scratch = [pltpu.VMEM(args[at].shape, args[at].dtype) for at in late]
     if late:
         scratch.append(pltpu.SemaphoreType.DMA((len(late),)))
+    if stream:
+        scratch += [pltpu.VMEM(*outs[0]), pltpu.SemaphoreType.DMA((outs[0][0][0],))]
+    out_space = pltpu.HBM if stream else pltpu.VMEM
     return pl.pallas_call(
         body,
         out_shape=shapes,
@@ -286,7 +323,7 @@
             pl.BlockSpec(memory_space=pltpu.HBM if i in late else pltpu.VMEM)
             for i in range(len(args))
         ],
-        out_specs=tuple([pl.BlockSpec(memory_space=pltpu.VMEM)] * len(outs)),
+        out_specs=tuple([pl.BlockSpec(memory_space=out_space)] * len(outs)),
         scratch_shapes=scratch,
         compiler_params=pltpu.CompilerParams(vmem_limit_bytes=grant),
         cost_estimate=pl.CostEstimate(flops=flops, bytes_accessed=4 << 20, transcendentals=0),
@@ -301,11 +338,11 @@
 def local(queries, keys, values, filter_weight, out_weight, cotangent):
     first, second, second_back, twist, last = make_tables()
     core_pair = [(0, 1), (1, 0)]
-    packed, query_t = call(
-        pack_kernel,
-        [((HALF, 2 * CH, LANE), BF), ((WIDE, LANE), BF)],
-        keys, values, filter_weight, queries, late=(0, 1, 2, 3), grant=FULL,
-    )
+    (packed,) = call(
+        pack_kernel, [((HALF, 2 * CH, LANE), BF)], keys, values, filter_weight,
+        late=(0, 1, 2), grant=FULL,
+    )
+    (query_t,) = call(turn_kernel, [((WIDE, LANE), BF)], queries)
     (shared,) = call(share_kernel, [((H * C, LANE, K * LANE), BF)], cotangent)
     query = (query_t, lax.ppermute(query_t, "h", core_pair))
     own = lax.all_gather(out_weight, "z")
@@ -321,10 +358,11 @@
     own, cot, conv = lax.optimization_barrier((own, cot, conv))
     other = lax.ppermute(own, "k", core_pair)
     cot_other = lax.ppermute(cot, "k", core_pair)
+    (own_part,) = call(own_grad_kernel, [((WIDE, H * LANE), F32)], own, cot)
     sent, kept, passed = call(
         grad_kernel,
         [((HALF, 4 * CH, LANE), BF), ((WIDE, LANE), F32), ((WIDE, LANE), BF)],
-        own, other, cot, conv, *query,
+        own_part, other, cot, conv, *query,
     )
     received = lax.ppermute(passed, "h", core_pair)
     moved = exchange(sent, SEQ)
@@ -334,7 +372,7 @@
     (weight_part,) = call(
         weight_kernel,
         [((Z, WIDE, LANE), F32)],
-        moved, moved_other, *query, *query_other, cot, cot_other,
+        moved, moved_other, *query, *query_other, cot, cot_other, stream=True,
     )
     weight_grad = lax.psum_scatter(
         weight_part.reshape(Z * WIDE, LANE), "z", scatter_dimension=0, tiled=True

time: 146 us -> 144 us (0.986)
  waiting for transfers between devices: 52.8 us -> 49.7 us
    ppermute x1, waiting for transfers between devices: 2.5 us -> 0.8 us  [local(): other = lax.ppermute(own, 'k', core_pair)]
    unnamed x38 -> x34, local copies, waits for them, and re-layouts: 12.3 us -> 13.2 us
    pallas_call x9 -> x11, Pallas kernels: 23.4 us -> 23.4 us  [call(): pl.pallas_call(body, out_shape=shapes, in_specs=[pl.BlockSpec(memory_spac...]
where the time goes in v3:
time: 144 us; the launch traced here: 143 us
  waiting for transfers between devices  49.7 us (35%)
  starting transfers between devices  42.3 us (29%)
  Pallas kernels  23.4 us (16%)
  between operations  14.3 us (10%)
  local copies, waits for them, and re-layouts  13.2 us (9%)
    all_to_all x5, waiting for transfers between devices, exchange(): return lax.all_to_all(x, axes, split_axis=0, concat_axis=0, tiled=True)  41.7 us
    all_to_all x5, starting transfers between devices, exchange(): return lax.all_to_all(x, axes, split_axis=0, concat_axis=0, tiled=True)  31.5 us
    pallas_call x11, Pallas kernels, call(): pl.pallas_call(body, out_shape=shapes, in_specs=[pl.BlockSpec(memory_spac...  23.4 us
    unnamed x34, local copies, waits for them, and re-layouts  13.2 us
    ppermute x1, waiting for transfers between devices, local(): received = lax.ppermute(passed, 'h', core_pair)  4.1 us
    ppermute x1, starting transfers between devices, local(): received = lax.ppermute(passed, 'h', core_pair)  2.98 us
    ppermute x1, starting transfers between devices, local(): query = (query_t, lax.ppermute(query_t, 'h', core_pair))  2.98 us
  transfers between devices with their start and end apart: 14, of which 8 were waited for; matrix products, arithmetic and copies ran while one was open for 0% of the time, Pallas kernels for 13%

profile of v3, /device:TPU:1, one launch (start us, length us, event | category | flops | bytes accessed | tf_op | source)
XLA Modules:
  0.0 142.9 jit_solution(8927717913211376748)
XLA Ops:
  7.9 1.9 %pack_kernel.1 = bf16[32,32,128]{2,1,0:T(8,128)(2,1)} custom-call(bf16[128,512]{1,0:T(8,128)(2,1)} %refs_1_.4, bf16[128,512]{1,0:T(8,128)(2,1)} %refs_2_.5, f32[128,512]{1,0:T(8,128)} %refs_2_.4), custom_call_target="tpu_custom_call" | custom-call | bytes 4194304 | tf_op jit(solution)/shard_map/pack_kernel/pallas_call | solution.py:319
  9.9 12.9 %all-to-all-start = ((bf16[32,32,128]{2,1,0:T(8,128)(2,1)}), bf16[32,32,128]{2,1,0:T(8,128)(2,1)S(1)}, u32[]{:S(2)}, u32[]{:S(2)}) async-start(bf16[32,32,128]{2,1,0:T(8,128)(2,1)} %pack_kernel.1), calls=%async_computation | async-start | bytes 524288 | tf_op jit(solution)/shard_map/all_to_all | solution.py:335
  23.8 3.0 %collective-permute-start = (bf16[512,128]{1,0:T(8,128)(2,1)S(1)}, bf16[512,128]{1,0:T(8,128)(2,1)S(1)}, u32[]{:S(2)}, u32[]{:S(2)}) collective-permute-start(bf16[512,128]{1,0:T(8,128)(2,1)S(1)} %turn_kernel.1.refs_4_.refs_1_.refs_2_), channel_id=1, source_target_pairs={{0,16},{16,0},{1,17},{17,1},{2,18},{18,2},{3,19},{19,3},{4,20},{20... | collective-permute-start | bytes 393224 | tf_op jit(solution)/shard_map/ppermute | solution.py:347
  27.7 1.1 share_kernel.1
  28.8 2.4 %collective-permute-done.refs_5_.refs_2_.refs_3_ = bf16[512,128]{1,0:T(8,128)(2,1)S(1)} collective-permute-done((bf16[512,128]{1,0:T(8,128)(2,1)S(1)}, bf16[512,128]{1,0:T(8,128)(2,1)S(1)}, u32[]{:S(2)}, u32[]{:S(2)}) %collective-permute-start) | collective-permute-done | bytes 131104 | tf_op jit(solution)/shard_map/ppermute | solution.py:347
  31.2 5.6 %all-to-all-done.refs_0_ = bf16[32,32,128]{2,1,0:T(8,128)(2,1)S(1)} async-done(((bf16[32,32,128]{2,1,0:T(8,128)(2,1)}), bf16[32,32,128]{2,1,0:T(8,128)(2,1)S(1)}, u32[]{:S(2)}, u32[]{:S(2)}) %all-to-all-start) | async-done | bytes 262176 | tf_op jit(solution)/shard_map/all_to_all | solution.py:335
  36.8 5.5 %all-to-all-start.1 = ((bf16[16,128,256]{2,1,0:T(8,128)(2,1)}), bf16[16,128,256]{2,1,0:T(8,128)(2,1)S(1)}, u32[]{:S(2)}, u32[]{:S(2)}) async-start(bf16[16,128,256]{2,1,0:T(8,128)(2,1)} %share_kernel.1), calls=%async_computation.1 | async-start | bytes 2097152 | tf_op jit(solution)/shard_map/all_to_all | solution.py:335
  42.3 1.7 %copy-done.6 = bf16[2,512,1056]{2,1,0:T(8,128)(2,1)S(1)} copy-done((bf16[2,512,1056]{2,1,0:T(8,128)(2,1)S(1)}, bf16[2,512,1056]{2,1,0:T(8,128)(2,1)}, u32[]{:S(2)}) %copy-start.6) | copy-done | bytes 2162712
  44.0 1.6 %copy-done.8 = bf16[2,1056,512]{2,1,0:T(8,128)(2,1)S(1)} copy-done((bf16[2,1056,512]{2,1,0:T(8,128)(2,1)S(1)}, bf16[2,1056,512]{2,1,0:T(8,128)(2,1)}, u32[]{:S(2)}) %copy-start.8) | copy-done | bytes 2162712
  45.6 4.9 %conv_kernel.1 = (bf16[512,128]{1,0:T(8,128)(2,1)S(1)}, f32[1056,256]{1,0:T(8,128)S(1)}) custom-call(bf16[32,32,128]{2,1,0:T(8,128)(2,1)S(1)} %all-to-all-done.refs_0_, bf16[2,1056,512]{2,1,0:T(8,128)(2,1)S(1)} %copy-done.8, bf16[2,256,256]{2,1,0:T(8,128)(2,1)S(1)} %copy-done.12, bf16[2,256,256]{2,1,0:T(8,128)(2,1)S(1)} %copy-done.13, ...), custom_call_target="tpu_custom_call" | custom-call | flops 5000000000 | bytes 4194304 | tf_op jit(solution)/shard_map/conv_kernel/pallas_call | solution.py:319
  50.6 1.0 copy-done.15
  51.6 6.5 %all-to-all-done.1.refs_1_.refs_2_.refs_6_ = bf16[16,128,256]{2,1,0:T(8,128)(2,1)S(1)} async-done(((bf16[16,128,256]{2,1,0:T(8,128)(2,1)}), bf16[16,128,256]{2,1,0:T(8,128)(2,1)S(1)}, u32[]{:S(2)}, u32[]{:S(2)}) %all-to-all-start.1) | async-done | bytes 1048608 | tf_op jit(solution)/shard_map/all_to_all | solution.py:335
  58.1 2.8 %collective-permute-start.1 = (bf16[8,512,128]{2,1,0:T(8,128)(2,1)}, bf16[8,512,128]{2,1,0:T(8,128)(2,1)S(1)}, u32[]{:S(2)}, u32[]{:S(2)}) collective-permute-start(bf16[8,512,128]{2,1,0:T(8,128)(2,1)} %bitcast.2), channel_id=1, source_target_pairs={{0,8},{8,0},{1,9},{9,1},{2,10},{10,2},{3,11},{11,3},{4,12},{12,4},... | collective-permute-start | bytes 3145736 | tf_op jit(solution)/shard_map/ppermute | solution.py:359
  61.0 1.2 copy-done
  63.5 1.3 grad_kernel.1
  64.7 3.9 %all-to-all-start.2 = ((bf16[32,64,128]{2,1,0:T(8,128)(2,1)}), bf16[32,64,128]{2,1,0:T(8,128)(2,1)S(1)}, u32[]{:S(2)}, u32[]{:S(2)}) async-start(bf16[32,64,128]{2,1,0:T(8,128)(2,1)} %get-tuple-element.34), calls=%async_computation.2 | async-start | bytes 1048576 | tf_op jit(solution)/shard_map/all_to_all | solution.py:335
  69.1 16.9 %all-to-all-done.2.refs_0_.refs_1_ = bf16[32,64,128]{2,1,0:T(8,128)(2,1)S(1)} async-done(((bf16[32,64,128]{2,1,0:T(8,128)(2,1)}), bf16[32,64,128]{2,1,0:T(8,128)(2,1)S(1)}, u32[]{:S(2)}, u32[]{:S(2)}) %all-to-all-start.2) | async-done | bytes 524320 | tf_op jit(solution)/shard_map/all_to_all | solution.py:335
  86.0 1.0 collective-permute-start.3
  87.5 1.2 copy-done.1
  88.8 1.8 %project_kernel.1 = bf16[16,128,256]{2,1,0:T(8,128)(2,1)} custom-call(bf16[32,64,128]{2,1,0:T(8,128)(2,1)S(1)} %all-to-all-done.2.refs_0_.refs_1_, bf16[512,128]{1,0:T(8,128)(2,1)S(1)} %turn_kernel.1.refs_4_.refs_1_.refs_2_, bf16[512,128]{1,0:T(8,128)(2,1)S(1)} %collective-permute-done.refs_5_.refs_2_.refs_3_, bf16[8,512,128]{2,1,0:T(8,128)(2,1)S(1)} %bitcast.4, ...), custom_call_target="tpu_custom_call" | custom-call | bytes 4194304 | tf_op jit(solution)/shard_map/project_kernel/pallas_call | solution.py:319
  90.6 3.1 %weight_kernel.1 = f32[8,512,128]{2,1,0:T(8,128)} custom-call(bf16[32,64,128]{2,1,0:T(8,128)(2,1)S(1)} %all-to-all-done.2.refs_0_.refs_1_, bf16[32,64,128]{2,1,0:T(8,128)(2,1)S(1)} %collective-permute-done.3.refs_1_, bf16[512,128]{1,0:T(8,128)(2,1)S(1)} %turn_kernel.1.refs_4_.refs_1_.refs_2_, ...), custom_call_target="tpu_custom_call" | custom-call | bytes 4194304 | tf_op jit(solution)/shard_map/weight_kernel/pallas_call | solution.py:319
  93.7 4.6 %all-to-all-start.3 = ((bf16[16,128,256]{2,1,0:T(8,128)(2,1)}), bf16[16,128,256]{2,1,0:T(8,128)(2,1)S(1)}, u32[]{:S(2)}, u32[]{:S(2)}) async-start(bf16[16,128,256]{2,1,0:T(8,128)(2,1)} %project_kernel.1), calls=%async_computation.3 | async-start | bytes 2097152 | tf_op jit(solution)/shard_map/all_to_all | solution.py:335
  98.4 1.7 %copy-done.7 = bf16[2,512,1056]{2,1,0:T(8,128)(2,1)S(1)} copy-done((bf16[2,512,1056]{2,1,0:T(8,128)(2,1)S(1)}, bf16[2,512,1056]{2,1,0:T(8,128)(2,1)}, u32[]{:S(2)}) %copy-start.7) | copy-done | bytes 2162712
  100.1 1.6 %copy-done.9 = bf16[2,1056,512]{2,1,0:T(8,128)(2,1)S(1)} copy-done((bf16[2,1056,512]{2,1,0:T(8,128)(2,1)S(1)}, bf16[2,1056,512]{2,1,0:T(8,128)(2,1)}, u32[]{:S(2)}) %copy-start.9) | copy-done | bytes 2162712
  101.7 1.2 copy-done.16
  103.0 6.8 %back_kernel.1 = bf16[32,32,128]{2,1,0:T(8,128)(2,1)} custom-call(bf16[32,64,128]{2,1,0:T(8,128)(2,1)S(1)} %all-to-all-done.2.refs_0_.refs_1_, f32[1056,256]{1,0:T(8,128)S(1)} %copy-done.16, bf16[2,1056,512]{2,1,0:T(8,128)(2,1)S(1)} %copy-done.9, bf16[2,256,256]{2,1,0:T(8,128)(2,1)S(1)} %copy-done.12, bf16[2,256,256]{2,1,0:T(8,128)(2,1)S(1)} %copy-done.14, ...), custom_call_target="tpu_custom_call" | custom-call | flops 8000000000 | bytes 4194304 | tf_op jit(solution)/shard_map/back_kernel/pallas_call | solution.py:319
  109.8 6.9 %all-to-all-done.3.refs_0_ = bf16[16,128,256]{2,1,0:T(8,128)(2,1)S(1)} async-done(((bf16[16,128,256]{2,1,0:T(8,128)(2,1)}), bf16[16,128,256]{2,1,0:T(8,128)(2,1)S(1)}, u32[]{:S(2)}, u32[]{:S(2)}) %all-to-all-start.3) | async-done | bytes 1048608 | tf_op jit(solution)/shard_map/all_to_all | solution.py:335
  116.7 4.6 %all-to-all-start.4 = ((bf16[32,32,128]{2,1,0:T(8,128)(2,1)}), bf16[32,32,128]{2,1,0:T(8,128)(2,1)S(1)}, u32[]{:S(2)}, u32[]{:S(2)}) async-start(bf16[32,32,128]{2,1,0:T(8,128)(2,1)} %back_kernel.1), calls=%async_computation.4 | async-start | bytes 524288 | tf_op jit(solution)/shard_map/all_to_all | solution.py:335
  121.3 3.0 %collective-permute-start.2 = (bf16[512,128]{1,0:T(8,128)(2,1)S(1)}, bf16[512,128]{1,0:T(8,128)(2,1)S(1)}, u32[]{:S(2)}, u32[]{:S(2)}) collective-permute-start(bf16[512,128]{1,0:T(8,128)(2,1)S(1)} %get-tuple-element.38), channel_id=1, source_target_pairs={{0,16},{16,0},{1,17},{17,1},{2,18},{18,2},{3,19},{19,3},{4,20},{20... | collective-permute-start | bytes 393224 | tf_op jit(solution)/shard_map/ppermute | solution.py:367
  124.3 4.1 %collective-permute-done.2.refs_3_ = bf16[512,128]{1,0:T(8,128)(2,1)S(1)} collective-permute-done((bf16[512,128]{1,0:T(8,128)(2,1)S(1)}, bf16[512,128]{1,0:T(8,128)(2,1)S(1)}, u32[]{:S(2)}, u32[]{:S(2)}) %collective-permute-start.2) | collective-permute-done | bytes 131104 | tf_op jit(solution)/shard_map/ppermute | solution.py:367
  129.3 5.8 %all-to-all-done.4.refs_0_ = bf16[32,32,128]{2,1,0:T(8,128)(2,1)S(1)} async-done(((bf16[32,32,128]{2,1,0:T(8,128)(2,1)}), bf16[32,32,128]{2,1,0:T(8,128)(2,1)S(1)}, u32[]{:S(2)}, u32[]{:S(2)}) %all-to-all-start.4) | async-done | bytes 262176 | tf_op jit(solution)/shard_map/all_to_all | solution.py:335
  135.1 0.9 finish_kernel.1
  (43 shorter events, 5.9 us)
Async XLA Ops:
  7.2 51.0 %all-gather.3.cloned.1.call-start = ((), (), s32[]{:S(2)}) async-start(), calls=%async_computation.7 | async-start | bytes 1179648 | tf_op jit(solution)/shard_map/all_gather | solution.py:348
  9.9 32.4 %copy-start.12 = (bf16[2,256,256]{2,1,0:T(8,128)(2,1)S(1)}, bf16[2,256,256]{2,1,0:T(8,128)(2,1)}, u32[]{:S(2)}) copy-start(bf16[2,256,256]{2,1,0:T(8,128)(2,1)} %constant.11.clone.refs_2_.refs_3_) | copy-start | bytes 786436
  9.9 32.4 %copy-start.13 = (bf16[2,256,256]{2,1,0:T(8,128)(2,1)S(1)}, bf16[2,256,256]{2,1,0:T(8,128)(2,1)}, u32[]{:S(2)}) copy-start(bf16[2,256,256]{2,1,0:T(8,128)(2,1)} %constant.12.clone.refs_3_.refs_4_) | copy-start | bytes 786436
  9.9 26.9 %all-to-all-start = ((bf16[32,32,128]{2,1,0:T(8,128)(2,1)}), bf16[32,32,128]{2,1,0:T(8,128)(2,1)S(1)}, u32[]{:S(2)}, u32[]{:S(2)}) async-start(bf16[32,32,128]{2,1,0:T(8,128)(2,1)} %pack_kernel.1), calls=%async_computation | async-start | bytes 524288 | tf_op jit(solution)/shard_map/all_to_all | solution.py:335
  22.8 0.9 copy-start.5
  23.8 7.4 %collective-permute-start = (bf16[512,128]{1,0:T(8,128)(2,1)S(1)}, bf16[512,128]{1,0:T(8,128)(2,1)S(1)}, u32[]{:S(2)}, u32[]{:S(2)}) collective-permute-start(bf16[512,128]{1,0:T(8,128)(2,1)S(1)} %turn_kernel.1.refs_4_.refs_1_.refs_2_), channel_id=1, source_target_pairs={{0,16},{16,0},{1,17},{17,1},{2,18},{18,2},{3,19},{19,3},{4,20},{20... | collective-permute-start | bytes 393224 | tf_op jit(solution)/shard_map/ppermute | solution.py:347
  26.8 0.9 copy-start.4
  27.7 14.6 %copy-start.10 = (f32[2,528,128]{2,1,0:T(8,128)S(1)}, f32[2,528,128]{2,1,0:T(8,128)}, u32[]{:S(2)}) copy-start(f32[2,528,128]{2,1,0:T(8,128)} %constant.13.clone.refs_4_.refs_5_) | copy-start | bytes 1622020
  36.8 21.3 %all-to-all-start.1 = ((bf16[16,128,256]{2,1,0:T(8,128)(2,1)}), bf16[16,128,256]{2,1,0:T(8,128)(2,1)S(1)}, u32[]{:S(2)}, u32[]{:S(2)}) async-start(bf16[16,128,256]{2,1,0:T(8,128)(2,1)} %share_kernel.1), calls=%async_computation.1 | async-start | bytes 2097152 | tf_op jit(solution)/shard_map/all_to_all | solution.py:335
  42.3 1.7 %copy-start.6 = (bf16[2,512,1056]{2,1,0:T(8,128)(2,1)S(1)}, bf16[2,512,1056]{2,1,0:T(8,128)(2,1)}, u32[]{:S(2)}) copy-start(bf16[2,512,1056]{2,1,0:T(8,128)(2,1)} %constant.14.clone.refs_5_.refs_6_) | copy-start | bytes 6488068
  44.0 1.6 %copy-start.8 = (bf16[2,1056,512]{2,1,0:T(8,128)(2,1)S(1)}, bf16[2,1056,512]{2,1,0:T(8,128)(2,1)}, u32[]{:S(2)}) copy-start(bf16[2,1056,512]{2,1,0:T(8,128)(2,1)} %constant.10.clone.refs_1_.refs_2_) | copy-start | bytes 6488068
  50.6 1.0 copy-start.15
  58.1 5.3 %collective-permute-start.1 = (bf16[8,512,128]{2,1,0:T(8,128)(2,1)}, bf16[8,512,128]{2,1,0:T(8,128)(2,1)S(1)}, u32[]{:S(2)}, u32[]{:S(2)}) collective-permute-start(bf16[8,512,128]{2,1,0:T(8,128)(2,1)} %bitcast.2), channel_id=1, source_target_pairs={{0,8},{8,0},{1,9},{9,1},{2,10},{10,2},{3,11},{11,3},{4,12},{12,4},... | collective-permute-start | bytes 3145736 | tf_op jit(solution)/shard_map/ppermute | solution.py:359
  61.0 1.2 copy-start
  64.7 21.3 %all-to-all-start.2 = ((bf16[32,64,128]{2,1,0:T(8,128)(2,1)}), bf16[32,64,128]{2,1,0:T(8,128)(2,1)S(1)}, u32[]{:S(2)}, u32[]{:S(2)}) async-start(bf16[32,64,128]{2,1,0:T(8,128)(2,1)} %get-tuple-element.34), calls=%async_computation.2 | async-start | bytes 1048576 | tf_op jit(solution)/shard_map/all_to_all | solution.py:335
  68.7 67.4 %reduce-scatter.2.cloned.1.call-start = ((), (), s32[]{:S(2)}) async-start(), calls=%async_computation.6 | async-start | bytes 2359296 | tf_op jit(solution)/shard_map/reduce_scatter | solution.py:377
  68.7 21.9 %collective-permute-start.6 = (bf16[16,128,256]{2,1,0:T(8,128)(2,1)S(1)}, bf16[16,128,256]{2,1,0:T(8,128)(2,1)}, u32[]{:S(2)}, u32[]{:S(2)}) collective-permute-start(bf16[16,128,256]{2,1,0:T(8,128)(2,1)S(1)} %all-to-all-done.1.refs_1_.refs_2_.refs_6_), channel_id=1, source_target_pairs={{0,8},{8,0},{1,9},{9,1},{2,10},{10,2},{3,11},{11,3},{4,12},{12,4},... | collective-permute-start | bytes 3145736 | tf_op jit(solution)/shard_map/ppermute | solution.py:360
  86.0 4.5 %collective-permute-start.3 = (bf16[32,64,128]{2,1,0:T(8,128)(2,1)S(1)}, bf16[32,64,128]{2,1,0:T(8,128)(2,1)S(1)}, u32[]{:S(2)}, u32[]{:S(2)}) collective-permute-start(bf16[32,64,128]{2,1,0:T(8,128)(2,1)S(1)} %all-to-all-done.2.refs_0_.refs_1_), channel_id=1, source_target_pairs={{0,8},{8,0},{1,9},{9,1},{2,10},{10,2},{3,11},{11,3},{4,12},{12,4},... | collective-permute-start | bytes 1572872 | tf_op jit(solution)/shard_map/ppermute | solution.py:369
  87.0 3.5 %collective-permute-start.4 = (bf16[512,128]{1,0:T(8,128)(2,1)S(1)}, bf16[512,128]{1,0:T(8,128)(2,1)S(1)}, u32[]{:S(2)}, u32[]{:S(2)}) collective-permute-start(bf16[512,128]{1,0:T(8,128)(2,1)S(1)} %turn_kernel.1.refs_4_.refs_1_.refs_2_), channel_id=1, source_target_pairs={{0,8},{8,0},{1,9},{9,1},{2,10},{10,2},{3,11},{11,3},{4,12},{12,4},... | collective-permute-start | bytes 393224 | tf_op jit(solution)/shard_map/ppermute | solution.py:351
  87.0 3.5 %collective-permute-start.5 = (bf16[512,128]{1,0:T(8,128)(2,1)S(1)}, bf16[512,128]{1,0:T(8,128)(2,1)S(1)}, u32[]{:S(2)}, u32[]{:S(2)}) collective-permute-start(bf16[512,128]{1,0:T(8,128)(2,1)S(1)} %collective-permute-done.refs_5_.refs_2_.refs_3_), channel_id=1, source_target_pairs={{0,8},{8,0},{1,9},{9,1},{2,10},{10,2},{3,11},{11,3},{4,12},{12,4},... | collective-permute-start | bytes 393224 | tf_op jit(solution)/shard_map/ppermute | solution.py:351
  87.5 1.2 copy-start.1
  93.7 4.7 %copy-start.11 = (f32[2,528,128]{2,1,0:T(8,128)S(1)}, f32[2,528,128]{2,1,0:T(8,128)}, u32[]{:S(2)}) copy-start(f32[2,528,128]{2,1,0:T(8,128)} %constant.13.clone.refs_4_.refs_5_) | copy-start | bytes 1622020
  93.7 4.7 %copy-start.14 = (bf16[2,256,256]{2,1,0:T(8,128)(2,1)S(1)}, bf16[2,256,256]{2,1,0:T(8,128)(2,1)}, u32[]{:S(2)}) copy-start(bf16[2,256,256]{2,1,0:T(8,128)(2,1)} %constant.12.clone.refs_3_.refs_4_) | copy-start | bytes 786436
  93.7 23.0 %all-to-all-start.3 = ((bf16[16,128,256]{2,1,0:T(8,128)(2,1)}), bf16[16,128,256]{2,1,0:T(8,128)(2,1)S(1)}, u32[]{:S(2)}, u32[]{:S(2)}) async-start(bf16[16,128,256]{2,1,0:T(8,128)(2,1)} %project_kernel.1), calls=%async_computation.3 | async-start | bytes 2097152 | tf_op jit(solution)/shard_map/all_to_all | solution.py:335
  98.4 1.7 %copy-start.7 = (bf16[2,512,1056]{2,1,0:T(8,128)(2,1)S(1)}, bf16[2,512,1056]{2,1,0:T(8,128)(2,1)}, u32[]{:S(2)}) copy-start(bf16[2,512,1056]{2,1,0:T(8,128)(2,1)} %constant.14.clone.refs_5_.refs_6_) | copy-start | bytes 6488068
  100.1 1.6 %copy-start.9 = (bf16[2,1056,512]{2,1,0:T(8,128)(2,1)S(1)}, bf16[2,1056,512]{2,1,0:T(8,128)(2,1)}, u32[]{:S(2)}) copy-start(bf16[2,1056,512]{2,1,0:T(8,128)(2,1)} %constant.10.clone.refs_1_.refs_2_) | copy-start | bytes 6488068
  101.7 1.2 copy-start.16
  109.8 25.3 %copy-start.2 = (bf16[128,512]{1,0:T(8,128)(2,1)S(1)}, bf16[128,512]{1,0:T(8,128)(2,1)}, u32[]{:S(2)}) copy-start(bf16[128,512]{1,0:T(8,128)(2,1)} %refs_1_.4) | copy-start | bytes 393220
  109.8 25.3 %copy-start.3 = (bf16[128,512]{1,0:T(8,128)(2,1)S(1)}, bf16[128,512]{1,0:T(8,128)(2,1)}, u32[]{:S(2)}) copy-start(bf16[128,512]{1,0:T(8,128)(2,1)} %refs_2_.5) | copy-start | bytes 393220
  116.7 18.4 %all-to-all-start.4 = ((bf16[32,32,128]{2,1,0:T(8,128)(2,1)}), bf16[32,32,128]{2,1,0:T(8,128)(2,1)S(1)}, u32[]{:S(2)}, u32[]{:S(2)}) async-start(bf16[32,32,128]{2,1,0:T(8,128)(2,1)} %back_kernel.1), calls=%async_computation.4 | async-start | bytes 524288 | tf_op jit(solution)/shard_map/all_to_all | solution.py:335
  121.3 7.1 %collective-permute-start.2 = (bf16[512,128]{1,0:T(8,128)(2,1)S(1)}, bf16[512,128]{1,0:T(8,128)(2,1)S(1)}, u32[]{:S(2)}, u32[]{:S(2)}) collective-permute-start(bf16[512,128]{1,0:T(8,128)(2,1)S(1)} %get-tuple-element.38), channel_id=1, source_target_pairs={{0,16},{16,0},{1,17},{17,1},{2,18},{18,2},{3,19},{19,3},{4,20},{20... | collective-permute-start | bytes 393224 | tf_op jit(solution)/shard_map/ppermute | solution.py:367
Sparse Core Ops, SparseCore 0:
  9.8 40.9 all-gather.2
  93.8 31.5 reduce-scatter.1

commit v4 on v3

--- a/solution.py
+++ b/solution.py
@@ -156,7 +156,8 @@
     return total
 
 
-def own_grad_kernel(own, cot, out):
+def own_grad_kernel(own, cot, out, side):
+    side[...] = cot[:, :, LANE:]
     out[...] = partial_grad(own, cot, 0)
 
 
@@ -207,7 +208,7 @@
         columns = []
         for y in (z, z + 1):
             rows = [cot[h * C + y, :, :LANE] for h in range(H)]
-            rows += [cot_other[h * C + y, :, LANE:] for h in range(H)]
+            rows += [cot_other[h * C + y] for h in range(H)]
             columns.append(jnp.concatenate(rows, axis=0))
         grad = dot(mixed, jnp.concatenate(columns, axis=1)) * SCALE
         out[z] = grad[:, :LANE].astype(out.dtype)
@@ -357,13 +358,17 @@
     )
     own, cot, conv = lax.optimization_barrier((own, cot, conv))
     other = lax.ppermute(own, "k", core_pair)
-    cot_other = lax.ppermute(cot, "k", core_pair)
-    (own_part,) = call(own_grad_kernel, [((WIDE, H * LANE), F32)], own, cot)
+    own_part, side = call(
+        own_grad_kernel,
+        [((WIDE, H * LANE), F32), ((H * C, LANE, LANE), BF)],
+        own, cot,
+    )
     sent, kept, passed = call(
         grad_kernel,
         [((HALF, 4 * CH, LANE), BF), ((WIDE, LANE), F32), ((WIDE, LANE), BF)],
         own_part, other, cot, conv, *query,
     )
+    cot_other = lax.ppermute(side, "k", core_pair)
     received = lax.ppermute(passed, "h", core_pair)
     moved = exchange(sent, SEQ)
     moved_other = lax.ppermute(moved, "k", core_pair)
@@ -372,7 +377,7 @@
     (weight_part,) = call(
         weight_kernel,
         [((Z, WIDE, LANE), F32)],
-        moved, moved_other, *query, *query_other, cot, cot_other, stream=True,
+        moved, moved_other, *query, *query_other, cot, cot_other, late=(7,), stream=True,
     )
     weight_grad = lax.psum_scatter(
         weight_part.reshape(Z * WIDE, LANE), "z", scatter_dimension=0, tiled=True

time: 144 us -> 141 us (0.979)
  blocking collectives: 0 us -> 20.6 us
  waiting for transfers between devices: 49.7 us -> 31.5 us
  starting transfers between devices: 42.3 us -> 38.8 us
  Pallas kernels: 23.4 us -> 21.9 us
    all_to_all x0 -> x1, blocking collectives: none -> 20.6 us  [exchange(): return lax.all_to_all(x, axes, split_axis=0, concat_axis=0, tiled=True)]
    all_to_all x5 -> x4, waiting for transfers between devices: 41.7 us -> 23.3 us  [exchange(): return lax.all_to_all(x, axes, split_axis=0, concat_axis=0, tiled=True)]
    all_to_all x5 -> x4, starting transfers between devices: 31.5 us -> 28.2 us  [exchange(): return lax.all_to_all(x, axes, split_axis=0, concat_axis=0, tiled=True)]
    pallas_call x11, Pallas kernels: 23.4 us -> 21.9 us  [call(): pl.pallas_call(body, out_shape=shapes, in_specs=[pl.BlockSpec(memory_spac...]
    unnamed x34 -> x30, local copies, waits for them, and re-layouts: 13.2 us -> 13.4 us
  transfers between devices with their start and end apart: 14 -> 13, of which waited for: 8 -> 9; matrix products, arithmetic and copies ran while one was open for 0% -> 0% of each run, Pallas kernels for 13% -> 14%
where the time goes in v4:
time: 141 us
  starting transfers between devices  38.8 us (28%)
  waiting for transfers between devices  31.5 us (22%)
  Pallas kernels  21.9 us (16%)
  blocking collectives  20.6 us (15%)
  between operations  14.2 us (10%)
  local copies, waits for them, and re-layouts  13.4 us (10%)
    all_to_all x4, starting transfers between devices, exchange(): return lax.all_to_all(x, axes, split_axis=0, concat_axis=0, tiled=True)  28.2 us
    all_to_all x4, waiting for transfers between devices, exchange(): return lax.all_to_all(x, axes, split_axis=0, concat_axis=0, tiled=True)  23.3 us
    pallas_call x11, Pallas kernels, call(): pl.pallas_call(body, out_shape=shapes, in_specs=[pl.BlockSpec(memory_spac...  21.9 us
    all_to_all x1, blocking collectives, exchange(): return lax.all_to_all(x, axes, split_axis=0, concat_axis=0, tiled=True)  20.6 us
    unnamed x30, local copies, waits for them, and re-layouts  13.4 us
    ppermute x1, waiting for transfers between devices, local(): received = lax.ppermute(passed, 'h', core_pair)  4.16 us
    ppermute x1, starting transfers between devices, local(): received = lax.ppermute(passed, 'h', core_pair)  2.98 us
    ppermute x1, starting transfers between devices, local(): query = (query_t, lax.ppermute(query_t, 'h', core_pair))  2.98 us
  transfers between devices with their start and end apart: 13, of which 9 were waited for; matrix products, arithmetic and copies ran while one was open for 0% of the time, Pallas kernels for 14%

profile of v4, /device:TPU:1, one launch (start us, length us, event | category | flops | bytes accessed | tf_op | source)
XLA Modules:
  0.0 140.5 jit_solution(7727806688629994186)
XLA Ops:
  7.9 1.9 %pack_kernel.1 = bf16[32,32,128]{2,1,0:T(8,128)(2,1)} custom-call(bf16[128,512]{1,0:T(8,128)(2,1)} %refs_1_.4, bf16[128,512]{1,0:T(8,128)(2,1)} %refs_2_.5, f32[128,512]{1,0:T(8,128)} %refs_2_.4), custom_call_target="tpu_custom_call" | custom-call | bytes 4194304 | tf_op jit(solution)/shard_map/pack_kernel/pallas_call | solution.py:320
  9.9 12.9 %all-to-all-start = ((bf16[32,32,128]{2,1,0:T(8,128)(2,1)}), bf16[32,32,128]{2,1,0:T(8,128)(2,1)S(1)}, u32[]{:S(2)}, u32[]{:S(2)}) async-start(bf16[32,32,128]{2,1,0:T(8,128)(2,1)} %pack_kernel.1), calls=%async_computation | async-start | bytes 524288 | tf_op jit(solution)/shard_map/all_to_all | solution.py:336
  23.8 3.0 %collective-permute-start = (bf16[512,128]{1,0:T(8,128)(2,1)S(1)}, bf16[512,128]{1,0:T(8,128)(2,1)S(1)}, u32[]{:S(2)}, u32[]{:S(2)}) collective-permute-start(bf16[512,128]{1,0:T(8,128)(2,1)S(1)} %turn_kernel.1.refs_4_.refs_1_.refs_2_), channel_id=1, source_target_pairs={{0,16},{16,0},{1,17},{17,1},{2,18},{18,2},{3,19},{19,3},{4,20},{20... | collective-permute-start | bytes 393224 | tf_op jit(solution)/shard_map/ppermute | solution.py:348
  26.8 0.9 copy-done.4
  27.7 1.1 share_kernel.1
  28.8 2.4 %collective-permute-done.refs_5_.refs_2_.refs_3_ = bf16[512,128]{1,0:T(8,128)(2,1)S(1)} collective-permute-done((bf16[512,128]{1,0:T(8,128)(2,1)S(1)}, bf16[512,128]{1,0:T(8,128)(2,1)S(1)}, u32[]{:S(2)}, u32[]{:S(2)}) %collective-permute-start) | collective-permute-done | bytes 131104 | tf_op jit(solution)/shard_map/ppermute | solution.py:348
  31.2 5.6 %all-to-all-done.refs_0_ = bf16[32,32,128]{2,1,0:T(8,128)(2,1)S(1)} async-done(((bf16[32,32,128]{2,1,0:T(8,128)(2,1)}), bf16[32,32,128]{2,1,0:T(8,128)(2,1)S(1)}, u32[]{:S(2)}, u32[]{:S(2)}) %all-to-all-start) | async-done | bytes 262176 | tf_op jit(solution)/shard_map/all_to_all | solution.py:336
  36.8 5.5 %all-to-all-start.1 = ((bf16[16,128,256]{2,1,0:T(8,128)(2,1)}), bf16[16,128,256]{2,1,0:T(8,128)(2,1)S(1)}, u32[]{:S(2)}, u32[]{:S(2)}) async-start(bf16[16,128,256]{2,1,0:T(8,128)(2,1)} %share_kernel.1), calls=%async_computation.1 | async-start | bytes 2097152 | tf_op jit(solution)/shard_map/all_to_all | solution.py:336
  42.4 1.7 %copy-done.6 = bf16[2,512,1056]{2,1,0:T(8,128)(2,1)S(1)} copy-done((bf16[2,512,1056]{2,1,0:T(8,128)(2,1)S(1)}, bf16[2,512,1056]{2,1,0:T(8,128)(2,1)}, u32[]{:S(2)}) %copy-start.6) | copy-done | bytes 2162712
  44.0 1.6 %copy-done.8 = bf16[2,1056,512]{2,1,0:T(8,128)(2,1)S(1)} copy-done((bf16[2,1056,512]{2,1,0:T(8,128)(2,1)S(1)}, bf16[2,1056,512]{2,1,0:T(8,128)(2,1)}, u32[]{:S(2)}) %copy-start.8) | copy-done | bytes 2162712
  45.7 4.9 %conv_kernel.1 = (bf16[512,128]{1,0:T(8,128)(2,1)S(1)}, f32[1056,256]{1,0:T(8,128)S(1)}) custom-call(bf16[32,32,128]{2,1,0:T(8,128)(2,1)S(1)} %all-to-all-done.refs_0_, bf16[2,1056,512]{2,1,0:T(8,128)(2,1)S(1)} %copy-done.8, bf16[2,256,256]{2,1,0:T(8,128)(2,1)S(1)} %copy-done.11, bf16[2,256,256]{2,1,0:T(8,128)(2,1)S(1)} %copy-done.12, ...), custom_call_target="tpu_custom_call" | custom-call | flops 5000000000 | bytes 4194304 | tf_op jit(solution)/shard_map/conv_kernel/pallas_call | solution.py:320
  50.6 1.0 copy-done.13
  51.6 6.5 %all-to-all-done.1.refs_1_.refs_2_.refs_6_ = bf16[16,128,256]{2,1,0:T(8,128)(2,1)S(1)} async-done(((bf16[16,128,256]{2,1,0:T(8,128)(2,1)}), bf16[16,128,256]{2,1,0:T(8,128)(2,1)S(1)}, u32[]{:S(2)}, u32[]{:S(2)}) %all-to-all-start.1) | async-done | bytes 1048608 | tf_op jit(solution)/shard_map/all_to_all | solution.py:336
  58.1 2.8 %collective-permute-start.1 = (bf16[8,512,128]{2,1,0:T(8,128)(2,1)}, bf16[8,512,128]{2,1,0:T(8,128)(2,1)S(1)}, u32[]{:S(2)}, u32[]{:S(2)}) collective-permute-start(bf16[8,512,128]{2,1,0:T(8,128)(2,1)} %bitcast.3), channel_id=1, source_target_pairs={{0,8},{8,0},{1,9},{9,1},{2,10},{10,2},{3,11},{11,3},{4,12},{12,4},... | collective-permute-start | bytes 3145736 | tf_op jit(solution)/shard_map/ppermute | solution.py:360
  61.0 1.2 copy-done.1
  63.9 20.6 %all_to_all.25.refs_0_.refs_1_ = bf16[32,64,128]{2,1,0:T(8,128)(2,1)S(1)} all-to-all(bf16[32,64,128]{2,1,0:T(8,128)(2,1)S(1)} %get-tuple-element.37), channel_id=1, replica_groups=mesh['z'=8,'h'=2,'k'=2,'chan'=8] {'z','h','k'}, dimensions={0} | all-to-all | bytes 1048576 | tf_op jit(solution)/shard_map/all_to_all | solution.py:336
  84.5 1.3 collective-permute-start.3
  86.3 1.8 %project_kernel.1 = bf16[16,128,256]{2,1,0:T(8,128)(2,1)} custom-call(bf16[32,64,128]{2,1,0:T(8,128)(2,1)S(1)} %all_to_all.25.refs_0_.refs_1_, bf16[512,128]{1,0:T(8,128)(2,1)S(1)} %turn_kernel.1.refs_4_.refs_1_.refs_2_, bf16[512,128]{1,0:T(8,128)(2,1)S(1)} %collective-permute-done.refs_5_.refs_2_.refs_3_, bf16[8,512,128]{2,1,0:T(8,128)(2,1)S(1)} %bitcast.5, ...), custom_call_target="tpu_custom_call" | custom-call | bytes 4194304 | tf_op jit(solution)/shard_map/project_kernel/pallas_call | solution.py:320
  88.5 2.3 %weight_kernel.1 = f32[8,512,128]{2,1,0:T(8,128)S(1)} custom-call(bf16[32,64,128]{2,1,0:T(8,128)(2,1)S(1)} %all_to_all.25.refs_0_.refs_1_, bf16[32,64,128]{2,1,0:T(8,128)(2,1)S(1)} %collective-permute-done.3.refs_1_, bf16[512,128]{1,0:T(8,128)(2,1)S(1)} %turn_kernel.1.refs_4_.refs_1_.refs_2_, ...), custom_call_target="tpu_custom_call" | custom-call | bytes 4194304 | tf_op jit(solution)/shard_map/weight_kernel/pallas_call | solution.py:320
  90.8 1.4 copy-done
  92.2 4.7 %all-to-all-start.3 = ((bf16[16,128,256]{2,1,0:T(8,128)(2,1)}), bf16[16,128,256]{2,1,0:T(8,128)(2,1)S(1)}, u32[]{:S(2)}, u32[]{:S(2)}) async-start(bf16[16,128,256]{2,1,0:T(8,128)(2,1)} %project_kernel.1), calls=%async_computation.3 | async-start | bytes 2097152 | tf_op jit(solution)/shard_map/all_to_all | solution.py:336
  96.9 1.8 %copy-done.7 = bf16[2,512,1056]{2,1,0:T(8,128)(2,1)S(1)} copy-done((bf16[2,512,1056]{2,1,0:T(8,128)(2,1)S(1)}, bf16[2,512,1056]{2,1,0:T(8,128)(2,1)}, u32[]{:S(2)}) %copy-start.7) | copy-done | bytes 2162712
  98.7 1.6 %copy-done.9 = bf16[2,1056,512]{2,1,0:T(8,128)(2,1)S(1)} copy-done((bf16[2,1056,512]{2,1,0:T(8,128)(2,1)S(1)}, bf16[2,1056,512]{2,1,0:T(8,128)(2,1)}, u32[]{:S(2)}) %copy-start.9) | copy-done | bytes 2162712
  100.4 1.2 copy-done.14
  101.6 6.8 %back_kernel.1 = bf16[32,32,128]{2,1,0:T(8,128)(2,1)} custom-call(bf16[32,64,128]{2,1,0:T(8,128)(2,1)S(1)} %all_to_all.25.refs_0_.refs_1_, f32[1056,256]{1,0:T(8,128)S(1)} %copy-done.14, bf16[2,1056,512]{2,1,0:T(8,128)(2,1)S(1)} %copy-done.9, bf16[2,256,256]{2,1,0:T(8,128)(2,1)S(1)} %copy-done.11, bf16[2,256,256]{2,1,0:T(8,128)(2,1)S(1)} %copy-done.12, ...), custom_call_target="tpu_custom_call" | custom-call | flops 8000000000 | bytes 4194304 | tf_op jit(solution)/shard_map/back_kernel/pallas_call | solution.py:320
  108.5 5.9 %all-to-all-done.3.refs_0_ = bf16[16,128,256]{2,1,0:T(8,128)(2,1)S(1)} async-done(((bf16[16,128,256]{2,1,0:T(8,128)(2,1)}), bf16[16,128,256]{2,1,0:T(8,128)(2,1)S(1)}, u32[]{:S(2)}, u32[]{:S(2)}) %all-to-all-start.3) | async-done | bytes 1048608 | tf_op jit(solution)/shard_map/all_to_all | solution.py:336
  114.3 5.1 %all-to-all-start.4 = ((bf16[32,32,128]{2,1,0:T(8,128)(2,1)}), bf16[32,32,128]{2,1,0:T(8,128)(2,1)S(1)}, u32[]{:S(2)}, u32[]{:S(2)}) async-start(bf16[32,32,128]{2,1,0:T(8,128)(2,1)} %back_kernel.1), calls=%async_computation.4 | async-start | bytes 524288 | tf_op jit(solution)/shard_map/all_to_all | solution.py:336
  119.4 3.0 %collective-permute-start.2 = (bf16[512,128]{1,0:T(8,128)(2,1)S(1)}, bf16[512,128]{1,0:T(8,128)(2,1)S(1)}, u32[]{:S(2)}, u32[]{:S(2)}) collective-permute-start(bf16[512,128]{1,0:T(8,128)(2,1)S(1)} %get-tuple-element.41), channel_id=1, source_target_pairs={{0,16},{16,0},{1,17},{17,1},{2,18},{18,2},{3,19},{19,3},{4,20},{20... | collective-permute-start | bytes 393224 | tf_op jit(solution)/shard_map/ppermute | solution.py:372
  122.4 4.2 %collective-permute-done.2.refs_3_ = bf16[512,128]{1,0:T(8,128)(2,1)S(1)} collective-permute-done((bf16[512,128]{1,0:T(8,128)(2,1)S(1)}, bf16[512,128]{1,0:T(8,128)(2,1)S(1)}, u32[]{:S(2)}, u32[]{:S(2)}) %collective-permute-start.2) | collective-permute-done | bytes 131104 | tf_op jit(solution)/shard_map/ppermute | solution.py:372
  126.6 0.9 sum_kernel.1
  127.5 5.3 %all-to-all-done.4.refs_0_ = bf16[32,32,128]{2,1,0:T(8,128)(2,1)S(1)} async-done(((bf16[32,32,128]{2,1,0:T(8,128)(2,1)}), bf16[32,32,128]{2,1,0:T(8,128)(2,1)S(1)}, u32[]{:S(2)}, u32[]{:S(2)}) %all-to-all-start.4) | async-done | bytes 262176 | tf_op jit(solution)/shard_map/all_to_all | solution.py:336
  132.8 0.9 finish_kernel.1
  (38 shorter events, 4.4 us)
Async XLA Ops:
  7.2 51.0 %all-gather.3.cloned.1.call-start = ((), (), s32[]{:S(2)}) async-start(), calls=%async_computation.7 | async-start | bytes 1179648 | tf_op jit(solution)/shard_map/all_gather | solution.py:349
  9.9 32.5 %copy-start.11 = (bf16[2,256,256]{2,1,0:T(8,128)(2,1)S(1)}, bf16[2,256,256]{2,1,0:T(8,128)(2,1)}, u32[]{:S(2)}) copy-start(bf16[2,256,256]{2,1,0:T(8,128)(2,1)} %constant.11.clone.refs_2_.refs_3_) | copy-start | bytes 786436
  9.9 32.5 %copy-start.12 = (bf16[2,256,256]{2,1,0:T(8,128)(2,1)S(1)}, bf16[2,256,256]{2,1,0:T(8,128)(2,1)}, u32[]{:S(2)}) copy-start(bf16[2,256,256]{2,1,0:T(8,128)(2,1)} %constant.12.clone.refs_3_.refs_4_) | copy-start | bytes 786436
  9.9 26.9 %all-to-all-start = ((bf16[32,32,128]{2,1,0:T(8,128)(2,1)}), bf16[32,32,128]{2,1,0:T(8,128)(2,1)S(1)}, u32[]{:S(2)}, u32[]{:S(2)}) async-start(bf16[32,32,128]{2,1,0:T(8,128)(2,1)} %pack_kernel.1), calls=%async_computation | async-start | bytes 524288 | tf_op jit(solution)/shard_map/all_to_all | solution.py:336
  22.8 0.9 copy-start.5
  23.8 7.4 %collective-permute-start = (bf16[512,128]{1,0:T(8,128)(2,1)S(1)}, bf16[512,128]{1,0:T(8,128)(2,1)S(1)}, u32[]{:S(2)}, u32[]{:S(2)}) collective-permute-start(bf16[512,128]{1,0:T(8,128)(2,1)S(1)} %turn_kernel.1.refs_4_.refs_1_.refs_2_), channel_id=1, source_target_pairs={{0,16},{16,0},{1,17},{17,1},{2,18},{18,2},{3,19},{19,3},{4,20},{20... | collective-permute-start | bytes 393224 | tf_op jit(solution)/shard_map/ppermute | solution.py:348
  26.8 0.9 copy-start.4
  27.7 14.7 %copy-start.10 = (f32[2,528,128]{2,1,0:T(8,128)S(1)}, f32[2,528,128]{2,1,0:T(8,128)}, u32[]{:S(2)}) copy-start(f32[2,528,128]{2,1,0:T(8,128)} %constant.13.clone.refs_4_.refs_5_) | copy-start | bytes 1622020
  36.8 21.3 %all-to-all-start.1 = ((bf16[16,128,256]{2,1,0:T(8,128)(2,1)}), bf16[16,128,256]{2,1,0:T(8,128)(2,1)S(1)}, u32[]{:S(2)}, u32[]{:S(2)}) async-start(bf16[16,128,256]{2,1,0:T(8,128)(2,1)} %share_kernel.1), calls=%async_computation.1 | async-start | bytes 2097152 | tf_op jit(solution)/shard_map/all_to_all | solution.py:336
  42.3 91.4 %reduce-scatter.2.cloned.1.call-start = ((), (), s32[]{:S(2)}) async-start(), calls=%async_computation.6 | async-start | bytes 2359296 | tf_op jit(solution)/shard_map/reduce_scatter | solution.py:382
  42.4 1.7 %copy-start.6 = (bf16[2,512,1056]{2,1,0:T(8,128)(2,1)S(1)}, bf16[2,512,1056]{2,1,0:T(8,128)(2,1)}, u32[]{:S(2)}) copy-start(bf16[2,512,1056]{2,1,0:T(8,128)(2,1)} %constant.14.clone.refs_5_.refs_6_) | copy-start | bytes 6488068
  44.0 1.6 %copy-start.8 = (bf16[2,1056,512]{2,1,0:T(8,128)(2,1)S(1)}, bf16[2,1056,512]{2,1,0:T(8,128)(2,1)}, u32[]{:S(2)}) copy-start(bf16[2,1056,512]{2,1,0:T(8,128)(2,1)} %constant.10.clone.refs_1_.refs_2_) | copy-start | bytes 6488068
  50.6 1.0 copy-start.13
  58.1 5.3 %collective-permute-start.1 = (bf16[8,512,128]{2,1,0:T(8,128)(2,1)}, bf16[8,512,128]{2,1,0:T(8,128)(2,1)S(1)}, u32[]{:S(2)}, u32[]{:S(2)}) collective-permute-start(bf16[8,512,128]{2,1,0:T(8,128)(2,1)} %bitcast.3), channel_id=1, source_target_pairs={{0,8},{8,0},{1,9},{9,1},{2,10},{10,2},{3,11},{11,3},{4,12},{12,4},... | collective-permute-start | bytes 3145736 | tf_op jit(solution)/shard_map/ppermute | solution.py:360
  61.0 1.2 copy-start.1
  84.5 3.6 %collective-permute-start.3 = (bf16[32,64,128]{2,1,0:T(8,128)(2,1)S(1)}, bf16[32,64,128]{2,1,0:T(8,128)(2,1)S(1)}, u32[]{:S(2)}, u32[]{:S(2)}) collective-permute-start(bf16[32,64,128]{2,1,0:T(8,128)(2,1)S(1)} %all_to_all.25.refs_0_.refs_1_), channel_id=1, source_target_pairs={{0,8},{8,0},{1,9},{9,1},{2,10},{10,2},{3,11},{11,3},{4,12},{12,4},... | collective-permute-start | bytes 1572872 | tf_op jit(solution)/shard_map/ppermute | solution.py:374
  85.8 2.7 %collective-permute-start.6 = (bf16[16,128,128]{2,1,0:T(8,128)(2,1)S(1)}, bf16[16,128,128]{2,1,0:T(8,128)(2,1)S(1)}, u32[]{:S(2)}, u32[]{:S(2)}) collective-permute-start(bf16[16,128,128]{2,1,0:T(8,128)(2,1)S(1)} %get-tuple-element.49), channel_id=1, source_target_pairs={{0,8},{8,0},{1,9},{9,1},{2,10},{10,2},{3,11},{11,3},{4,12},{12,4},... | collective-permute-start | bytes 1572872 | tf_op jit(solution)/shard_map/ppermute | solution.py:371
  85.8 2.5 %collective-permute-start.4 = (bf16[512,128]{1,0:T(8,128)(2,1)S(1)}, bf16[512,128]{1,0:T(8,128)(2,1)S(1)}, u32[]{:S(2)}, u32[]{:S(2)}) collective-permute-start(bf16[512,128]{1,0:T(8,128)(2,1)S(1)} %turn_kernel.1.refs_4_.refs_1_.refs_2_), channel_id=1, source_target_pairs={{0,8},{8,0},{1,9},{9,1},{2,10},{10,2},{3,11},{11,3},{4,12},{12,4},... | collective-permute-start | bytes 393224 | tf_op jit(solution)/shard_map/ppermute | solution.py:352
  86.3 2.2 %collective-permute-start.5 = (bf16[512,128]{1,0:T(8,128)(2,1)S(1)}, bf16[512,128]{1,0:T(8,128)(2,1)S(1)}, u32[]{:S(2)}, u32[]{:S(2)}) collective-permute-start(bf16[512,128]{1,0:T(8,128)(2,1)S(1)} %collective-permute-done.refs_5_.refs_2_.refs_3_), channel_id=1, source_target_pairs={{0,8},{8,0},{1,9},{9,1},{2,10},{10,2},{3,11},{11,3},{4,12},{12,4},... | collective-permute-start | bytes 393224 | tf_op jit(solution)/shard_map/ppermute | solution.py:352
  90.8 1.4 copy-start
  92.2 22.1 %all-to-all-start.3 = ((bf16[16,128,256]{2,1,0:T(8,128)(2,1)}), bf16[16,128,256]{2,1,0:T(8,128)(2,1)S(1)}, u32[]{:S(2)}, u32[]{:S(2)}) async-start(bf16[16,128,256]{2,1,0:T(8,128)(2,1)} %project_kernel.1), calls=%async_computation.3 | async-start | bytes 2097152 | tf_op jit(solution)/shard_map/all_to_all | solution.py:336
  96.9 1.8 %copy-start.7 = (bf16[2,512,1056]{2,1,0:T(8,128)(2,1)S(1)}, bf16[2,512,1056]{2,1,0:T(8,128)(2,1)}, u32[]{:S(2)}) copy-start(bf16[2,512,1056]{2,1,0:T(8,128)(2,1)} %constant.14.clone.refs_5_.refs_6_) | copy-start | bytes 6488068
  98.7 1.6 %copy-start.9 = (bf16[2,1056,512]{2,1,0:T(8,128)(2,1)S(1)}, bf16[2,1056,512]{2,1,0:T(8,128)(2,1)}, u32[]{:S(2)}) copy-start(bf16[2,1056,512]{2,1,0:T(8,128)(2,1)} %constant.10.clone.refs_1_.refs_2_) | copy-start | bytes 6488068
  100.4 1.2 copy-start.14
  108.4 24.3 %copy-start.2 = (bf16[128,512]{1,0:T(8,128)(2,1)S(1)}, bf16[128,512]{1,0:T(8,128)(2,1)}, u32[]{:S(2)}) copy-start(bf16[128,512]{1,0:T(8,128)(2,1)} %refs_1_.4) | copy-start | bytes 393220
  108.5 24.3 %copy-start.3 = (bf16[128,512]{1,0:T(8,128)(2,1)S(1)}, bf16[128,512]{1,0:T(8,128)(2,1)}, u32[]{:S(2)}) copy-start(bf16[128,512]{1,0:T(8,128)(2,1)} %refs_2_.5) | copy-start | bytes 393220
  114.3 18.4 %all-to-all-start.4 = ((bf16[32,32,128]{2,1,0:T(8,128)(2,1)}), bf16[32,32,128]{2,1,0:T(8,128)(2,1)S(1)}, u32[]{:S(2)}, u32[]{:S(2)}) async-start(bf16[32,32,128]{2,1,0:T(8,128)(2,1)} %back_kernel.1), calls=%async_computation.4 | async-start | bytes 524288 | tf_op jit(solution)/shard_map/all_to_all | solution.py:336
  119.4 7.1 %collective-permute-start.2 = (bf16[512,128]{1,0:T(8,128)(2,1)S(1)}, bf16[512,128]{1,0:T(8,128)(2,1)S(1)}, u32[]{:S(2)}, u32[]{:S(2)}) collective-permute-start(bf16[512,128]{1,0:T(8,128)(2,1)S(1)} %get-tuple-element.41), channel_id=1, source_target_pairs={{0,16},{16,0},{1,17},{17,1},{2,18},{18,2},{3,19},{19,3},{4,20},{20... | collective-permute-start | bytes 393224 | tf_op jit(solution)/shard_map/ppermute | solution.py:372
Sparse Core Ops, SparseCore 0:
  9.8 40.9 all-gather.2
  92.3 32.0 reduce-scatter.1

commit v5 on v4

--- a/solution.py
+++ b/solution.py
@@ -294,7 +294,7 @@
 
 
 def call(kernel, outs, *args, flops=0, late=(), grant=GRANT, stream=False):
-    shapes = tuple(jax.ShapeDtypeStruct(s, d) for s, d in outs)
+    shapes = tuple((pltpu.HBM if stream else jax.ShapeDtypeStruct)(s, d) for s, d in outs)
     count = len(args) + len(outs)
 
     def body(*refs):

time: 141 us -> 140 us (level)
    unnamed x30 -> x28, local copies, waits for them, and re-layouts: 13.4 us -> 12 us
where the time goes in v5:
time: 140 us; the launch traced here: 139 us
  starting transfers between devices  38.9 us (28%)
  waiting for transfers between devices  31.6 us (23%)
  Pallas kernels  21.8 us (16%)
  blocking collectives  20.6 us (15%)
  between operations  14.2 us (10%)
  local copies, waits for them, and re-layouts  12 us (9%)
    all_to_all x4, starting transfers between devices, exchange(): return lax.all_to_all(x, axes, split_axis=0, concat_axis=0, tiled=True)  28.2 us
    all_to_all x4, waiting for transfers between devices, exchange(): return lax.all_to_all(x, axes, split_axis=0, concat_axis=0, tiled=True)  23.2 us
    pallas_call x11, Pallas kernels, call(): pl.pallas_call(body, out_shape=shapes, in_specs=[pl.BlockSpec(memory_spac...  21.8 us
    all_to_all x1, blocking collectives, exchange(): return lax.all_to_all(x, axes, split_axis=0, concat_axis=0, tiled=True)  20.6 us
    unnamed x28, local copies, waits for them, and re-layouts  12 us
    ppermute x1, waiting for transfers between devices, local(): received = lax.ppermute(passed, 'h', core_pair)  4.26 us
    ppermute x1, starting transfers between devices, local(): received = lax.ppermute(passed, 'h', core_pair)  2.98 us
    ppermute x1, starting transfers between devices, local(): query = (query_t, lax.ppermute(query_t, 'h', core_pair))  2.98 us
  transfers between devices with their start and end apart: 13, of which 9 were waited for; matrix products, arithmetic and copies ran while one was open for 0% of the time, Pallas kernels for 14%

profile of v5, /device:TPU:1, one launch (start us, length us, event | category | flops | bytes accessed | tf_op | source)
XLA Modules:
  0.0 139.1 jit_solution(8114808305640915191)
XLA Ops:
  7.9 1.9 %pack_kernel.1 = bf16[32,32,128]{2,1,0:T(8,128)(2,1)} custom-call(bf16[128,512]{1,0:T(8,128)(2,1)} %refs_1_.4, bf16[128,512]{1,0:T(8,128)(2,1)} %refs_2_.5, f32[128,512]{1,0:T(8,128)} %refs_2_.4), custom_call_target="tpu_custom_call" | custom-call | bytes 4194304 | tf_op jit(solution)/shard_map/pack_kernel/pallas_call | solution.py:320
  9.9 12.9 %all-to-all-start = ((bf16[32,32,128]{2,1,0:T(8,128)(2,1)}), bf16[32,32,128]{2,1,0:T(8,128)(2,1)S(1)}, u32[]{:S(2)}, u32[]{:S(2)}) async-start(bf16[32,32,128]{2,1,0:T(8,128)(2,1)} %pack_kernel.1), calls=%async_computation | async-start | bytes 524288 | tf_op jit(solution)/shard_map/all_to_all | solution.py:336
  22.8 0.9 copy-done.4
  23.8 3.0 %collective-permute-start = (bf16[512,128]{1,0:T(8,128)(2,1)S(1)}, bf16[512,128]{1,0:T(8,128)(2,1)S(1)}, u32[]{:S(2)}, u32[]{:S(2)}) collective-permute-start(bf16[512,128]{1,0:T(8,128)(2,1)S(1)} %turn_kernel.1.refs_4_.refs_1_.refs_2_), channel_id=1, source_target_pairs={{0,16},{16,0},{1,17},{17,1},{2,18},{18,2},{3,19},{19,3},{4,20},{20... | collective-permute-start | bytes 393224 | tf_op jit(solution)/shard_map/ppermute | solution.py:348
  26.8 0.9 copy-done.3
  27.7 1.1 share_kernel.1
  28.8 2.4 %collective-permute-done.refs_5_.refs_2_.refs_3_ = bf16[512,128]{1,0:T(8,128)(2,1)S(1)} collective-permute-done((bf16[512,128]{1,0:T(8,128)(2,1)S(1)}, bf16[512,128]{1,0:T(8,128)(2,1)S(1)}, u32[]{:S(2)}, u32[]{:S(2)}) %collective-permute-start) | collective-permute-done | bytes 131104 | tf_op jit(solution)/shard_map/ppermute | solution.py:348
  31.2 5.6 %all-to-all-done.refs_0_ = bf16[32,32,128]{2,1,0:T(8,128)(2,1)S(1)} async-done(((bf16[32,32,128]{2,1,0:T(8,128)(2,1)}), bf16[32,32,128]{2,1,0:T(8,128)(2,1)S(1)}, u32[]{:S(2)}, u32[]{:S(2)}) %all-to-all-start) | async-done | bytes 262176 | tf_op jit(solution)/shard_map/all_to_all | solution.py:336
  36.8 5.5 %all-to-all-start.1 = ((bf16[16,128,256]{2,1,0:T(8,128)(2,1)}), bf16[16,128,256]{2,1,0:T(8,128)(2,1)S(1)}, u32[]{:S(2)}, u32[]{:S(2)}) async-start(bf16[16,128,256]{2,1,0:T(8,128)(2,1)} %share_kernel.1), calls=%async_computation.1 | async-start | bytes 2097152 | tf_op jit(solution)/shard_map/all_to_all | solution.py:336
  42.4 1.7 %copy-done.5 = bf16[2,512,1056]{2,1,0:T(8,128)(2,1)S(1)} copy-done((bf16[2,512,1056]{2,1,0:T(8,128)(2,1)S(1)}, bf16[2,512,1056]{2,1,0:T(8,128)(2,1)}, u32[]{:S(2)}) %copy-start.5) | copy-done | bytes 2162712
  44.0 1.6 %copy-done.7 = bf16[2,1056,512]{2,1,0:T(8,128)(2,1)S(1)} copy-done((bf16[2,1056,512]{2,1,0:T(8,128)(2,1)S(1)}, bf16[2,1056,512]{2,1,0:T(8,128)(2,1)}, u32[]{:S(2)}) %copy-start.7) | copy-done | bytes 2162712
  45.7 4.9 %conv_kernel.1 = (bf16[512,128]{1,0:T(8,128)(2,1)S(1)}, f32[1056,256]{1,0:T(8,128)S(1)}) custom-call(bf16[32,32,128]{2,1,0:T(8,128)(2,1)S(1)} %all-to-all-done.refs_0_, bf16[2,1056,512]{2,1,0:T(8,128)(2,1)S(1)} %copy-done.7, bf16[2,256,256]{2,1,0:T(8,128)(2,1)S(1)} %copy-done.10, bf16[2,256,256]{2,1,0:T(8,128)(2,1)S(1)} %copy-done.11, ...), custom_call_target="tpu_custom_call" | custom-call | flops 5000000000 | bytes 4194304 | tf_op jit(solution)/shard_map/conv_kernel/pallas_call | solution.py:320
  50.6 1.0 copy-done.12
  51.6 6.5 %all-to-all-done.1.refs_1_.refs_2_.refs_6_ = bf16[16,128,256]{2,1,0:T(8,128)(2,1)S(1)} async-done(((bf16[16,128,256]{2,1,0:T(8,128)(2,1)}), bf16[16,128,256]{2,1,0:T(8,128)(2,1)S(1)}, u32[]{:S(2)}, u32[]{:S(2)}) %all-to-all-start.1) | async-done | bytes 1048608 | tf_op jit(solution)/shard_map/all_to_all | solution.py:336
  58.1 2.8 %collective-permute-start.1 = (bf16[8,512,128]{2,1,0:T(8,128)(2,1)}, bf16[8,512,128]{2,1,0:T(8,128)(2,1)S(1)}, u32[]{:S(2)}, u32[]{:S(2)}) collective-permute-start(bf16[8,512,128]{2,1,0:T(8,128)(2,1)} %bitcast.2), channel_id=1, source_target_pairs={{0,8},{8,0},{1,9},{9,1},{2,10},{10,2},{3,11},{11,3},{4,12},{12,4},... | collective-permute-start | bytes 3145736 | tf_op jit(solution)/shard_map/ppermute | solution.py:360
  61.0 1.2 copy-done
  63.9 20.6 %all_to_all.25.refs_0_.refs_1_ = bf16[32,64,128]{2,1,0:T(8,128)(2,1)S(1)} all-to-all(bf16[32,64,128]{2,1,0:T(8,128)(2,1)S(1)} %get-tuple-element.37), channel_id=1, replica_groups=mesh['z'=8,'h'=2,'k'=2,'chan'=8] {'z','h','k'}, dimensions={0} | all-to-all | bytes 1048576 | tf_op jit(solution)/shard_map/all_to_all | solution.py:336
  84.5 1.3 collective-permute-start.3
  86.3 1.8 %project_kernel.1 = bf16[16,128,256]{2,1,0:T(8,128)(2,1)} custom-call(bf16[32,64,128]{2,1,0:T(8,128)(2,1)S(1)} %all_to_all.25.refs_0_.refs_1_, bf16[512,128]{1,0:T(8,128)(2,1)S(1)} %turn_kernel.1.refs_4_.refs_1_.refs_2_, bf16[512,128]{1,0:T(8,128)(2,1)S(1)} %collective-permute-done.refs_5_.refs_2_.refs_3_, bf16[8,512,128]{2,1,0:T(8,128)(2,1)S(1)} %bitcast.4, ...), custom_call_target="tpu_custom_call" | custom-call | bytes 4194304 | tf_op jit(solution)/shard_map/project_kernel/pallas_call | solution.py:320
  88.5 2.2 %weight_kernel.1 = f32[8,512,128]{2,1,0:T(8,128)} custom-call(bf16[32,64,128]{2,1,0:T(8,128)(2,1)S(1)} %all_to_all.25.refs_0_.refs_1_, bf16[32,64,128]{2,1,0:T(8,128)(2,1)S(1)} %collective-permute-done.3.refs_1_, bf16[512,128]{1,0:T(8,128)(2,1)S(1)} %turn_kernel.1.refs_4_.refs_1_.refs_2_, bf16[512,128]{1,0:T(8,128)(2,1)S(1)} %collective-permute-done.refs_5_.refs_2_.refs_3_, ...), custom_call_target="tpu_custom_call" | custom-call | bytes 4194304 | tf_op jit(solution)/shard_map/weight_kernel/pallas_call | solution.py:320
  90.7 4.7 %all-to-all-start.3 = ((bf16[16,128,256]{2,1,0:T(8,128)(2,1)}), bf16[16,128,256]{2,1,0:T(8,128)(2,1)S(1)}, u32[]{:S(2)}, u32[]{:S(2)}) async-start(bf16[16,128,256]{2,1,0:T(8,128)(2,1)} %project_kernel.1), calls=%async_computation.3 | async-start | bytes 2097152 | tf_op jit(solution)/shard_map/all_to_all | solution.py:336
  95.4 1.8 %copy-done.6 = bf16[2,512,1056]{2,1,0:T(8,128)(2,1)S(1)} copy-done((bf16[2,512,1056]{2,1,0:T(8,128)(2,1)S(1)}, bf16[2,512,1056]{2,1,0:T(8,128)(2,1)}, u32[]{:S(2)}) %copy-start.6) | copy-done | bytes 2162712
  97.3 1.6 %copy-done.8 = bf16[2,1056,512]{2,1,0:T(8,128)(2,1)S(1)} copy-done((bf16[2,1056,512]{2,1,0:T(8,128)(2,1)S(1)}, bf16[2,1056,512]{2,1,0:T(8,128)(2,1)}, u32[]{:S(2)}) %copy-start.8) | copy-done | bytes 2162712
  98.9 1.2 copy-done.13
  100.1 6.8 %back_kernel.1 = bf16[32,32,128]{2,1,0:T(8,128)(2,1)} custom-call(bf16[32,64,128]{2,1,0:T(8,128)(2,1)S(1)} %all_to_all.25.refs_0_.refs_1_, f32[1056,256]{1,0:T(8,128)S(1)} %copy-done.13, bf16[2,1056,512]{2,1,0:T(8,128)(2,1)S(1)} %copy-done.8, bf16[2,256,256]{2,1,0:T(8,128)(2,1)S(1)} %copy-done.10, bf16[2,256,256]{2,1,0:T(8,128)(2,1)S(1)} %copy-done.11, ...), custom_call_target="tpu_custom_call" | custom-call | flops 8000000000 | bytes 4194304 | tf_op jit(solution)/shard_map/back_kernel/pallas_call | solution.py:320
  107.0 5.8 %all-to-all-done.3.refs_0_ = bf16[16,128,256]{2,1,0:T(8,128)(2,1)S(1)} async-done(((bf16[16,128,256]{2,1,0:T(8,128)(2,1)}), bf16[16,128,256]{2,1,0:T(8,128)(2,1)S(1)}, u32[]{:S(2)}, u32[]{:S(2)}) %all-to-all-start.3) | async-done | bytes 1048608 | tf_op jit(solution)/shard_map/all_to_all | solution.py:336
  112.8 5.1 %all-to-all-start.4 = ((bf16[32,32,128]{2,1,0:T(8,128)(2,1)}), bf16[32,32,128]{2,1,0:T(8,128)(2,1)S(1)}, u32[]{:S(2)}, u32[]{:S(2)}) async-start(bf16[32,32,128]{2,1,0:T(8,128)(2,1)} %back_kernel.1), calls=%async_computation.4 | async-start | bytes 524288 | tf_op jit(solution)/shard_map/all_to_all | solution.py:336
  117.9 3.0 %collective-permute-start.2 = (bf16[512,128]{1,0:T(8,128)(2,1)S(1)}, bf16[512,128]{1,0:T(8,128)(2,1)S(1)}, u32[]{:S(2)}, u32[]{:S(2)}) collective-permute-start(bf16[512,128]{1,0:T(8,128)(2,1)S(1)} %get-tuple-element.41), channel_id=1, source_target_pairs={{0,16},{16,0},{1,17},{17,1},{2,18},{18,2},{3,19},{19,3},{4,20},{20... | collective-permute-start | bytes 393224 | tf_op jit(solution)/shard_map/ppermute | solution.py:372
  120.9 4.3 %collective-permute-done.2.refs_3_ = bf16[512,128]{1,0:T(8,128)(2,1)S(1)} collective-permute-done((bf16[512,128]{1,0:T(8,128)(2,1)S(1)}, bf16[512,128]{1,0:T(8,128)(2,1)S(1)}, u32[]{:S(2)}, u32[]{:S(2)}) %collective-permute-start.2) | collective-permute-done | bytes 131104 | tf_op jit(solution)/shard_map/ppermute | solution.py:372
  125.2 0.9 sum_kernel.1
  126.1 5.2 %all-to-all-done.4.refs_0_ = bf16[32,32,128]{2,1,0:T(8,128)(2,1)S(1)} async-done(((bf16[32,32,128]{2,1,0:T(8,128)(2,1)}), bf16[32,32,128]{2,1,0:T(8,128)(2,1)S(1)}, u32[]{:S(2)}, u32[]{:S(2)}) %all-to-all-start.4) | async-done | bytes 262176 | tf_op jit(solution)/shard_map/all_to_all | solution.py:336
  131.3 0.9 finish_kernel.1
  (36 shorter events, 3.6 us)
Async XLA Ops:
  7.2 51.0 %all-gather.3.cloned.1.call-start = ((), (), s32[]{:S(2)}) async-start(), calls=%async_computation.7 | async-start | bytes 1179648 | tf_op jit(solution)/shard_map/all_gather | solution.py:349
  9.9 32.5 %copy-start.10 = (bf16[2,256,256]{2,1,0:T(8,128)(2,1)S(1)}, bf16[2,256,256]{2,1,0:T(8,128)(2,1)}, u32[]{:S(2)}) copy-start(bf16[2,256,256]{2,1,0:T(8,128)(2,1)} %constant.11.clone.refs_2_.refs_3_) | copy-start | bytes 786436
  9.9 32.5 %copy-start.11 = (bf16[2,256,256]{2,1,0:T(8,128)(2,1)S(1)}, bf16[2,256,256]{2,1,0:T(8,128)(2,1)}, u32[]{:S(2)}) copy-start(bf16[2,256,256]{2,1,0:T(8,128)(2,1)} %constant.12.clone.refs_3_.refs_4_) | copy-start | bytes 786436
  9.9 26.9 %all-to-all-start = ((bf16[32,32,128]{2,1,0:T(8,128)(2,1)}), bf16[32,32,128]{2,1,0:T(8,128)(2,1)S(1)}, u32[]{:S(2)}, u32[]{:S(2)}) async-start(bf16[32,32,128]{2,1,0:T(8,128)(2,1)} %pack_kernel.1), calls=%async_computation | async-start | bytes 524288 | tf_op jit(solution)/shard_map/all_to_all | solution.py:336
  22.8 0.9 copy-start.4
  23.8 7.4 %collective-permute-start = (bf16[512,128]{1,0:T(8,128)(2,1)S(1)}, bf16[512,128]{1,0:T(8,128)(2,1)S(1)}, u32[]{:S(2)}, u32[]{:S(2)}) collective-permute-start(bf16[512,128]{1,0:T(8,128)(2,1)S(1)} %turn_kernel.1.refs_4_.refs_1_.refs_2_), channel_id=1, source_target_pairs={{0,16},{16,0},{1,17},{17,1},{2,18},{18,2},{3,19},{19,3},{4,20},{20... | collective-permute-start | bytes 393224 | tf_op jit(solution)/shard_map/ppermute | solution.py:348
  26.8 0.9 copy-start.3
  27.7 14.7 %copy-start.9 = (f32[2,528,128]{2,1,0:T(8,128)S(1)}, f32[2,528,128]{2,1,0:T(8,128)}, u32[]{:S(2)}) copy-start(f32[2,528,128]{2,1,0:T(8,128)} %constant.13.clone.refs_4_.refs_5_) | copy-start | bytes 1622020
  36.8 21.3 %all-to-all-start.1 = ((bf16[16,128,256]{2,1,0:T(8,128)(2,1)}), bf16[16,128,256]{2,1,0:T(8,128)(2,1)S(1)}, u32[]{:S(2)}, u32[]{:S(2)}) async-start(bf16[16,128,256]{2,1,0:T(8,128)(2,1)} %share_kernel.1), calls=%async_computation.1 | async-start | bytes 2097152 | tf_op jit(solution)/shard_map/all_to_all | solution.py:336
  42.3 89.9 %reduce-scatter.2.cloned.1.call-start = ((), (), s32[]{:S(2)}) async-start(), calls=%async_computation.6 | async-start | bytes 2359296 | tf_op jit(solution)/shard_map/reduce_scatter | solution.py:382
  42.4 1.7 %copy-start.5 = (bf16[2,512,1056]{2,1,0:T(8,128)(2,1)S(1)}, bf16[2,512,1056]{2,1,0:T(8,128)(2,1)}, u32[]{:S(2)}) copy-start(bf16[2,512,1056]{2,1,0:T(8,128)(2,1)} %constant.14.clone.refs_5_.refs_6_) | copy-start | bytes 6488068
  44.0 1.6 %copy-start.7 = (bf16[2,1056,512]{2,1,0:T(8,128)(2,1)S(1)}, bf16[2,1056,512]{2,1,0:T(8,128)(2,1)}, u32[]{:S(2)}) copy-start(bf16[2,1056,512]{2,1,0:T(8,128)(2,1)} %constant.10.clone.refs_1_.refs_2_) | copy-start | bytes 6488068
  50.6 1.0 copy-start.12
  58.1 5.3 %collective-permute-start.1 = (bf16[8,512,128]{2,1,0:T(8,128)(2,1)}, bf16[8,512,128]{2,1,0:T(8,128)(2,1)S(1)}, u32[]{:S(2)}, u32[]{:S(2)}) collective-permute-start(bf16[8,512,128]{2,1,0:T(8,128)(2,1)} %bitcast.2), channel_id=1, source_target_pairs={{0,8},{8,0},{1,9},{9,1},{2,10},{10,2},{3,11},{11,3},{4,12},{12,4},... | collective-permute-start | bytes 3145736 | tf_op jit(solution)/shard_map/ppermute | solution.py:360
  61.0 1.2 copy-start
  84.5 3.6 %collective-permute-start.3 = (bf16[32,64,128]{2,1,0:T(8,128)(2,1)S(1)}, bf16[32,64,128]{2,1,0:T(8,128)(2,1)S(1)}, u32[]{:S(2)}, u32[]{:S(2)}) collective-permute-start(bf16[32,64,128]{2,1,0:T(8,128)(2,1)S(1)} %all_to_all.25.refs_0_.refs_1_), channel_id=1, source_target_pairs={{0,8},{8,0},{1,9},{9,1},{2,10},{10,2},{3,11},{11,3},{4,12},{12,4},... | collective-permute-start | bytes 1572872 | tf_op jit(solution)/shard_map/ppermute | solution.py:374
  85.8 2.7 %collective-permute-start.6 = (bf16[16,128,128]{2,1,0:T(8,128)(2,1)S(1)}, bf16[16,128,128]{2,1,0:T(8,128)(2,1)S(1)}, u32[]{:S(2)}, u32[]{:S(2)}) collective-permute-start(bf16[16,128,128]{2,1,0:T(8,128)(2,1)S(1)} %get-tuple-element.49), channel_id=1, source_target_pairs={{0,8},{8,0},{1,9},{9,1},{2,10},{10,2},{3,11},{11,3},{4,12},{12,4},... | collective-permute-start | bytes 1572872 | tf_op jit(solution)/shard_map/ppermute | solution.py:371
  85.8 2.5 %collective-permute-start.4 = (bf16[512,128]{1,0:T(8,128)(2,1)S(1)}, bf16[512,128]{1,0:T(8,128)(2,1)S(1)}, u32[]{:S(2)}, u32[]{:S(2)}) collective-permute-start(bf16[512,128]{1,0:T(8,128)(2,1)S(1)} %turn_kernel.1.refs_4_.refs_1_.refs_2_), channel_id=1, source_target_pairs={{0,8},{8,0},{1,9},{9,1},{2,10},{10,2},{3,11},{11,3},{4,12},{12,4},... | collective-permute-start | bytes 393224 | tf_op jit(solution)/shard_map/ppermute | solution.py:352
  86.3 2.2 %collective-permute-start.5 = (bf16[512,128]{1,0:T(8,128)(2,1)S(1)}, bf16[512,128]{1,0:T(8,128)(2,1)S(1)}, u32[]{:S(2)}, u32[]{:S(2)}) collective-permute-start(bf16[512,128]{1,0:T(8,128)(2,1)S(1)} %collective-permute-done.refs_5_.refs_2_.refs_3_), channel_id=1, source_target_pairs={{0,8},{8,0},{1,9},{9,1},{2,10},{10,2},{3,11},{11,3},{4,12},{12,4},... | collective-permute-start | bytes 393224 | tf_op jit(solution)/shard_map/ppermute | solution.py:352
  90.7 22.1 %all-to-all-start.3 = ((bf16[16,128,256]{2,1,0:T(8,128)(2,1)}), bf16[16,128,256]{2,1,0:T(8,128)(2,1)S(1)}, u32[]{:S(2)}, u32[]{:S(2)}) async-start(bf16[16,128,256]{2,1,0:T(8,128)(2,1)} %project_kernel.1), calls=%async_computation.3 | async-start | bytes 2097152 | tf_op jit(solution)/shard_map/all_to_all | solution.py:336
  95.4 1.8 %copy-start.6 = (bf16[2,512,1056]{2,1,0:T(8,128)(2,1)S(1)}, bf16[2,512,1056]{2,1,0:T(8,128)(2,1)}, u32[]{:S(2)}) copy-start(bf16[2,512,1056]{2,1,0:T(8,128)(2,1)} %constant.14.clone.refs_5_.refs_6_) | copy-start | bytes 6488068
  97.3 1.6 %copy-start.8 = (bf16[2,1056,512]{2,1,0:T(8,128)(2,1)S(1)}, bf16[2,1056,512]{2,1,0:T(8,128)(2,1)}, u32[]{:S(2)}) copy-start(bf16[2,1056,512]{2,1,0:T(8,128)(2,1)} %constant.10.clone.refs_1_.refs_2_) | copy-start | bytes 6488068
  98.9 1.2 copy-start.13
  107.0 24.3 %copy-start.1 = (bf16[128,512]{1,0:T(8,128)(2,1)S(1)}, bf16[128,512]{1,0:T(8,128)(2,1)}, u32[]{:S(2)}) copy-start(bf16[128,512]{1,0:T(8,128)(2,1)} %refs_1_.4) | copy-start | bytes 393220
  107.0 24.3 %copy-start.2 = (bf16[128,512]{1,0:T(8,128)(2,1)S(1)}, bf16[128,512]{1,0:T(8,128)(2,1)}, u32[]{:S(2)}) copy-start(bf16[128,512]{1,0:T(8,128)(2,1)} %refs_2_.5) | copy-start | bytes 393220
  112.8 18.5 %all-to-all-start.4 = ((bf16[32,32,128]{2,1,0:T(8,128)(2,1)}), bf16[32,32,128]{2,1,0:T(8,128)(2,1)S(1)}, u32[]{:S(2)}, u32[]{:S(2)}) async-start(bf16[32,32,128]{2,1,0:T(8,128)(2,1)} %back_kernel.1), calls=%async_computation.4 | async-start | bytes 524288 | tf_op jit(solution)/shard_map/all_to_all | solution.py:336
  117.9 7.2 %collective-permute-start.2 = (bf16[512,128]{1,0:T(8,128)(2,1)S(1)}, bf16[512,128]{1,0:T(8,128)(2,1)S(1)}, u32[]{:S(2)}, u32[]{:S(2)}) collective-permute-start(bf16[512,128]{1,0:T(8,128)(2,1)S(1)} %get-tuple-element.41), channel_id=1, source_target_pairs={{0,16},{16,0},{1,17},{17,1},{2,18},{18,2},{3,19},{19,3},{4,20},{20... | collective-permute-start | bytes 393224 | tf_op jit(solution)/shard_map/ppermute | solution.py:372
Sparse Core Ops, SparseCore 0:
  9.8 40.9 all-gather.2
  90.8 32.0 reduce-scatter.1

commit v6 on v5

--- a/solution.py
+++ b/solution.py
@@ -341,7 +341,7 @@
     core_pair = [(0, 1), (1, 0)]
     (packed,) = call(
         pack_kernel, [((HALF, 2 * CH, LANE), BF)], keys, values, filter_weight,
-        late=(0, 1, 2), grant=FULL,
+        late=(0, 1, 2), grant=FULL, stream=True,
     )
     (query_t,) = call(turn_kernel, [((WIDE, LANE), BF)], queries)
     (shared,) = call(share_kernel, [((H * C, LANE, K * LANE), BF)], cotangent)
@@ -372,7 +372,7 @@
     received = lax.ppermute(passed, "h", core_pair)
     moved = exchange(sent, SEQ)
     moved_other = lax.ppermute(moved, "k", core_pair)
-    (out_part,) = call(project_kernel, [((H * C, LANE, K * LANE), BF)], moved, *query, own, other)
+    (out_part,) = call(project_kernel, [((H * C, LANE, K * LANE), BF)], moved, *query, own, other, stream=True)
     moved_other, _ = lax.optimization_barrier((moved_other, out_part))
     (weight_part,) = call(
         weight_kernel,

time: 140 us -> 140 us (level)
  no operation moved by 1% of the time
where the time goes in v6:
time: 140 us; the launch traced here: 139 us
  starting transfers between devices  38.8 us (28%)
  waiting for transfers between devices  31.8 us (23%)
  Pallas kernels  21.8 us (16%)
  blocking collectives  20.4 us (15%)
  between operations  14.2 us (10%)
  local copies, waits for them, and re-layouts  12 us (9%)
    all_to_all x4, starting transfers between devices, exchange(): return lax.all_to_all(x, axes, split_axis=0, concat_axis=0, tiled=True)  28.2 us
    all_to_all x4, waiting for transfers between devices, exchange(): return lax.all_to_all(x, axes, split_axis=0, concat_axis=0, tiled=True)  23.6 us
    pallas_call x11, Pallas kernels, call(): pl.pallas_call(body, out_shape=shapes, in_specs=[pl.BlockSpec(memory_spac...  21.8 us
    all_to_all x1, blocking collectives, exchange(): return lax.all_to_all(x, axes, split_axis=0, concat_axis=0, tiled=True)  20.4 us
    unnamed x28, local copies, waits for them, and re-layouts  12 us
    ppermute x1, waiting for transfers between devices, local(): received = lax.ppermute(passed, 'h', core_pair)  3.98 us
    ppermute x1, starting transfers between devices, local(): received = lax.ppermute(passed, 'h', core_pair)  2.98 us
    ppermute x1, starting transfers between devices, local(): query = (query_t, lax.ppermute(query_t, 'h', core_pair))  2.98 us
  transfers between devices with their start and end apart: 13, of which 9 were waited for; matrix products, arithmetic and copies ran while one was open for 0% of the time, Pallas kernels for 14%

profile of v6, /device:TPU:1, one launch (start us, length us, event | category | flops | bytes accessed | tf_op | source)
XLA Modules:
  0.0 139.2 jit_solution(17157506834433942015)
XLA Ops:
  7.9 2.2 %pack_kernel.1 = bf16[32,32,128]{2,1,0:T(8,128)(2,1)} custom-call(bf16[128,512]{1,0:T(8,128)(2,1)} %refs_1_.4, bf16[128,512]{1,0:T(8,128)(2,1)} %refs_2_.5, f32[128,512]{1,0:T(8,128)} %refs_2_.4), custom_call_target="tpu_custom_call" | custom-call | bytes 4194304 | tf_op jit(solution)/shard_map/pack_kernel/pallas_call | solution.py:320
  10.1 12.9 %all-to-all-start = ((bf16[32,32,128]{2,1,0:T(8,128)(2,1)}), bf16[32,32,128]{2,1,0:T(8,128)(2,1)S(1)}, u32[]{:S(2)}, u32[]{:S(2)}) async-start(bf16[32,32,128]{2,1,0:T(8,128)(2,1)} %pack_kernel.1), calls=%async_computation | async-start | bytes 524288 | tf_op jit(solution)/shard_map/all_to_all | solution.py:336
  23.0 0.9 copy-done.4
  24.1 3.0 %collective-permute-start = (bf16[512,128]{1,0:T(8,128)(2,1)S(1)}, bf16[512,128]{1,0:T(8,128)(2,1)S(1)}, u32[]{:S(2)}, u32[]{:S(2)}) collective-permute-start(bf16[512,128]{1,0:T(8,128)(2,1)S(1)} %turn_kernel.1.refs_4_.refs_1_.refs_2_), channel_id=1, source_target_pairs={{0,16},{16,0},{1,17},{17,1},{2,18},{18,2},{3,19},{19,3},{4,20},{20... | collective-permute-start | bytes 393224 | tf_op jit(solution)/shard_map/ppermute | solution.py:348
  27.0 0.9 copy-done.3
  27.9 1.1 share_kernel.1
  29.0 2.3 %collective-permute-done.refs_5_.refs_2_.refs_3_ = bf16[512,128]{1,0:T(8,128)(2,1)S(1)} collective-permute-done((bf16[512,128]{1,0:T(8,128)(2,1)S(1)}, bf16[512,128]{1,0:T(8,128)(2,1)S(1)}, u32[]{:S(2)}, u32[]{:S(2)}) %collective-permute-start) | collective-permute-done | bytes 131104 | tf_op jit(solution)/shard_map/ppermute | solution.py:348
  31.4 5.9 %all-to-all-done.refs_0_ = bf16[32,32,128]{2,1,0:T(8,128)(2,1)S(1)} async-done(((bf16[32,32,128]{2,1,0:T(8,128)(2,1)}), bf16[32,32,128]{2,1,0:T(8,128)(2,1)S(1)}, u32[]{:S(2)}, u32[]{:S(2)}) %all-to-all-start) | async-done | bytes 262176 | tf_op jit(solution)/shard_map/all_to_all | solution.py:336
  37.3 5.5 %all-to-all-start.1 = ((bf16[16,128,256]{2,1,0:T(8,128)(2,1)}), bf16[16,128,256]{2,1,0:T(8,128)(2,1)S(1)}, u32[]{:S(2)}, u32[]{:S(2)}) async-start(bf16[16,128,256]{2,1,0:T(8,128)(2,1)} %share_kernel.1), calls=%async_computation.1 | async-start | bytes 2097152 | tf_op jit(solution)/shard_map/all_to_all | solution.py:336
  42.9 1.7 %copy-done.5 = bf16[2,512,1056]{2,1,0:T(8,128)(2,1)S(1)} copy-done((bf16[2,512,1056]{2,1,0:T(8,128)(2,1)S(1)}, bf16[2,512,1056]{2,1,0:T(8,128)(2,1)}, u32[]{:S(2)}) %copy-start.5) | copy-done | bytes 2162712
  44.5 1.6 %copy-done.7 = bf16[2,1056,512]{2,1,0:T(8,128)(2,1)S(1)} copy-done((bf16[2,1056,512]{2,1,0:T(8,128)(2,1)S(1)}, bf16[2,1056,512]{2,1,0:T(8,128)(2,1)}, u32[]{:S(2)}) %copy-start.7) | copy-done | bytes 2162712
  46.2 4.9 %conv_kernel.1 = (bf16[512,128]{1,0:T(8,128)(2,1)S(1)}, f32[1056,256]{1,0:T(8,128)S(1)}) custom-call(bf16[32,32,128]{2,1,0:T(8,128)(2,1)S(1)} %all-to-all-done.refs_0_, bf16[2,1056,512]{2,1,0:T(8,128)(2,1)S(1)} %copy-done.7, bf16[2,256,256]{2,1,0:T(8,128)(2,1)S(1)} %copy-done.10, bf16[2,256,256]{2,1,0:T(8,128)(2,1)S(1)} %copy-done.11, ...), custom_call_target="tpu_custom_call" | custom-call | flops 5000000000 | bytes 4194304 | tf_op jit(solution)/shard_map/conv_kernel/pallas_call | solution.py:320
  51.1 1.0 copy-done.12
  52.1 6.5 %all-to-all-done.1.refs_1_.refs_2_.refs_6_ = bf16[16,128,256]{2,1,0:T(8,128)(2,1)S(1)} async-done(((bf16[16,128,256]{2,1,0:T(8,128)(2,1)}), bf16[16,128,256]{2,1,0:T(8,128)(2,1)S(1)}, u32[]{:S(2)}, u32[]{:S(2)}) %all-to-all-start.1) | async-done | bytes 1048608 | tf_op jit(solution)/shard_map/all_to_all | solution.py:336
  58.6 2.8 %collective-permute-start.1 = (bf16[8,512,128]{2,1,0:T(8,128)(2,1)}, bf16[8,512,128]{2,1,0:T(8,128)(2,1)S(1)}, u32[]{:S(2)}, u32[]{:S(2)}) collective-permute-start(bf16[8,512,128]{2,1,0:T(8,128)(2,1)} %bitcast.2), channel_id=1, source_target_pairs={{0,8},{8,0},{1,9},{9,1},{2,10},{10,2},{3,11},{11,3},{4,12},{12,4},... | collective-permute-start | bytes 3145736 | tf_op jit(solution)/shard_map/ppermute | solution.py:360
  61.4 1.2 copy-done
  64.4 20.4 %all_to_all.25.refs_0_.refs_1_ = bf16[32,64,128]{2,1,0:T(8,128)(2,1)S(1)} all-to-all(bf16[32,64,128]{2,1,0:T(8,128)(2,1)S(1)} %get-tuple-element.37), channel_id=1, replica_groups=mesh['z'=8,'h'=2,'k'=2,'chan'=8] {'z','h','k'}, dimensions={0} | all-to-all | bytes 1048576 | tf_op jit(solution)/shard_map/all_to_all | solution.py:336
  84.8 1.3 collective-permute-start.3
  86.6 1.6 %project_kernel.1 = bf16[16,128,256]{2,1,0:T(8,128)(2,1)} custom-call(bf16[32,64,128]{2,1,0:T(8,128)(2,1)S(1)} %all_to_all.25.refs_0_.refs_1_, bf16[512,128]{1,0:T(8,128)(2,1)S(1)} %turn_kernel.1.refs_4_.refs_1_.refs_2_, bf16[512,128]{1,0:T(8,128)(2,1)S(1)} %collective-permute-done.refs_5_.refs_2_.refs_3_, bf16[8,512,128]{2,1,0:T(8,128)(2,1)S(1)} %bitcast.4, ...), custom_call_target="tpu_custom_call" | custom-call | bytes 4194304 | tf_op jit(solution)/shard_map/project_kernel/pallas_call | solution.py:320
  88.7 2.2 %weight_kernel.1 = f32[8,512,128]{2,1,0:T(8,128)} custom-call(bf16[32,64,128]{2,1,0:T(8,128)(2,1)S(1)} %all_to_all.25.refs_0_.refs_1_, bf16[32,64,128]{2,1,0:T(8,128)(2,1)S(1)} %collective-permute-done.3.refs_1_, bf16[512,128]{1,0:T(8,128)(2,1)S(1)} %turn_kernel.1.refs_4_.refs_1_.refs_2_, bf16[512,128]{1,0:T(8,128)(2,1)S(1)} %collective-permute-done.refs_5_.refs_2_.refs_3_, ...), custom_call_target="tpu_custom_call" | custom-call | bytes 4194304 | tf_op jit(solution)/shard_map/weight_kernel/pallas_call | solution.py:320
  91.0 4.7 %all-to-all-start.3 = ((bf16[16,128,256]{2,1,0:T(8,128)(2,1)}), bf16[16,128,256]{2,1,0:T(8,128)(2,1)S(1)}, u32[]{:S(2)}, u32[]{:S(2)}) async-start(bf16[16,128,256]{2,1,0:T(8,128)(2,1)} %project_kernel.1), calls=%async_computation.3 | async-start | bytes 2097152 | tf_op jit(solution)/shard_map/all_to_all | solution.py:336
  95.7 1.8 %copy-done.6 = bf16[2,512,1056]{2,1,0:T(8,128)(2,1)S(1)} copy-done((bf16[2,512,1056]{2,1,0:T(8,128)(2,1)S(1)}, bf16[2,512,1056]{2,1,0:T(8,128)(2,1)}, u32[]{:S(2)}) %copy-start.6) | copy-done | bytes 2162712
  97.6 1.6 %copy-done.8 = bf16[2,1056,512]{2,1,0:T(8,128)(2,1)S(1)} copy-done((bf16[2,1056,512]{2,1,0:T(8,128)(2,1)S(1)}, bf16[2,1056,512]{2,1,0:T(8,128)(2,1)}, u32[]{:S(2)}) %copy-start.8) | copy-done | bytes 2162712
  99.2 1.2 copy-done.13
  100.4 6.8 %back_kernel.1 = bf16[32,32,128]{2,1,0:T(8,128)(2,1)} custom-call(bf16[32,64,128]{2,1,0:T(8,128)(2,1)S(1)} %all_to_all.25.refs_0_.refs_1_, f32[1056,256]{1,0:T(8,128)S(1)} %copy-done.13, bf16[2,1056,512]{2,1,0:T(8,128)(2,1)S(1)} %copy-done.8, bf16[2,256,256]{2,1,0:T(8,128)(2,1)S(1)} %copy-done.10, bf16[2,256,256]{2,1,0:T(8,128)(2,1)S(1)} %copy-done.11, ...), custom_call_target="tpu_custom_call" | custom-call | flops 8000000000 | bytes 4194304 | tf_op jit(solution)/shard_map/back_kernel/pallas_call | solution.py:320
  107.3 5.9 %all-to-all-done.3.refs_0_ = bf16[16,128,256]{2,1,0:T(8,128)(2,1)S(1)} async-done(((bf16[16,128,256]{2,1,0:T(8,128)(2,1)}), bf16[16,128,256]{2,1,0:T(8,128)(2,1)S(1)}, u32[]{:S(2)}, u32[]{:S(2)}) %all-to-all-start.3) | async-done | bytes 1048608 | tf_op jit(solution)/shard_map/all_to_all | solution.py:336
  113.2 5.1 %all-to-all-start.4 = ((bf16[32,32,128]{2,1,0:T(8,128)(2,1)}), bf16[32,32,128]{2,1,0:T(8,128)(2,1)S(1)}, u32[]{:S(2)}, u32[]{:S(2)}) async-start(bf16[32,32,128]{2,1,0:T(8,128)(2,1)} %back_kernel.1), calls=%async_computation.4 | async-start | bytes 524288 | tf_op jit(solution)/shard_map/all_to_all | solution.py:336
  118.3 3.0 %collective-permute-start.2 = (bf16[512,128]{1,0:T(8,128)(2,1)S(1)}, bf16[512,128]{1,0:T(8,128)(2,1)S(1)}, u32[]{:S(2)}, u32[]{:S(2)}) collective-permute-start(bf16[512,128]{1,0:T(8,128)(2,1)S(1)} %get-tuple-element.41), channel_id=1, source_target_pairs={{0,16},{16,0},{1,17},{17,1},{2,18},{18,2},{3,19},{19,3},{4,20},{20... | collective-permute-start | bytes 393224 | tf_op jit(solution)/shard_map/ppermute | solution.py:372
  121.2 4.0 %collective-permute-done.2.refs_3_ = bf16[512,128]{1,0:T(8,128)(2,1)S(1)} collective-permute-done((bf16[512,128]{1,0:T(8,128)(2,1)S(1)}, bf16[512,128]{1,0:T(8,128)(2,1)S(1)}, u32[]{:S(2)}, u32[]{:S(2)}) %collective-permute-start.2) | collective-permute-done | bytes 131104 | tf_op jit(solution)/shard_map/ppermute | solution.py:372
  125.2 0.9 sum_kernel.1
  126.1 5.3 %all-to-all-done.4.refs_0_ = bf16[32,32,128]{2,1,0:T(8,128)(2,1)S(1)} async-done(((bf16[32,32,128]{2,1,0:T(8,128)(2,1)}), bf16[32,32,128]{2,1,0:T(8,128)(2,1)S(1)}, u32[]{:S(2)}, u32[]{:S(2)}) %all-to-all-start.4) | async-done | bytes 262176 | tf_op jit(solution)/shard_map/all_to_all | solution.py:336
  131.4 0.9 finish_kernel.1
  (36 shorter events, 3.7 us)
Async XLA Ops:
  7.2 51.4 %all-gather.3.cloned.1.call-start = ((), (), s32[]{:S(2)}) async-start(), calls=%async_computation.7 | async-start | bytes 1179648 | tf_op jit(solution)/shard_map/all_gather | solution.py:349
  10.1 32.7 %copy-start.10 = (bf16[2,256,256]{2,1,0:T(8,128)(2,1)S(1)}, bf16[2,256,256]{2,1,0:T(8,128)(2,1)}, u32[]{:S(2)}) copy-start(bf16[2,256,256]{2,1,0:T(8,128)(2,1)} %constant.11.clone.refs_2_.refs_3_) | copy-start | bytes 786436
  10.1 32.7 %copy-start.11 = (bf16[2,256,256]{2,1,0:T(8,128)(2,1)S(1)}, bf16[2,256,256]{2,1,0:T(8,128)(2,1)}, u32[]{:S(2)}) copy-start(bf16[2,256,256]{2,1,0:T(8,128)(2,1)} %constant.12.clone.refs_3_.refs_4_) | copy-start | bytes 786436
  10.1 27.1 %all-to-all-start = ((bf16[32,32,128]{2,1,0:T(8,128)(2,1)}), bf16[32,32,128]{2,1,0:T(8,128)(2,1)S(1)}, u32[]{:S(2)}, u32[]{:S(2)}) async-start(bf16[32,32,128]{2,1,0:T(8,128)(2,1)} %pack_kernel.1), calls=%async_computation | async-start | bytes 524288 | tf_op jit(solution)/shard_map/all_to_all | solution.py:336
  23.0 0.9 copy-start.4
  24.1 7.3 %collective-permute-start = (bf16[512,128]{1,0:T(8,128)(2,1)S(1)}, bf16[512,128]{1,0:T(8,128)(2,1)S(1)}, u32[]{:S(2)}, u32[]{:S(2)}) collective-permute-start(bf16[512,128]{1,0:T(8,128)(2,1)S(1)} %turn_kernel.1.refs_4_.refs_1_.refs_2_), channel_id=1, source_target_pairs={{0,16},{16,0},{1,17},{17,1},{2,18},{18,2},{3,19},{19,3},{4,20},{20... | collective-permute-start | bytes 393224 | tf_op jit(solution)/shard_map/ppermute | solution.py:348
  27.0 0.9 copy-start.3
  27.9 14.9 %copy-start.9 = (f32[2,528,128]{2,1,0:T(8,128)S(1)}, f32[2,528,128]{2,1,0:T(8,128)}, u32[]{:S(2)}) copy-start(f32[2,528,128]{2,1,0:T(8,128)} %constant.13.clone.refs_4_.refs_5_) | copy-start | bytes 1622020
  37.3 21.3 %all-to-all-start.1 = ((bf16[16,128,256]{2,1,0:T(8,128)(2,1)}), bf16[16,128,256]{2,1,0:T(8,128)(2,1)S(1)}, u32[]{:S(2)}, u32[]{:S(2)}) async-start(bf16[16,128,256]{2,1,0:T(8,128)(2,1)} %share_kernel.1), calls=%async_computation.1 | async-start | bytes 2097152 | tf_op jit(solution)/shard_map/all_to_all | solution.py:336
  42.8 89.6 %reduce-scatter.2.cloned.1.call-start = ((), (), s32[]{:S(2)}) async-start(), calls=%async_computation.6 | async-start | bytes 2359296 | tf_op jit(solution)/shard_map/reduce_scatter | solution.py:382
  42.8 1.7 %copy-start.5 = (bf16[2,512,1056]{2,1,0:T(8,128)(2,1)S(1)}, bf16[2,512,1056]{2,1,0:T(8,128)(2,1)}, u32[]{:S(2)}) copy-start(bf16[2,512,1056]{2,1,0:T(8,128)(2,1)} %constant.14.clone.refs_5_.refs_6_) | copy-start | bytes 6488068
  44.5 1.6 %copy-start.7 = (bf16[2,1056,512]{2,1,0:T(8,128)(2,1)S(1)}, bf16[2,1056,512]{2,1,0:T(8,128)(2,1)}, u32[]{:S(2)}) copy-start(bf16[2,1056,512]{2,1,0:T(8,128)(2,1)} %constant.10.clone.refs_1_.refs_2_) | copy-start | bytes 6488068
  51.1 1.0 copy-start.12
  58.6 5.3 %collective-permute-start.1 = (bf16[8,512,128]{2,1,0:T(8,128)(2,1)}, bf16[8,512,128]{2,1,0:T(8,128)(2,1)S(1)}, u32[]{:S(2)}, u32[]{:S(2)}) collective-permute-start(bf16[8,512,128]{2,1,0:T(8,128)(2,1)} %bitcast.2), channel_id=1, source_target_pairs={{0,8},{8,0},{1,9},{9,1},{2,10},{10,2},{3,11},{11,3},{4,12},{12,4},... | collective-permute-start | bytes 3145736 | tf_op jit(solution)/shard_map/ppermute | solution.py:360
  61.4 1.2 copy-start
  84.8 3.4 %collective-permute-start.3 = (bf16[32,64,128]{2,1,0:T(8,128)(2,1)S(1)}, bf16[32,64,128]{2,1,0:T(8,128)(2,1)S(1)}, u32[]{:S(2)}, u32[]{:S(2)}) collective-permute-start(bf16[32,64,128]{2,1,0:T(8,128)(2,1)S(1)} %all_to_all.25.refs_0_.refs_1_), channel_id=1, source_target_pairs={{0,8},{8,0},{1,9},{9,1},{2,10},{10,2},{3,11},{11,3},{4,12},{12,4},... | collective-permute-start | bytes 1572872 | tf_op jit(solution)/shard_map/ppermute | solution.py:374
  86.1 2.7 %collective-permute-start.6 = (bf16[16,128,128]{2,1,0:T(8,128)(2,1)S(1)}, bf16[16,128,128]{2,1,0:T(8,128)(2,1)S(1)}, u32[]{:S(2)}, u32[]{:S(2)}) collective-permute-start(bf16[16,128,128]{2,1,0:T(8,128)(2,1)S(1)} %get-tuple-element.49), channel_id=1, source_target_pairs={{0,8},{8,0},{1,9},{9,1},{2,10},{10,2},{3,11},{11,3},{4,12},{12,4},... | collective-permute-start | bytes 1572872 | tf_op jit(solution)/shard_map/ppermute | solution.py:371
  86.1 2.5 %collective-permute-start.4 = (bf16[512,128]{1,0:T(8,128)(2,1)S(1)}, bf16[512,128]{1,0:T(8,128)(2,1)S(1)}, u32[]{:S(2)}, u32[]{:S(2)}) collective-permute-start(bf16[512,128]{1,0:T(8,128)(2,1)S(1)} %turn_kernel.1.refs_4_.refs_1_.refs_2_), channel_id=1, source_target_pairs={{0,8},{8,0},{1,9},{9,1},{2,10},{10,2},{3,11},{11,3},{4,12},{12,4},... | collective-permute-start | bytes 393224 | tf_op jit(solution)/shard_map/ppermute | solution.py:352
  86.6 2.2 %collective-permute-start.5 = (bf16[512,128]{1,0:T(8,128)(2,1)S(1)}, bf16[512,128]{1,0:T(8,128)(2,1)S(1)}, u32[]{:S(2)}, u32[]{:S(2)}) collective-permute-start(bf16[512,128]{1,0:T(8,128)(2,1)S(1)} %collective-permute-done.refs_5_.refs_2_.refs_3_), channel_id=1, source_target_pairs={{0,8},{8,0},{1,9},{9,1},{2,10},{10,2},{3,11},{11,3},{4,12},{12,4},... | collective-permute-start | bytes 393224 | tf_op jit(solution)/shard_map/ppermute | solution.py:352
  91.0 22.2 %all-to-all-start.3 = ((bf16[16,128,256]{2,1,0:T(8,128)(2,1)}), bf16[16,128,256]{2,1,0:T(8,128)(2,1)S(1)}, u32[]{:S(2)}, u32[]{:S(2)}) async-start(bf16[16,128,256]{2,1,0:T(8,128)(2,1)} %project_kernel.1), calls=%async_computation.3 | async-start | bytes 2097152 | tf_op jit(solution)/shard_map/all_to_all | solution.py:336
  95.7 1.8 %copy-start.6 = (bf16[2,512,1056]{2,1,0:T(8,128)(2,1)S(1)}, bf16[2,512,1056]{2,1,0:T(8,128)(2,1)}, u32[]{:S(2)}) copy-start(bf16[2,512,1056]{2,1,0:T(8,128)(2,1)} %constant.14.clone.refs_5_.refs_6_) | copy-start | bytes 6488068
  97.6 1.6 %copy-start.8 = (bf16[2,1056,512]{2,1,0:T(8,128)(2,1)S(1)}, bf16[2,1056,512]{2,1,0:T(8,128)(2,1)}, u32[]{:S(2)}) copy-start(bf16[2,1056,512]{2,1,0:T(8,128)(2,1)} %constant.10.clone.refs_1_.refs_2_) | copy-start | bytes 6488068
  99.2 1.2 copy-start.13
  107.3 24.2 %copy-start.1 = (bf16[128,512]{1,0:T(8,128)(2,1)S(1)}, bf16[128,512]{1,0:T(8,128)(2,1)}, u32[]{:S(2)}) copy-start(bf16[128,512]{1,0:T(8,128)(2,1)} %refs_1_.4) | copy-start | bytes 393220
  107.3 24.2 %copy-start.2 = (bf16[128,512]{1,0:T(8,128)(2,1)S(1)}, bf16[128,512]{1,0:T(8,128)(2,1)}, u32[]{:S(2)}) copy-start(bf16[128,512]{1,0:T(8,128)(2,1)} %refs_2_.5) | copy-start | bytes 393220
  113.2 18.3 %all-to-all-start.4 = ((bf16[32,32,128]{2,1,0:T(8,128)(2,1)}), bf16[32,32,128]{2,1,0:T(8,128)(2,1)S(1)}, u32[]{:S(2)}, u32[]{:S(2)}) async-start(bf16[32,32,128]{2,1,0:T(8,128)(2,1)} %back_kernel.1), calls=%async_computation.4 | async-start | bytes 524288 | tf_op jit(solution)/shard_map/all_to_all | solution.py:336
  118.3 7.0 %collective-permute-start.2 = (bf16[512,128]{1,0:T(8,128)(2,1)S(1)}, bf16[512,128]{1,0:T(8,128)(2,1)S(1)}, u32[]{:S(2)}, u32[]{:S(2)}) collective-permute-start(bf16[512,128]{1,0:T(8,128)(2,1)S(1)} %get-tuple-element.41), channel_id=1, source_target_pairs={{0,16},{16,0},{1,17},{17,1},{2,18},{18,2},{3,19},{19,3},{4,20},{20... | collective-permute-start | bytes 393224 | tf_op jit(solution)/shard_map/ppermute | solution.py:372
Sparse Core Ops, SparseCore 0:
  9.8 41.4 all-gather.2
  91.1 32.8 reduce-scatter.1

commit v7 on v5

--- a/solution.py
+++ b/solution.py
@@ -356,7 +356,7 @@
         [((HALF * CH, LANE), BF), ((2 * N, 2 * LANE), F32)],
         packed, first, second, second_back, twist, last, flops=5_000_000_000, late=(1, 2, 3, 4, 5),
     )
-    own, cot, conv = lax.optimization_barrier((own, cot, conv))
+    own, cot, conv, query_other = lax.optimization_barrier((own, cot, conv, query_other))
     other = lax.ppermute(own, "k", core_pair)
     own_part, side = call(
         own_grad_kernel,

time: 140 us -> 139 us (level)
  waiting for transfers between devices: 31.6 us -> 29.7 us
  starting transfers between devices: 38.9 us -> 40.4 us
    all_to_all x4, waiting for transfers between devices: 23.2 us -> 21.1 us  [exchange(): return lax.all_to_all(x, axes, split_axis=0, concat_axis=0, tiled=True)]
    ppermute x2, starting transfers between devices: 0.51 us -> 2.04 us  [local(): query_other = tuple((lax.ppermute(side, 'k', core_pair) for side in query))]
  transfers between devices with their start and end apart: 13 -> 13, of which waited for: 9 -> 8; matrix products, arithmetic and copies ran while one was open for 0% -> 0% of each run, Pallas kernels for 14% -> 14%
where the time goes in v7:
time: 139 us
  starting transfers between devices  40.4 us (29%)
  waiting for transfers between devices  29.7 us (21%)
  Pallas kernels  21.8 us (16%)
  blocking collectives  20.6 us (15%)
  between operations  14.2 us (10%)
  local copies, waits for them, and re-layouts  12 us (9%)
    all_to_all x4, starting transfers between devices, exchange(): return lax.all_to_all(x, axes, split_axis=0, concat_axis=0, tiled=True)  28.2 us
    pallas_call x11, Pallas kernels, call(): pl.pallas_call(body, out_shape=shapes, in_specs=[pl.BlockSpec(memory_spac...  21.8 us
    all_to_all x4, waiting for transfers between devices, exchange(): return lax.all_to_all(x, axes, split_axis=0, concat_axis=0, tiled=True)  21.1 us
    all_to_all x1, blocking collectives, exchange(): return lax.all_to_all(x, axes, split_axis=0, concat_axis=0, tiled=True)  20.6 us
    unnamed x28, local copies, waits for them, and re-layouts  12 us
    ppermute x1, waiting for transfers between devices, local(): received = lax.ppermute(passed, 'h', core_pair)  4.26 us
    ppermute x1, starting transfers between devices, local(): received = lax.ppermute(passed, 'h', core_pair)  2.98 us
    ppermute x1, starting transfers between devices, local(): query = (query_t, lax.ppermute(query_t, 'h', core_pair))  2.98 us
  transfers between devices with their start and end apart: 13, of which 8 were waited for; matrix products, arithmetic and copies ran while one was open for 0% of the time, Pallas kernels for 14%

profile of v7, /device:TPU:1, one launch (start us, length us, event | category | flops | bytes accessed | tf_op | source)
XLA Modules:
  0.0 138.7 jit_solution(18269430194343563064)
XLA Ops:
  7.9 1.9 %pack_kernel.1 = bf16[32,32,128]{2,1,0:T(8,128)(2,1)} custom-call(bf16[128,512]{1,0:T(8,128)(2,1)} %refs_1_.4, bf16[128,512]{1,0:T(8,128)(2,1)} %refs_2_.5, f32[128,512]{1,0:T(8,128)} %refs_2_.4), custom_call_target="tpu_custom_call" | custom-call | bytes 4194304 | tf_op jit(solution)/shard_map/pack_kernel/pallas_call | solution.py:320
  9.9 12.9 %all-to-all-start = ((bf16[32,32,128]{2,1,0:T(8,128)(2,1)}), bf16[32,32,128]{2,1,0:T(8,128)(2,1)S(1)}, u32[]{:S(2)}, u32[]{:S(2)}) async-start(bf16[32,32,128]{2,1,0:T(8,128)(2,1)} %pack_kernel.1), calls=%async_computation | async-start | bytes 524288 | tf_op jit(solution)/shard_map/all_to_all | solution.py:336
  23.8 3.0 %collective-permute-start = (bf16[512,128]{1,0:T(8,128)(2,1)S(1)}, bf16[512,128]{1,0:T(8,128)(2,1)S(1)}, u32[]{:S(2)}, u32[]{:S(2)}) collective-permute-start(bf16[512,128]{1,0:T(8,128)(2,1)S(1)} %turn_kernel.1.refs_4_.refs_1_.refs_2_), channel_id=1, source_target_pairs={{0,16},{16,0},{1,17},{17,1},{2,18},{18,2},{3,19},{19,3},{4,20},{20... | collective-permute-start | bytes 393224 | tf_op jit(solution)/shard_map/ppermute | solution.py:348
  26.8 0.9 copy-done.3
  27.7 1.1 share_kernel.1
  28.8 2.4 %collective-permute-done.refs_5_.refs_2_.refs_3_ = bf16[512,128]{1,0:T(8,128)(2,1)S(1)} collective-permute-done((bf16[512,128]{1,0:T(8,128)(2,1)S(1)}, bf16[512,128]{1,0:T(8,128)(2,1)S(1)}, u32[]{:S(2)}, u32[]{:S(2)}) %collective-permute-start) | collective-permute-done | bytes 131104 | tf_op jit(solution)/shard_map/ppermute | solution.py:348
  31.2 5.6 %all-to-all-done.refs_0_ = bf16[32,32,128]{2,1,0:T(8,128)(2,1)S(1)} async-done(((bf16[32,32,128]{2,1,0:T(8,128)(2,1)}), bf16[32,32,128]{2,1,0:T(8,128)(2,1)S(1)}, u32[]{:S(2)}, u32[]{:S(2)}) %all-to-all-start) | async-done | bytes 262176 | tf_op jit(solution)/shard_map/all_to_all | solution.py:336
  36.8 5.5 %all-to-all-start.1 = ((bf16[16,128,256]{2,1,0:T(8,128)(2,1)}), bf16[16,128,256]{2,1,0:T(8,128)(2,1)S(1)}, u32[]{:S(2)}, u32[]{:S(2)}) async-start(bf16[16,128,256]{2,1,0:T(8,128)(2,1)} %share_kernel.1), calls=%async_computation.1 | async-start | bytes 2097152 | tf_op jit(solution)/shard_map/all_to_all | solution.py:336
  42.3 1.9 %collective-permute-start.1 = (bf16[512,128]{1,0:T(8,128)(2,1)S(1)}, bf16[512,128]{1,0:T(8,128)(2,1)S(1)}, u32[]{:S(2)}, u32[]{:S(2)}) collective-permute-start(bf16[512,128]{1,0:T(8,128)(2,1)S(1)} %turn_kernel.1.refs_4_.refs_1_.refs_2_), channel_id=1, source_target_pairs={{0,8},{8,0},{1,9},{9,1},{2,10},{10,2},{3,11},{11,3},{4,12},{12,4},... | collective-permute-start | bytes 393224 | tf_op jit(solution)/shard_map/ppermute | solution.py:352
  44.4 1.7 %copy-done.5 = bf16[2,512,1056]{2,1,0:T(8,128)(2,1)S(1)} copy-done((bf16[2,512,1056]{2,1,0:T(8,128)(2,1)S(1)}, bf16[2,512,1056]{2,1,0:T(8,128)(2,1)}, u32[]{:S(2)}) %copy-start.5) | copy-done | bytes 2162712
  46.1 1.6 %copy-done.7 = bf16[2,1056,512]{2,1,0:T(8,128)(2,1)S(1)} copy-done((bf16[2,1056,512]{2,1,0:T(8,128)(2,1)S(1)}, bf16[2,1056,512]{2,1,0:T(8,128)(2,1)}, u32[]{:S(2)}) %copy-start.7) | copy-done | bytes 2162712
  47.7 4.9 %conv_kernel.1 = (bf16[512,128]{1,0:T(8,128)(2,1)S(1)}, f32[1056,256]{1,0:T(8,128)S(1)}) custom-call(bf16[32,32,128]{2,1,0:T(8,128)(2,1)S(1)} %all-to-all-done.refs_0_, bf16[2,1056,512]{2,1,0:T(8,128)(2,1)S(1)} %copy-done.7, bf16[2,256,256]{2,1,0:T(8,128)(2,1)S(1)} %copy-done.10, bf16[2,256,256]{2,1,0:T(8,128)(2,1)S(1)} %copy-done.11, ...), custom_call_target="tpu_custom_call" | custom-call | flops 5000000000 | bytes 4194304 | tf_op jit(solution)/shard_map/conv_kernel/pallas_call | solution.py:320
  52.6 1.0 copy-done.12
  53.6 4.5 %all-to-all-done.1.refs_1_.refs_2_.refs_6_ = bf16[16,128,256]{2,1,0:T(8,128)(2,1)S(1)} async-done(((bf16[16,128,256]{2,1,0:T(8,128)(2,1)}), bf16[16,128,256]{2,1,0:T(8,128)(2,1)S(1)}, u32[]{:S(2)}, u32[]{:S(2)}) %all-to-all-start.1) | async-done | bytes 1048608 | tf_op jit(solution)/shard_map/all_to_all | solution.py:336
  58.1 2.8 %collective-permute-start.3 = (bf16[8,512,128]{2,1,0:T(8,128)(2,1)}, bf16[8,512,128]{2,1,0:T(8,128)(2,1)S(1)}, u32[]{:S(2)}, u32[]{:S(2)}) collective-permute-start(bf16[8,512,128]{2,1,0:T(8,128)(2,1)} %bitcast.2), channel_id=1, source_target_pairs={{0,8},{8,0},{1,9},{9,1},{2,10},{10,2},{3,11},{11,3},{4,12},{12,4},... | collective-permute-start | bytes 3145736 | tf_op jit(solution)/shard_map/ppermute | solution.py:360
  61.0 1.2 copy-done
  63.9 20.6 %all_to_all.25.refs_0_.refs_1_ = bf16[32,64,128]{2,1,0:T(8,128)(2,1)S(1)} all-to-all(bf16[32,64,128]{2,1,0:T(8,128)(2,1)S(1)} %get-tuple-element.39), channel_id=1, replica_groups=mesh['z'=8,'h'=2,'k'=2,'chan'=8] {'z','h','k'}, dimensions={0} | all-to-all | bytes 1048576 | tf_op jit(solution)/shard_map/all_to_all | solution.py:336
  84.5 1.3 collective-permute-start.5
  85.8 1.8 %project_kernel.1 = bf16[16,128,256]{2,1,0:T(8,128)(2,1)} custom-call(bf16[32,64,128]{2,1,0:T(8,128)(2,1)S(1)} %all_to_all.25.refs_0_.refs_1_, bf16[512,128]{1,0:T(8,128)(2,1)S(1)} %turn_kernel.1.refs_4_.refs_1_.refs_2_, bf16[512,128]{1,0:T(8,128)(2,1)S(1)} %collective-permute-done.refs_5_.refs_2_.refs_3_, bf16[8,512,128]{2,1,0:T(8,128)(2,1)S(1)} %bitcast.4, ...), custom_call_target="tpu_custom_call" | custom-call | bytes 4194304 | tf_op jit(solution)/shard_map/project_kernel/pallas_call | solution.py:320
  88.1 2.2 %weight_kernel.1 = f32[8,512,128]{2,1,0:T(8,128)} custom-call(bf16[32,64,128]{2,1,0:T(8,128)(2,1)S(1)} %all_to_all.25.refs_0_.refs_1_, bf16[32,64,128]{2,1,0:T(8,128)(2,1)S(1)} %collective-permute-done.5.refs_1_, bf16[512,128]{1,0:T(8,128)(2,1)S(1)} %turn_kernel.1.refs_4_.refs_1_.refs_2_, bf16[512,128]{1,0:T(8,128)(2,1)S(1)} %collective-permute-done.refs_5_.refs_2_.refs_3_, ...), custom_call_target="tpu_custom_call" | custom-call | bytes 4194304 | tf_op jit(solution)/shard_map/weight_kernel/pallas_call | solution.py:320
  90.3 4.7 %all-to-all-start.3 = ((bf16[16,128,256]{2,1,0:T(8,128)(2,1)}), bf16[16,128,256]{2,1,0:T(8,128)(2,1)S(1)}, u32[]{:S(2)}, u32[]{:S(2)}) async-start(bf16[16,128,256]{2,1,0:T(8,128)(2,1)} %project_kernel.1), calls=%async_computation.3 | async-start | bytes 2097152 | tf_op jit(solution)/shard_map/all_to_all | solution.py:336
  95.1 1.8 %copy-done.6 = bf16[2,512,1056]{2,1,0:T(8,128)(2,1)S(1)} copy-done((bf16[2,512,1056]{2,1,0:T(8,128)(2,1)S(1)}, bf16[2,512,1056]{2,1,0:T(8,128)(2,1)}, u32[]{:S(2)}) %copy-start.6) | copy-done | bytes 2162712
  96.9 1.6 %copy-done.8 = bf16[2,1056,512]{2,1,0:T(8,128)(2,1)S(1)} copy-done((bf16[2,1056,512]{2,1,0:T(8,128)(2,1)S(1)}, bf16[2,1056,512]{2,1,0:T(8,128)(2,1)}, u32[]{:S(2)}) %copy-start.8) | copy-done | bytes 2162712
  98.5 1.2 copy-done.13
  99.7 6.8 %back_kernel.1 = bf16[32,32,128]{2,1,0:T(8,128)(2,1)} custom-call(bf16[32,64,128]{2,1,0:T(8,128)(2,1)S(1)} %all_to_all.25.refs_0_.refs_1_, f32[1056,256]{1,0:T(8,128)S(1)} %copy-done.13, bf16[2,1056,512]{2,1,0:T(8,128)(2,1)S(1)} %copy-done.8, bf16[2,256,256]{2,1,0:T(8,128)(2,1)S(1)} %copy-done.10, bf16[2,256,256]{2,1,0:T(8,128)(2,1)S(1)} %copy-done.11, ...), custom_call_target="tpu_custom_call" | custom-call | flops 8000000000 | bytes 4194304 | tf_op jit(solution)/shard_map/back_kernel/pallas_call | solution.py:320
  106.6 5.8 %all-to-all-done.3.refs_0_ = bf16[16,128,256]{2,1,0:T(8,128)(2,1)S(1)} async-done(((bf16[16,128,256]{2,1,0:T(8,128)(2,1)}), bf16[16,128,256]{2,1,0:T(8,128)(2,1)S(1)}, u32[]{:S(2)}, u32[]{:S(2)}) %all-to-all-start.3) | async-done | bytes 1048608 | tf_op jit(solution)/shard_map/all_to_all | solution.py:336
  112.4 5.1 %all-to-all-start.4 = ((bf16[32,32,128]{2,1,0:T(8,128)(2,1)}), bf16[32,32,128]{2,1,0:T(8,128)(2,1)S(1)}, u32[]{:S(2)}, u32[]{:S(2)}) async-start(bf16[32,32,128]{2,1,0:T(8,128)(2,1)} %back_kernel.1), calls=%async_computation.4 | async-start | bytes 524288 | tf_op jit(solution)/shard_map/all_to_all | solution.py:336
  117.6 3.0 %collective-permute-start.4 = (bf16[512,128]{1,0:T(8,128)(2,1)S(1)}, bf16[512,128]{1,0:T(8,128)(2,1)S(1)}, u32[]{:S(2)}, u32[]{:S(2)}) collective-permute-start(bf16[512,128]{1,0:T(8,128)(2,1)S(1)} %get-tuple-element.43), channel_id=1, source_target_pairs={{0,16},{16,0},{1,17},{17,1},{2,18},{18,2},{3,19},{19,3},{4,20},{20... | collective-permute-start | bytes 393224 | tf_op jit(solution)/shard_map/ppermute | solution.py:372
  120.5 4.3 %collective-permute-done.4.refs_3_ = bf16[512,128]{1,0:T(8,128)(2,1)S(1)} collective-permute-done((bf16[512,128]{1,0:T(8,128)(2,1)S(1)}, bf16[512,128]{1,0:T(8,128)(2,1)S(1)}, u32[]{:S(2)}, u32[]{:S(2)}) %collective-permute-start.4) | collective-permute-done | bytes 131104 | tf_op jit(solution)/shard_map/ppermute | solution.py:372
  124.8 0.9 sum_kernel.1
  125.7 5.2 %all-to-all-done.4.refs_0_ = bf16[32,32,128]{2,1,0:T(8,128)(2,1)S(1)} async-done(((bf16[32,32,128]{2,1,0:T(8,128)(2,1)}), bf16[32,32,128]{2,1,0:T(8,128)(2,1)S(1)}, u32[]{:S(2)}, u32[]{:S(2)}) %all-to-all-start.4) | async-done | bytes 262176 | tf_op jit(solution)/shard_map/all_to_all | solution.py:336
  130.9 0.9 finish_kernel.1
  (36 shorter events, 4.2 us)
Async XLA Ops:
  7.2 51.0 %all-gather.3.cloned.1.call-start = ((), (), s32[]{:S(2)}) async-start(), calls=%async_computation.7 | async-start | bytes 1179648 | tf_op jit(solution)/shard_map/all_gather | solution.py:349
  9.9 34.5 %copy-start.10 = (bf16[2,256,256]{2,1,0:T(8,128)(2,1)S(1)}, bf16[2,256,256]{2,1,0:T(8,128)(2,1)}, u32[]{:S(2)}) copy-start(bf16[2,256,256]{2,1,0:T(8,128)(2,1)} %constant.11.clone.refs_2_.refs_3_) | copy-start | bytes 786436
  9.9 34.5 %copy-start.11 = (bf16[2,256,256]{2,1,0:T(8,128)(2,1)S(1)}, bf16[2,256,256]{2,1,0:T(8,128)(2,1)}, u32[]{:S(2)}) copy-start(bf16[2,256,256]{2,1,0:T(8,128)(2,1)} %constant.12.clone.refs_3_.refs_4_) | copy-start | bytes 786436
  9.9 26.9 %all-to-all-start = ((bf16[32,32,128]{2,1,0:T(8,128)(2,1)}), bf16[32,32,128]{2,1,0:T(8,128)(2,1)S(1)}, u32[]{:S(2)}, u32[]{:S(2)}) async-start(bf16[32,32,128]{2,1,0:T(8,128)(2,1)} %pack_kernel.1), calls=%async_computation | async-start | bytes 524288 | tf_op jit(solution)/shard_map/all_to_all | solution.py:336
  22.8 0.9 copy-start.4
  23.8 7.4 %collective-permute-start = (bf16[512,128]{1,0:T(8,128)(2,1)S(1)}, bf16[512,128]{1,0:T(8,128)(2,1)S(1)}, u32[]{:S(2)}, u32[]{:S(2)}) collective-permute-start(bf16[512,128]{1,0:T(8,128)(2,1)S(1)} %turn_kernel.1.refs_4_.refs_1_.refs_2_), channel_id=1, source_target_pairs={{0,16},{16,0},{1,17},{17,1},{2,18},{18,2},{3,19},{19,3},{4,20},{20... | collective-permute-start | bytes 393224 | tf_op jit(solution)/shard_map/ppermute | solution.py:348
  26.8 0.9 copy-start.3
  27.7 16.7 %copy-start.9 = (f32[2,528,128]{2,1,0:T(8,128)S(1)}, f32[2,528,128]{2,1,0:T(8,128)}, u32[]{:S(2)}) copy-start(f32[2,528,128]{2,1,0:T(8,128)} %constant.13.clone.refs_4_.refs_5_) | copy-start | bytes 1622020
  36.8 21.3 %all-to-all-start.1 = ((bf16[16,128,256]{2,1,0:T(8,128)(2,1)}), bf16[16,128,256]{2,1,0:T(8,128)(2,1)S(1)}, u32[]{:S(2)}, u32[]{:S(2)}) async-start(bf16[16,128,256]{2,1,0:T(8,128)(2,1)} %share_kernel.1), calls=%async_computation.1 | async-start | bytes 2097152 | tf_op jit(solution)/shard_map/all_to_all | solution.py:336
  42.3 89.6 %reduce-scatter.2.cloned.1.call-start = ((), (), s32[]{:S(2)}) async-start(), calls=%async_computation.6 | async-start | bytes 2359296 | tf_op jit(solution)/shard_map/reduce_scatter | solution.py:382
  42.3 11.3 %collective-permute-start.1 = (bf16[512,128]{1,0:T(8,128)(2,1)S(1)}, bf16[512,128]{1,0:T(8,128)(2,1)S(1)}, u32[]{:S(2)}, u32[]{:S(2)}) collective-permute-start(bf16[512,128]{1,0:T(8,128)(2,1)S(1)} %turn_kernel.1.refs_4_.refs_1_.refs_2_), channel_id=1, source_target_pairs={{0,8},{8,0},{1,9},{9,1},{2,10},{10,2},{3,11},{11,3},{4,12},{12,4},... | collective-permute-start | bytes 393224 | tf_op jit(solution)/shard_map/ppermute | solution.py:352
  44.3 9.3 %collective-permute-start.2 = (bf16[512,128]{1,0:T(8,128)(2,1)S(1)}, bf16[512,128]{1,0:T(8,128)(2,1)S(1)}, u32[]{:S(2)}, u32[]{:S(2)}) collective-permute-start(bf16[512,128]{1,0:T(8,128)(2,1)S(1)} %collective-permute-done.refs_5_.refs_2_.refs_3_), channel_id=1, source_target_pairs={{0,8},{8,0},{1,9},{9,1},{2,10},{10,2},{3,11},{11,3},{4,12},{12,4},... | collective-permute-start | bytes 393224 | tf_op jit(solution)/shard_map/ppermute | solution.py:352
  44.4 1.7 %copy-start.5 = (bf16[2,512,1056]{2,1,0:T(8,128)(2,1)S(1)}, bf16[2,512,1056]{2,1,0:T(8,128)(2,1)}, u32[]{:S(2)}) copy-start(bf16[2,512,1056]{2,1,0:T(8,128)(2,1)} %constant.14.clone.refs_5_.refs_6_) | copy-start | bytes 6488068
  46.1 1.6 %copy-start.7 = (bf16[2,1056,512]{2,1,0:T(8,128)(2,1)S(1)}, bf16[2,1056,512]{2,1,0:T(8,128)(2,1)}, u32[]{:S(2)}) copy-start(bf16[2,1056,512]{2,1,0:T(8,128)(2,1)} %constant.10.clone.refs_1_.refs_2_) | copy-start | bytes 6488068
  52.6 1.0 copy-start.12
  58.1 5.3 %collective-permute-start.3 = (bf16[8,512,128]{2,1,0:T(8,128)(2,1)}, bf16[8,512,128]{2,1,0:T(8,128)(2,1)S(1)}, u32[]{:S(2)}, u32[]{:S(2)}) collective-permute-start(bf16[8,512,128]{2,1,0:T(8,128)(2,1)} %bitcast.2), channel_id=1, source_target_pairs={{0,8},{8,0},{1,9},{9,1},{2,10},{10,2},{3,11},{11,3},{4,12},{12,4},... | collective-permute-start | bytes 3145736 | tf_op jit(solution)/shard_map/ppermute | solution.py:360
  61.0 1.2 copy-start
  84.5 3.1 %collective-permute-start.5 = (bf16[32,64,128]{2,1,0:T(8,128)(2,1)S(1)}, bf16[32,64,128]{2,1,0:T(8,128)(2,1)S(1)}, u32[]{:S(2)}, u32[]{:S(2)}) collective-permute-start(bf16[32,64,128]{2,1,0:T(8,128)(2,1)S(1)} %all_to_all.25.refs_0_.refs_1_), channel_id=1, source_target_pairs={{0,8},{8,0},{1,9},{9,1},{2,10},{10,2},{3,11},{11,3},{4,12},{12,4},... | collective-permute-start | bytes 1572872 | tf_op jit(solution)/shard_map/ppermute | solution.py:374
  85.8 2.3 %collective-permute-start.6 = (bf16[16,128,128]{2,1,0:T(8,128)(2,1)S(1)}, bf16[16,128,128]{2,1,0:T(8,128)(2,1)S(1)}, u32[]{:S(2)}, u32[]{:S(2)}) collective-permute-start(bf16[16,128,128]{2,1,0:T(8,128)(2,1)S(1)} %get-tuple-element.53), channel_id=1, source_target_pairs={{0,8},{8,0},{1,9},{9,1},{2,10},{10,2},{3,11},{11,3},{4,12},{12,4},... | collective-permute-start | bytes 1572872 | tf_op jit(solution)/shard_map/ppermute | solution.py:371
  90.3 22.1 %all-to-all-start.3 = ((bf16[16,128,256]{2,1,0:T(8,128)(2,1)}), bf16[16,128,256]{2,1,0:T(8,128)(2,1)S(1)}, u32[]{:S(2)}, u32[]{:S(2)}) async-start(bf16[16,128,256]{2,1,0:T(8,128)(2,1)} %project_kernel.1), calls=%async_computation.3 | async-start | bytes 2097152 | tf_op jit(solution)/shard_map/all_to_all | solution.py:336
  95.1 1.8 %copy-start.6 = (bf16[2,512,1056]{2,1,0:T(8,128)(2,1)S(1)}, bf16[2,512,1056]{2,1,0:T(8,128)(2,1)}, u32[]{:S(2)}) copy-start(bf16[2,512,1056]{2,1,0:T(8,128)(2,1)} %constant.14.clone.refs_5_.refs_6_) | copy-start | bytes 6488068
  96.9 1.6 %copy-start.8 = (bf16[2,1056,512]{2,1,0:T(8,128)(2,1)S(1)}, bf16[2,1056,512]{2,1,0:T(8,128)(2,1)}, u32[]{:S(2)}) copy-start(bf16[2,1056,512]{2,1,0:T(8,128)(2,1)} %constant.10.clone.refs_1_.refs_2_) | copy-start | bytes 6488068
  98.5 1.2 copy-start.13
  106.6 24.3 %copy-start.1 = (bf16[128,512]{1,0:T(8,128)(2,1)S(1)}, bf16[128,512]{1,0:T(8,128)(2,1)}, u32[]{:S(2)}) copy-start(bf16[128,512]{1,0:T(8,128)(2,1)} %refs_1_.4) | copy-start | bytes 393220
  106.6 24.3 %copy-start.2 = (bf16[128,512]{1,0:T(8,128)(2,1)S(1)}, bf16[128,512]{1,0:T(8,128)(2,1)}, u32[]{:S(2)}) copy-start(bf16[128,512]{1,0:T(8,128)(2,1)} %refs_2_.5) | copy-start | bytes 393220
  112.4 18.5 %all-to-all-start.4 = ((bf16[32,32,128]{2,1,0:T(8,128)(2,1)}), bf16[32,32,128]{2,1,0:T(8,128)(2,1)S(1)}, u32[]{:S(2)}, u32[]{:S(2)}) async-start(bf16[32,32,128]{2,1,0:T(8,128)(2,1)} %back_kernel.1), calls=%async_computation.4 | async-start | bytes 524288 | tf_op jit(solution)/shard_map/all_to_all | solution.py:336
  117.6 7.2 %collective-permute-start.4 = (bf16[512,128]{1,0:T(8,128)(2,1)S(1)}, bf16[512,128]{1,0:T(8,128)(2,1)S(1)}, u32[]{:S(2)}, u32[]{:S(2)}) collective-permute-start(bf16[512,128]{1,0:T(8,128)(2,1)S(1)} %get-tuple-element.43), channel_id=1, source_target_pairs={{0,16},{16,0},{1,17},{17,1},{2,18},{18,2},{3,19},{19,3},{4,20},{20... | collective-permute-start | bytes 393224 | tf_op jit(solution)/shard_map/ppermute | solution.py:372
Sparse Core Ops, SparseCore 0:
  9.8 40.9 all-gather.2
  90.5 32.0 reduce-scatter.1
